TPU v7x, 32 devices: a whole 2x2x4 slice. The times are simulated.
32 devices in a mesh: dp: 8 (over z, x), seq: 4 (over y, core).
Axes of the slice: x: 2, y: 2, z: 4, core: 2. Of those that a mesh axis runs over, the one named last changes fastest.
Arguments:
- tokens: bfloat16 [16, 2048, 512], P('dp', 'seq'), may hold values from -6 to 6
- feature_matrix: bfloat16 [64, 256], replicated, may hold values from -6 to 6
- input_weight: bfloat16 [512, 1536], P(('dp', 'seq')), may hold values from -0.125 to 0.125
- output_weight: bfloat16 [512, 512], P(('dp', 'seq')), may hold values from -3 to 3
- output_bias: bfloat16 [512], P(('dp', 'seq')), may hold values from -1.75 to 1.75
- up_weight: bfloat16 [512, 2048], P(('dp', 'seq')), may hold values from -0.25 to 0.25
- up_bias: bfloat16 [2048], P(('dp', 'seq')), may hold values from -1.75 to 1.75
- down_weight: bfloat16 [2048, 512], P(('dp', 'seq')), may hold values from -0.125 to 0.125
- down_bias: bfloat16 [512], P(('dp', 'seq')), may hold values from -1.75 to 1.75
- first_gain: bfloat16 [512], P(('dp', 'seq')), may hold values from 0.5 to 1.5
- first_shift: bfloat16 [512], P(('dp', 'seq')), may hold values from -1.25 to 1.25
- second_gain: bfloat16 [512], P(('dp', 'seq')), may hold values from 0.5 to 1.5
- second_shift: bfloat16 [512], P(('dp', 'seq')), may hold values from -1.25 to 1.25
- cotangent: bfloat16 [16, 2048, 512], P('dp', 'seq'), may hold values from -6 to 6
Outputs:
- result: float32 [16, 2048, 512], P('dp', 'seq')
- tokens_grad: float32 [16, 2048, 512], P('dp', 'seq')
- input_weight_grad: float32 [512, 1536], P(('dp', 'seq'))
- output_weight_grad: float32 [512, 512], P(('dp', 'seq'))
- output_bias_grad: float32 [512], P(('dp', 'seq'))
- up_weight_grad: float32 [512, 2048], P(('dp', 'seq'))
- up_bias_grad: float32 [2048], P(('dp', 'seq'))
- down_weight_grad: float32 [2048, 512], P(('dp', 'seq'))
- down_bias_grad: float32 [512], P(('dp', 'seq'))
- first_gain_grad: float32 [512], P(('dp', 'seq'))
- first_shift_grad: float32 [512], P(('dp', 'seq'))
- second_gain_grad: float32 [512], P(('dp', 'seq'))
- second_shift_grad: float32 [512], P(('dp', 'seq'))
All inputs are finite; a program needn't handle non-finite values.
Results may differ from a plain program's by a relative error of at most 0.015.
Values may be sent and summed in bfloat16 or wider, within the bound.
A program may use at most 192 MiB of HBM per device.

v0:
```python
import math

import jax
import jax.numpy as jnp
from jax import lax
from jax.sharding import PartitionSpec as P

H = 8
DH = 64


epsilon = 1e-05
finest_precision = lax.Precision.HIGHEST


def prefix(array, axis, combine, identity):
    count, here = (lax.axis_size(axis), lax.axis_index(axis))
    everything = jax.tree.map(
        lambda part, kind: lax.all_gather(part.astype(kind), axis),
        array,
        (jnp.bfloat16, jnp.bfloat16),
    )
    start = jax.tree.map(
        lambda part, zero: jnp.broadcast_to(jnp.asarray(zero, part.dtype), part.shape),
        array,
        identity,
    )

    def hop(k, before):
        reached = k < here
        new = combine(
            before, jax.tree.map(lambda part, own: part[k].astype(own.dtype), everything, array)
        )
        return jax.tree.map(lambda a, b: jnp.where(reached, a, b), new, before)

    return lax.fori_loop(0, count, hop, start)


def prefix_2(array, axis, join, neutral):
    count = lax.axis_size(axis)
    place = lax.axis_index(axis)
    ahead = count - 1 - place
    gathered = jax.tree.map(
        lambda a, kind: lax.all_gather(a.astype(kind), axis),
        array,
        jax.tree.map(lambda a: jnp.bfloat16 if a.dtype == jnp.float32 else a.dtype, array),
    )
    state = jax.tree.map(lambda a, e: jnp.zeros_like(a) + jnp.asarray(e, a.dtype), array, neutral)

    def one(hop, state):
        source = count - 1 - hop
        return join(
            state,
            jax.tree.map(
                lambda a, own: lax.dynamic_index_in_dim(a, source, 0, False).astype(own.dtype),
                gathered,
                array,
            ),
        )

    return lax.fori_loop(0, ahead, one, state)


def layer_norm(value_rows, norm_gain, norm_shift):
    center = jnp.mean(value_rows, axis=-1, keepdims=True)
    centred = value_rows - center
    spread = jnp.mean(centred * centred, axis=-1, keepdims=True)
    return centred * lax.rsqrt(spread + epsilon) * norm_gain + norm_shift


def gelu_tanh(value_rows):
    return jax.nn.gelu(value_rows, approximate=True)


def add_pair(earlier, later_term):
    return (earlier[0] + later_term[0], earlier[1] + later_term[1])


def causal_mask(length):
    positions = jnp.arange(length)
    return (positions[:, None] >= positions[None, :]).astype(jnp.float32)


def favor_map(proj_low, matrix, feature_scale):
    raw_proj = jnp.einsum("rhd,dm->rhm", proj_low, matrix, preferred_element_type=jnp.float32)
    projection = proj_low.astype(jnp.float32)
    half_norm = (
        0.5
        * feature_scale
        * feature_scale
        * jnp.sum(projection * projection, axis=-1, keepdims=True)
    )
    return jnp.exp(feature_scale * raw_proj - half_norm) / math.sqrt(matrix.shape[1])


def favor_back(map_grad, favor_value, proj_low, matrix, feature_scale):
    log_grad = map_grad * favor_value
    raw_grad = (feature_scale * log_grad).astype(jnp.bfloat16)
    projection = proj_low.astype(jnp.float32)
    through = jnp.einsum("rhm,dm->rhd", raw_grad, matrix, preferred_element_type=jnp.float32)
    return (
        through
        - feature_scale * feature_scale * jnp.sum(log_grad, axis=-1, keepdims=True) * projection
    )


def front(token_block, matrix, params):
    inputs = token_block.astype(jnp.float32)
    length = inputs.shape[0]
    normed = layer_norm(
        inputs, params[7].astype(jnp.float32), params[8].astype(jnp.float32)
    ).astype(jnp.bfloat16)
    mixed = jnp.dot(normed, params[0], preferred_element_type=jnp.float32).astype(jnp.bfloat16)
    head_parts = mixed.reshape(length, 3, H, DH)
    feature_scale = DH ** (-0.25)
    query_features = favor_map(head_parts[:, 0], matrix, feature_scale)
    key_features = favor_map(head_parts[:, 1], matrix, feature_scale)
    query_reduced = query_features.astype(jnp.bfloat16)
    key_reduced = key_features.astype(jnp.bfloat16)
    value_rows = head_parts[:, 2]
    block_local_state = jnp.einsum(
        "nqo,nqi->qoi", key_reduced, value_rows, preferred_element_type=jnp.float32
    )
    local_sum = jnp.sum(key_reduced.astype(jnp.float32), axis=0)
    return (
        inputs,
        normed,
        head_parts,
        query_features,
        key_features,
        query_reduced,
        key_reduced,
        value_rows,
        block_local_state,
        local_sum,
    )


def attend(query_reduced, key_reduced, value_rows, running_prefix_state, norm_sum):
    causal = causal_mask(query_reduced.shape[0])
    scores = (
        jnp.einsum("ihm,jhm->hij", query_reduced, key_reduced, preferred_element_type=jnp.float32)
        * causal[None]
    )
    denominator = jnp.sum(scores, axis=-1).T + jnp.einsum(
        "ihm,hm->ih", query_reduced.astype(jnp.float32), norm_sum, precision=finest_precision
    )
    attention_numerator = jnp.einsum(
        "hij,jhd->ihd", scores.astype(jnp.bfloat16), value_rows, preferred_element_type=jnp.float32
    )
    attention_numerator = attention_numerator + jnp.einsum(
        "plq,lqu->plu",
        query_reduced,
        running_prefix_state.astype(jnp.bfloat16),
        preferred_element_type=jnp.float32,
    )
    return (attention_numerator / denominator[:, :, None], attention_numerator, denominator)


def upper(inputs, output, params):
    length = output.shape[0]
    attended = output.reshape(length, -1).astype(jnp.bfloat16)
    middle = (
        inputs
        + jnp.dot(attended, params[1], preferred_element_type=jnp.float32)
        + params[2].astype(jnp.float32)
    )
    return (attended, middle)


def feed(middle, params):
    normed_two = layer_norm(
        middle, params[9].astype(jnp.float32), params[10].astype(jnp.float32)
    ).astype(jnp.bfloat16)
    hidden = jnp.dot(normed_two, params[3], preferred_element_type=jnp.float32) + params[4].astype(
        jnp.float32
    )
    active = gelu_tanh(hidden).astype(jnp.bfloat16)
    return (
        middle
        + jnp.dot(active, params[5], preferred_element_type=jnp.float32)
        + params[6].astype(jnp.float32)
    )


def upper_back(token_block, upstream, matrix, params, block_carry):
    pieces = front(token_block, matrix, params)
    (
        inputs,
        normed,
        head_parts,
        query_features,
        key_features,
        query_reduced,
        key_reduced,
        value_rows,
        block_local_state,
        local_sum,
    ) = pieces
    running_prefix_state, norm_sum = block_carry
    output, attention_numerator, denominator = attend(
        query_reduced, key_reduced, value_rows, running_prefix_state, norm_sum
    )
    attended, middle = upper(inputs, output, params)
    normed_float, second_pull = jax.vjp(
        layer_norm, middle, params[9].astype(jnp.float32), params[10].astype(jnp.float32)
    )
    normed_two = normed_float.astype(jnp.bfloat16)
    hidden = jnp.dot(normed_two, params[3], preferred_element_type=jnp.float32) + params[4].astype(
        jnp.float32
    )
    active_float, gelu_pull = jax.vjp(gelu_tanh, hidden)
    active = active_float.astype(jnp.bfloat16)
    stored = {"front": pieces, "carry": block_carry}
    down_term = upstream.astype(jnp.bfloat16)
    stored["down"] = jnp.einsum("rf,rd->fd", active, down_term, preferred_element_type=jnp.float32)
    stored["down_bias"] = jnp.sum(upstream, axis=0)
    active_grad = jnp.einsum("rd,fd->rf", down_term, params[5], preferred_element_type=jnp.float32)
    (hidden_grad,) = gelu_pull(active_grad)
    up_term = hidden_grad.astype(jnp.bfloat16)
    stored["up"] = jnp.einsum("rd,rf->df", normed_two, up_term, preferred_element_type=jnp.float32)
    stored["up_bias"] = jnp.sum(hidden_grad, axis=0)
    normed_two_grad = jnp.einsum(
        "rf,df->rd", up_term, params[3], preferred_element_type=jnp.float32
    )
    middle_part, gain_two_grad, shift_two_grad = second_pull(normed_two_grad)
    stored["gain_two"] = gain_two_grad
    stored["shift_two"] = shift_two_grad
    middle_grad = upstream + middle_part
    stored["middle_grad"] = middle_grad
    out_term = middle_grad.astype(jnp.bfloat16)
    stored["out"] = jnp.einsum("re,rd->ed", attended, out_term, preferred_element_type=jnp.float32)
    stored["out_bias"] = jnp.sum(middle_grad, axis=0)
    attended_grad = jnp.einsum(
        "rd,ed->re", out_term, params[1], preferred_element_type=jnp.float32
    ).reshape(output.shape)
    numerator_grad = (attended_grad / denominator[:, :, None]).astype(jnp.bfloat16)
    denom_grad = -jnp.sum(attended_grad * attention_numerator, axis=-1) / (
        denominator * denominator
    )
    stored["numer_grad"] = numerator_grad
    stored["denom_grad"] = denom_grad
    stored["state_grad"] = jnp.einsum(
        "jfp,jfl->fpl", query_reduced, numerator_grad, preferred_element_type=jnp.float32
    )
    stored["sum_grad"] = jnp.einsum(
        "ih,ihm->hm", denom_grad, query_reduced.astype(jnp.float32), precision=finest_precision
    )
    return stored


def lower_back(stored, later_part, matrix, params):
    (
        inputs,
        normed,
        head_parts,
        query_features,
        key_features,
        query_reduced,
        key_reduced,
        value_rows,
        block_local_state,
        local_sum,
    ) = stored["front"]
    running_prefix_state, norm_sum = stored["carry"]
    state_later, sum_later = later_part
    numerator_grad = stored["numer_grad"]
    denom_grad = stored["denom_grad"]
    length = inputs.shape[0]
    causal = causal_mask(length)
    scores = (
        jnp.einsum("ihm,jhm->hij", query_reduced, key_reduced, preferred_element_type=jnp.float32)
        * causal[None]
    )
    scores_grad = jnp.einsum(
        "ihd,jhd->hij", numerator_grad, value_rows, preferred_element_type=jnp.float32
    )
    score_term = ((scores_grad + denom_grad.T[:, :, None]) * causal[None]).astype(jnp.bfloat16)
    later_reduced = state_later.astype(jnp.bfloat16)
    query_grad = jnp.einsum(
        "hij,jhm->ihm", score_term, key_reduced, preferred_element_type=jnp.float32
    )
    query_grad = query_grad + jnp.einsum(
        "gvw,vcw->gvc",
        numerator_grad,
        running_prefix_state.astype(jnp.bfloat16),
        preferred_element_type=jnp.float32,
    )
    query_grad = query_grad + denom_grad[:, :, None] * norm_sum[None]
    key_grad = jnp.einsum(
        "hij,ihm->jhm", score_term, query_reduced, preferred_element_type=jnp.float32
    )
    key_grad = key_grad + jnp.einsum(
        "prc,rqc->prq", value_rows, later_reduced, preferred_element_type=jnp.float32
    )
    key_grad = key_grad + sum_later[None]
    value_grad = jnp.einsum(
        "hij,ihd->jhd",
        scores.astype(jnp.bfloat16),
        numerator_grad,
        preferred_element_type=jnp.float32,
    )
    value_grad = value_grad + jnp.einsum(
        "qsa,saw->qsw", key_reduced, later_reduced, preferred_element_type=jnp.float32
    )
    feature_scale = DH ** (-0.25)
    query_proj = favor_back(query_grad, query_features, head_parts[:, 0], matrix, feature_scale)
    key_proj = favor_back(key_grad, key_features, head_parts[:, 1], matrix, feature_scale)
    mixed_grad = (
        jnp.stack([query_proj, key_proj, value_grad], axis=1)
        .reshape(length, -1)
        .astype(jnp.bfloat16)
    )
    input_part = jnp.einsum("rd,re->de", normed, mixed_grad, preferred_element_type=jnp.float32)
    normed_grad = jnp.einsum("re,de->rd", mixed_grad, params[0], preferred_element_type=jnp.float32)
    _, first_pull = jax.vjp(
        layer_norm, inputs, params[7].astype(jnp.float32), params[8].astype(jnp.float32)
    )
    inputs_part, gain_one_grad, shift_one_grad = first_pull(normed_grad)
    return (stored["middle_grad"] + inputs_part, input_part, gain_one_grad, shift_one_grad)


def local(
    tokens,
    feature_matrix,
    input_weight,
    output_weight,
    output_bias,
    up_weight,
    up_bias,
    down_weight,
    down_bias,
    first_gain,
    first_shift,
    second_gain,
    second_shift,
    cotangent,
):
    params = (
        lax.all_gather(input_weight, ("dp", "seq"), axis=0, tiled=True),
        lax.all_gather(output_weight, ("dp", "seq"), axis=0, tiled=True),
        lax.all_gather(output_bias, ("dp", "seq"), axis=0, tiled=True),
        lax.all_gather(up_weight, ("dp", "seq"), axis=0, tiled=True),
        lax.all_gather(up_bias, ("dp", "seq"), axis=0, tiled=True),
        lax.all_gather(down_weight, ("dp", "seq"), axis=0, tiled=True),
        lax.all_gather(down_bias, ("dp", "seq"), axis=0, tiled=True),
        lax.all_gather(first_gain, ("dp", "seq"), axis=0, tiled=True),
        lax.all_gather(first_shift, ("dp", "seq"), axis=0, tiled=True),
        lax.all_gather(second_gain, ("dp", "seq"), axis=0, tiled=True),
        lax.all_gather(second_shift, ("dp", "seq"), axis=0, tiled=True),
    )
    micros = tokens.shape[0]
    fronts = []
    carries = []
    for micro_step in range(micros):
        pieces = front(tokens[micro_step], feature_matrix, params)
        fronts.append(pieces)
        carries.append(
            prefix(
                (pieces[8], pieces[9]),
                "seq",
                add_pair,
                (jnp.zeros_like(pieces[8]), jnp.zeros_like(pieces[9])),
            )
        )
    results = []
    for micro_step in range(micros):
        pieces = fronts[micro_step]
        running_prefix_state, norm_sum = carries[micro_step]
        output = attend(pieces[5], pieces[6], pieces[7], running_prefix_state, norm_sum)[0]
        attended, middle = upper(pieces[0], output, params)
        results.append(feed(middle, params))
    result = jnp.stack(results)
    back_params = (
        lax.all_gather(input_weight, ("dp", "seq"), axis=0, tiled=True),
        lax.all_gather(output_weight, ("dp", "seq"), axis=0, tiled=True),
        lax.all_gather(output_bias, ("dp", "seq"), axis=0, tiled=True),
        lax.all_gather(up_weight, ("dp", "seq"), axis=0, tiled=True),
        lax.all_gather(up_bias, ("dp", "seq"), axis=0, tiled=True),
        lax.all_gather(down_weight, ("dp", "seq"), axis=0, tiled=True),
        lax.all_gather(down_bias, ("dp", "seq"), axis=0, tiled=True),
        lax.all_gather(first_gain, ("dp", "seq"), axis=0, tiled=True),
        lax.all_gather(first_shift, ("dp", "seq"), axis=0, tiled=True),
        lax.all_gather(second_gain, ("dp", "seq"), axis=0, tiled=True),
        lax.all_gather(second_shift, ("dp", "seq"), axis=0, tiled=True),
    )
    stored_list = []
    later_list = []
    for micro_step in range(micros):
        stored = upper_back(
            tokens[micro_step],
            cotangent[micro_step].astype(jnp.float32),
            feature_matrix,
            back_params,
            carries[micro_step],
        )
        stored_list.append(stored)
        later_list.append(
            prefix_2(
                (stored["state_grad"], stored["sum_grad"]),
                "seq",
                add_pair,
                (jnp.zeros_like(stored["state_grad"]), jnp.zeros_like(stored["sum_grad"])),
            )
        )
    upper_names = ["out", "out_bias", "up", "up_bias", "down", "down_bias", "gain_two", "shift_two"]
    upper_totals = [stored_list[0][name] for name in upper_names]
    micro_step = 1
    upper_totals = [
        total + stored_list[micro_step][name] for total, name in zip(upper_totals, upper_names)
    ]
    token_grads = []
    lower_totals = None
    for micro_step in range(micros):
        stored = stored_list[micro_step]
        tokens_part, input_part, gain_part, shift_part = lower_back(
            stored, later_list[micro_step], feature_matrix, back_params
        )
        token_grads.append(tokens_part)
        lower_parts = (input_part, gain_part, shift_part)
        if micro_step == 0:
            lower_totals = lower_parts
        else:
            lower_totals = jax.tree.map(jnp.add, lower_totals, lower_parts)
    shares = (
        lax.psum_scatter(lower_totals[0], ("dp", "seq"), scatter_dimension=0, tiled=True),
        lax.psum_scatter(upper_totals[0], ("dp", "seq"), scatter_dimension=0, tiled=True),
        lax.psum_scatter(upper_totals[1], ("dp", "seq"), scatter_dimension=0, tiled=True),
        lax.psum_scatter(upper_totals[2], ("dp", "seq"), scatter_dimension=0, tiled=True),
        lax.psum_scatter(upper_totals[3], ("dp", "seq"), scatter_dimension=0, tiled=True),
        lax.psum_scatter(upper_totals[4], ("dp", "seq"), scatter_dimension=0, tiled=True),
        lax.psum_scatter(upper_totals[5], ("dp", "seq"), scatter_dimension=0, tiled=True),
        lax.psum_scatter(lower_totals[1], ("dp", "seq"), scatter_dimension=0, tiled=True),
        lax.psum_scatter(lower_totals[2], ("dp", "seq"), scatter_dimension=0, tiled=True),
        lax.psum_scatter(upper_totals[6], ("dp", "seq"), scatter_dimension=0, tiled=True),
        lax.psum_scatter(upper_totals[7], ("dp", "seq"), scatter_dimension=0, tiled=True),
    )
    return (
        result,
        jnp.stack(token_grads),
        shares[0],
        shares[1],
        shares[2],
        shares[3],
        shares[4],
        shares[5],
        shares[6],
        shares[7],
        shares[8],
        shares[9],
        shares[10],
    )


def solution(mesh):
    in_specs = (
        P("dp", "seq", None),
        P(),
        P(("dp", "seq"), None),
        P(("dp", "seq"), None),
        P(("dp", "seq")),
        P(("dp", "seq"), None),
        P(("dp", "seq")),
        P(("dp", "seq"), None),
        P(("dp", "seq")),
        P(("dp", "seq")),
        P(("dp", "seq")),
        P(("dp", "seq")),
        P(("dp", "seq")),
        P("dp", "seq", None),
    )
    out_specs = (
        P("dp", "seq", None),
        P("dp", "seq", None),
        P(("dp", "seq"), None),
        P(("dp", "seq"), None),
        P(("dp", "seq")),
        P(("dp", "seq"), None),
        P(("dp", "seq")),
        P(("dp", "seq"), None),
        P(("dp", "seq")),
        P(("dp", "seq")),
        P(("dp", "seq")),
        P(("dp", "seq")),
        P(("dp", "seq")),
    )
    return jax.shard_map(local, mesh=mesh, in_specs=in_specs, out_specs=out_specs, check_vma=False)
```

profile of v0, /device:TPU:0, one launch (start us, length us, event | category | flops | bytes accessed | tf_op | source)
XLA Modules:
  0.0 857.3 jit_solution(10769602985409667980)
XLA Ops:
  15.5 42.2 %all-reduce.15 = (bf16[512]{0:T(512)(128)(2,1)S(1)}, bf16[512]{0:T(512)(128)(2,1)S(1)}, bf16[512]{0:T(512)(128)(2,1)S(1)}, bf16[512]{0:T(512)(128)(2,1)}, bf16[5...) all-reduce(bf16[512]{0:T(512)(128)(2,1)S(1)} %dynamic-update-slice., ...), channel_id=1, replica_groups=mesh['dp'=8,'seq'=4] {'dp','seq'}, use_global_device_ids=true, to_apply=%add.1 | all-reduce | flops 5120 | bytes 20480
  58.6 10.2 %all-gather.16.cloned.1.call-done = bf16[512,1536]{1,0:T(8,128)(2,1)} async-done(((bf16[16,1536]{1,0:T(8,128)(2,1)}), bf16[512,1536]{1,0:T(8,128)(2,1)}) %all-gather.16.cloned.1.call-update) | async-done | bytes 1572880 | tf_op jit(solution)/shard_map/all_gather | solution.py:340
  68.7 3.7 convolution_convert_fusion
  74.4 3.4 fusion.180
  80.7 2.5 convolution_convert_fusion.1
  84.3 3.4 fusion.178
  92.5 43.9 %all_gather.98 = bf16[512,512]{1,0:T(8,128)(2,1)} all-gather(bf16[16,512]{1,0:T(8,128)(2,1)S(1)} %copy-done.100), channel_id=1, replica_groups=mesh['dp'=8,'seq'=4] {'dp','seq'}, dimensions={0}, use_global_device_ids=true | all-gather | bytes 540672 | tf_op jit(solution)/shard_map/all_gather | solution.py:341
  139.2 4.3 fusion.16
  143.4 2.9 fusion.196
  146.4 4.8 fusion.14
  151.1 5.2 all-gather.3
  156.3 5.6 all-gather.1
  161.9 5.6 multiply_reduce_fusion.1
  167.5 17.8 %while.63 = (s32[]{:T(128)}, f32[8,256,64]{2,1,0:T(8,128)}, f32[8,256]{1,0:T(8,128)S(1)}, s32[]{:T(128)}, bf16[4,8,256,64]{2,3,1,0:T(8,128)(2,1)}, /*index=5*/bf16[4,8,256]{2,1,0:T(8,128)(2,1)S(1)}, s32[]{:T(128)}, s32[]{:T(128)}) while((s32[]{:T(128)}, f32[8,256,64]{2,1,0:T(8,128)}, f32[8,256]{1,0:T(8,128)S(1)}, s32[]{:T(128)}, ...), condition=%wide.region_16.17_spmd.clone, body=%wide.region_15.16_spmd.clone.sunk | while | flops 532484 | bytes 2379899 | solution.py:36
  169.5 2.2 add_select_fusion.10
  173.7 2.5 add_select_fusion.10
  178.2 2.5 add_select_fusion.10
  182.7 2.5 add_select_fusion.10
  186.1 2.8 fusion.137
  188.9 20.5 %while.62 = (s32[]{:T(128)}, f32[8,256,64]{2,1,0:T(8,128)}, f32[8,256]{1,0:T(8,128)S(1)}, s32[]{:T(128)}, bf16[4,8,256,64]{2,3,1,0:T(8,128)(2,1)}, /*index=5*/bf16[4,8,256]{2,1,0:T(8,128)(2,1)}, s32[]{:T(128)}, s32[]{:T(128)}) while((s32[]{:T(128)}, f32[8,256,64]{2,1,0:T(8,128)}, f32[8,256]{1,0:T(8,128)S(1)}, s32[]{:T(128)}, ...), condition=%wide.region_6.7_spmd.clone, body=%wide.region_5.6_spmd.clone.sunk | while | flops 532484 | bytes 2379899 | solution.py:36
  195.7 2.5 add_select_fusion.8
  200.9 2.5 add_select_fusion.8
  206.0 2.5 add_select_fusion.8
  209.5 6.0 divide_convert_fusion.2
  218.8 3.2 divide_convert_fusion.3
  223.7 5.4 fusion.174
  229.1 4.1 all-gather.20.cloned.1.call-done
  233.1 7.3 fusion.190
  240.4 2.8 fusion.194
  243.3 2.6 copy.170
  245.8 3.5 fusion.175
  249.4 4.8 fusion.191
  254.1 2.9 fusion.195
  257.0 2.5 copy.185
  259.5 3.5 multiply_reduce_fusion.3
  270.2 3.5 fusion.154
  273.7 5.2 all-gather.5
  278.9 2.5 multiply_convert_fusion.1
  289.3 5.4 all-gather.7
  294.7 2.3 multiply_convert_fusion
  301.0 3.0 fusion.189
  305.5 2.4 fusion.33
  309.5 3.8 fusion.29
  314.8 6.4 fusion.198
  321.2 3.4 fusion.200
  324.8 4.6 while.60
  331.6 5.0 fusion.35
  337.4 4.0 fusion.186
  341.5 4.8 while.61
  346.3 4.6 fusion.188
  353.1 2.3 fusion.27
  359.5 2.7 convolution_add_fusion
  362.3 3.1 fusion.83
  365.4 3.4 convolution_add_fusion.2
  369.4 4.5 fusion.100
  374.0 4.4 convolution_add_fusion.1
  379.0 5.1 fusion.51
  388.6 2.9 fusion.192
  391.9 3.9 fusion.193
  402.6 38.9 %all-reduce.14 = (f32[512]{0:T(512)S(1)}, f32[2048]{0:T(1024)S(1)}, f32[512]{0:T(512)S(1)}, f32[512]{0:T(512)S(1)}, f32[512]{0:T(512)S(1)}, /*index=5*/f32[512]{0:T(512)S(1)}, f32[512]{0:T(512)S(1)}) all-reduce(f32[512]{0:T(512)S(1)} %add.551, f32[2048]{0:T(1024)S(1)} %add.553, ...), channel_id=12, replica_groups=mesh['dp'=8,'seq'=4] {'dp','seq'}, use_global_device_ids=true, to_apply=%region_42.43.clone | all-reduce | flops 5120 | bytes 40960
  445.6 17.3 %reduce-scatter.7.cloned.1.call-done = f32[16,512]{1,0:T(8,128)} async-done(((f32[512,512]{1,0:T(8,128)}), f32[16,512]{1,0:T(8,128)}) %reduce-scatter.7.cloned.1.call-update) | async-done | bytes 32784 | tf_op jit(solution)/shard_map/reduce_scatter | solution.py:427
  462.9 104.5 %reduce-scatter.5.cloned.1.call-done = f32[16,1536]{1,0:T(8,128)} async-done(((f32[512,1536]{1,0:T(8,128)}), f32[16,1536]{1,0:T(8,128)}) %reduce-scatter.5.cloned.1.call-update) | async-done | bytes 98320 | tf_op jit(solution)/shard_map/reduce_scatter | solution.py:426
  567.3 142.8 %reduce-scatter.9.cloned.1.call-done = f32[16,2048]{1,0:T(8,128)} async-done(((f32[512,2048]{1,0:T(8,128)}), f32[16,2048]{1,0:T(8,128)}) %reduce-scatter.9.cloned.1.call-update) | async-done | bytes 131088 | tf_op jit(solution)/shard_map/reduce_scatter | solution.py:429
  710.1 140.2 %reduce-scatter.11.cloned.1.call-done = f32[64,512]{1,0:T(8,128)} async-done(((f32[2048,512]{1,0:T(8,128)}), f32[64,512]{1,0:T(8,128)}) %reduce-scatter.11.cloned.1.call-update) | async-done | bytes 131088 | tf_op jit(solution)/shard_map/reduce_scatter | solution.py:431
  (444 shorter events, 107.1 us)
Async XLA Ops:
  7.2 67.3 %copy-start = (bf16[64,256]{1,0:T(8,128)(2,1)S(1)}, bf16[64,256]{1,0:T(8,128)(2,1)}, u32[]{:S(2)}) copy-start(bf16[64,256]{1,0:T(8,128)(2,1)} %param.23) | copy-start | bytes 98308
  7.2 61.5 %all-gather.16.cloned.1.call-start = ((), (), s32[]{:S(2)}) async-start(), calls=%async_computation.4 | async-start | bytes 1622016 | tf_op jit(solution)/shard_map/all_gather | solution.py:340
  7.9 159.6 %all-gather.24.cloned.1.call-start = ((), (), s32[]{:S(2)}) async-start(), calls=%async_computation.12 | async-start | bytes 1310720 | tf_op jit(solution)/shard_map/all_gather | solution.py:19
  9.5 62.9 %copy-start.23 = (bf16[1,512,512]{1,2,0:T(8,128)(2,1)}, bf16[1,512,512]{1,2,0:T(8,128)(2,1)S(1)}, u32[]{:S(2)}) copy-start(bf16[1,512,512]{1,2,0:T(8,128)(2,1)S(1)} %copy.256) | copy-start | bytes 1572868
  57.7 23.0 %copy-start.103 = (f32[512]{0:T(512)}, f32[512]{0:T(512)S(1)}, u32[]{:S(2)}) copy-start(f32[512]{0:T(512)S(1)} %convert_element_type.371) | copy-start | bytes 6148
  57.9 22.8 %copy-start.26 = (bf16[1,512,512]{1,2,0:T(8,128)(2,1)}, bf16[1,512,512]{1,2,0:T(8,128)(2,1)S(1)}, u32[]{:S(2)}) copy-start(bf16[1,512,512]{1,2,0:T(8,128)(2,1)S(1)} %copy.255) | copy-start | bytes 1572868
  58.2 10.6 %copy-start.85 = (f32[512]{0:T(512)}, f32[512]{0:T(512)S(1)}, u32[]{:S(2)}) copy-start(f32[512]{0:T(512)S(1)} %broadcast_multiply_fusion.9) | copy-start | bytes 6148
  58.3 10.4 %copy-start.96 = (f32[512]{0:T(512)}, f32[512]{0:T(512)S(1)}, u32[]{:S(2)}) copy-start(f32[512]{0:T(512)S(1)} %fusion.68) | copy-start | bytes 6148
  58.5 22.2 %copy-start.98 = (f32[512]{0:T(512)}, f32[512]{0:T(512)S(1)}, u32[]{:S(2)}) copy-start(f32[512]{0:T(512)S(1)} %fusion.70) | copy-start | bytes 6148
  58.5 10.2 %copy-start.87 = (f32[512]{0:T(512)}, f32[512]{0:T(512)S(1)}, u32[]{:S(2)}) copy-start(f32[512]{0:T(512)S(1)} %fusion.164) | copy-start | bytes 6148
  74.1 6.5 copy-start.29
  80.6 108.3 %all-gather.22.cloned.1.call-start = ((), (), s32[]{:S(2)}) async-start(), calls=%async_computation.11 | async-start | bytes 1310720 | tf_op jit(solution)/shard_map/all_gather | solution.py:19
  84.0 6.5 copy-start.30
  84.3 62.1 %copy-start.80 = (f32[512,8]{0,1:T(8,128)}, f32[512,8]{0,1:T(8,128)S(1)}, u32[]{:S(2)}) copy-start(f32[512,8]{0,1:T(8,128)S(1)} %get-tuple-element.699) | copy-start | bytes 49156
  84.3 8.2 copy-start.100
  87.8 49.3 %copy-start.77 = (bf16[2,512,512]{2,1,0:T(8,128)(2,1)S(1)}, bf16[2,512,512]{2,1,0:T(8,128)(2,1)}, u32[]{:S(2)}) copy-start(bf16[2,512,512]{2,1,0:T(8,128)(2,1)} %param.35) | copy-start | bytes 3145732
  90.6 133.1 %all-gather.18.cloned.1.call-start = ((), (), s32[]{:S(2)}) async-start(), calls=%async_computation.5 | async-start | bytes 2162688 | tf_op jit(solution)/shard_map/all_gather | solution.py:343
  91.2 142.0 %all-gather.20.cloned.1.call-start = ((), (), s32[]{:S(2)}) async-start(), calls=%async_computation.6 | async-start | bytes 2162688 | tf_op jit(solution)/shard_map/all_gather | solution.py:345
  91.7 232.9 %all-gather.26.cloned.1.call-start = ((), (), s32[]{:S(2)}) async-start(), calls=%async_computation.13 | async-start | bytes 1310720 | tf_op jit(solution)/shard_map/all_gather | solution.py:44
  146.3 15.6 %copy-start.1 = (f32[8,512,512]{1,2,0:T(8,128)}, f32[8,512,512]{1,2,0:T(8,128)S(1)}, u32[]{:S(2)}) copy-start(f32[8,512,512]{1,2,0:T(8,128)S(1)} %fusion.196) | copy-start | bytes 25165828
  146.3 15.6 %copy-start.15 = (bf16[512,8,256]{0,2,1:T(8,128)(2,1)S(1)}, bf16[512,8,256]{0,2,1:T(8,128)(2,1)}, u32[]{:S(2)}) copy-start(bf16[512,8,256]{0,2,1:T(8,128)(2,1)} %copy-done.14) | copy-start | bytes 6291460
  151.1 10.8 %copy-start.2 = (bf16[512,8,256]{0,2,1:T(8,128)(2,1)}, bf16[512,8,256]{0,2,1:T(8,128)(2,1)S(1)}, u32[]{:S(2)}) copy-start(bf16[512,8,256]{0,2,1:T(8,128)(2,1)S(1)} %get-tuple-element.660) | copy-start | bytes 6291460
  167.5 41.9 %copy-start.82 = (f32[8,512]{1,0:T(8,128)}, f32[8,512]{1,0:T(8,128)S(1)}, u32[]{:S(2)}) copy-start(f32[8,512]{1,0:T(8,128)S(1)} %get-tuple-element.569) | copy-start | bytes 49156
  209.4 9.3 %slice-start.2 = ((s8[8388608]{0:T(1024)(128)(4,1)}), s8[4194304]{0:T(1024)(128)(4,1)S(1)}, s32[]{:S(2)}) async-start(s8[8388608]{0:T(1024)(128)(4,1)} %bitcast.389), calls=%async_computation.17 | async-start | bytes 8388608
  209.4 6.1 copy-start.24
  209.5 6.1 copy-start.36
  209.5 6.1 copy-start.95
  209.5 7.8 copy-start.3
  209.5 9.3 %slice-start.3 = ((s8[8388608]{0:T(1024)(128)(4,1)}), s8[4194304]{0:T(1024)(128)(4,1)S(1)}, s32[]{:S(2)}) async-start(s8[8388608]{0:T(1024)(128)(4,1)} %bitcast.389), calls=%async_computation.18 | async-start | bytes 8388608
  223.4 9.7 %copy-start.107 = (f32[2048]{0:T(1024)S(1)}, f32[2048]{0:T(1024)}, u32[]{:S(2)}) copy-start(f32[2048]{0:T(1024)} %convert_element_type.388) | copy-start | bytes 24580
  233.1 7.3 copy-start.49
  249.3 4.8 copy-start.69
  249.3 4.8 copy-start.50
  259.5 3.6 copy-start.21
  259.5 3.6 copy-start.47
  259.5 3.6 copy-start.48
  263.7 3.9 copy-start.43
  263.7 3.9 copy-start.45
  270.2 71.3 %all-gather.28.cloned.1.call-start = ((), (), s32[]{:S(2)}) async-start(), calls=%async_computation.14 | async-start | bytes 1310720 | tf_op jit(solution)/shard_map/all_gather | solution.py:44
  270.2 11.2 %copy-start.16 = (bf16[512,8,256]{0,2,1:T(8,128)(2,1)S(1)}, bf16[512,8,256]{0,2,1:T(8,128)(2,1)}, u32[]{:S(2)}) copy-start(bf16[512,8,256]{0,2,1:T(8,128)(2,1)} %copy-done.14) | copy-start | bytes 6291460
  281.4 4.0 copy-start.35
  281.4 4.1 copy-start.41
  281.4 4.1 copy-start.81
  287.6 20.4 %copy-start.38 = (bf16[512,8,64]{0,2,1:T(8,128)(2,1)}, bf16[512,8,64]{0,2,1:T(8,128)(2,1)S(1)}, u32[]{:S(2)}) copy-start(bf16[512,8,64]{0,2,1:T(8,128)(2,1)S(1)} %divide_convert_fusion) | copy-start | bytes 1572868
  287.6 9.4 %copy-start.12 = (bf16[512,8,256]{0,2,1:T(8,128)(2,1)S(1)}, bf16[512,8,256]{0,2,1:T(8,128)(2,1)}, u32[]{:S(2)}) copy-start(bf16[512,8,256]{0,2,1:T(8,128)(2,1)} %copy-done.11) | copy-start | bytes 6291460
  297.0 4.0 copy-start.34
  309.4 153.5 %reduce-scatter.7.cloned.1.call-start = ((), (), s32[]{:S(2)}) async-start(), calls=%async_computation.8 | async-start | bytes 1081344 | tf_op jit(solution)/shard_map/reduce_scatter | solution.py:427
  309.5 3.8 copy-start.53
  309.5 3.8 copy-start.57
  309.5 3.8 copy-start.67
  314.8 6.4 copy-start.7
  324.6 242.7 %reduce-scatter.5.cloned.1.call-start = ((), (), s32[]{:S(2)}) async-start(), calls=%async_computation.7 | async-start | bytes 3244032 | tf_op jit(solution)/shard_map/reduce_scatter | solution.py:426
  331.5 5.1 copy-start.32
  331.6 5.9 copy-start.33
  346.3 4.8 copy-start.31
  351.2 4.8 slice-start
  353.1 5.2 copy-start.76
  362.2 347.9 %reduce-scatter.9.cloned.1.call-start = ((), (), s32[]{:S(2)}) async-start(), calls=%async_computation.9 | async-start | bytes 4325376 | tf_op jit(solution)/shard_map/reduce_scatter | solution.py:429
  368.7 481.6 %reduce-scatter.11.cloned.1.call-start = ((), (), s32[]{:S(2)}) async-start(), calls=%async_computation.10 | async-start | bytes 4325376 | tf_op jit(solution)/shard_map/reduce_scatter | solution.py:431
  369.4 4.5 copy-start.70
  369.4 4.5 copy-start.79
  379.0 5.1 copy-start.68
  379.0 5.1 copy-start.113
  391.9 5.7 copy-start.99
  (65 other events, 142.1 us)
Sparse Core Ops, SparseCore 0:
  10.9 57.7 all-gather.15
  80.8 15.8 all-gather.23
  98.2 17.6 all-gather.21
  118.6 56.4 all-gather.17
  177.9 55.2 all-gather.19
  270.3 15.5 all-gather.25
  309.5 15.5 all-gather.27
  328.0 134.8 reduce-scatter.6
  469.8 97.5 reduce-scatter.4
  570.1 139.9 reduce-scatter.8
  713.0 137.2 reduce-scatter.10
where the time goes:
time: 867 us; the launch traced here: 857 us
  waiting for transfers between devices  421 us (49%)
  matrix products  171 us (20%)
  blocking collectives  146 us (17%)
  local copies, waits for them, and re-layouts  66.6 us (8%)
  other arithmetic  34.8 us (4%)
  between operations  16 us (2%)
    reduce_scatter x1, waiting for transfers between devices, local(): lax.psum_scatter(upper_totals[2], ('dp', 'seq'), scatter_dimension=0, til...  143 us
    reduce_scatter x1, waiting for transfers between devices, local(): lax.psum_scatter(upper_totals[4], ('dp', 'seq'), scatter_dimension=0, til...  140 us
    reduce_scatter x1, waiting for transfers between devices, local(): lax.psum_scatter(lower_totals[0], ('dp', 'seq'), scatter_dimension=0, til...  104 us
    unnamed x2, blocking collectives  81.1 us
    all_gather x1, blocking collectives, local(): lax.all_gather(output_weight, ('dp', 'seq'), axis=0, tiled=True)  43.9 us
    unnamed x263, local copies, waits for them, and re-layouts  32.4 us
    select_n x16, other arithmetic, hop(): return jax.tree.map(lambda a, b: jnp.where(reached, a, b), new, before)  22.2 us
  transfers between devices with their start and end apart: 11, of which 6 were waited for; matrix products, arithmetic and copies ran while one was open for 25% of the time, Pallas kernels for 0%

commit v1 on v0

--- a/solution.py
+++ b/solution.py
@@ -7,6 +7,342 @@
 
 H = 8
 DH = 64
+
+from jax.experimental import pallas as pl
+from jax.experimental.pallas import tpu as pltpu
+
+MESH = pl.DeviceIdType.MESH
+
+
+class Geometry:
+    def __init__(self, mesh):
+        dp, seq = mesh.shape["dp"], mesh.shape["seq"]
+        self.C = 2
+        self.Y = seq // 2
+        self.X = 1 << ((dp.bit_length() - 1) // 2)
+        self.Z = dp // self.X
+
+    def me(self):
+        dp, seq = lax.axis_index("dp"), lax.axis_index("seq")
+        return dp // self.X, dp % self.X, seq // 2, seq % 2
+
+    def device(self, z, x, y, c):
+        return (z * self.X + x, y * 2 + c)
+
+    def barrier(self):
+        z, x, y, c = self.me()
+        peers = [self.device(z, x, y, 1 - c)]
+        peers += [self.device((z + k) % self.Z, x, y, c) for k in range(1, self.Z)]
+        peers += [self.device(z, (x + k) % self.X, y, c) for k in range(1, self.X)]
+        peers += [self.device(z, x, (y + k) % self.Y, c) for k in range(1, self.Y)]
+        semaphore = pltpu.get_barrier_semaphore()
+        for peer in peers:
+            pl.semaphore_signal(semaphore, inc=1, device_id=peer, device_id_type=MESH)
+        pl.semaphore_wait(semaphore, len(peers))
+
+
+class Lane:
+    def __init__(self):
+        self.count = 0
+        self.send = self.recv = None
+
+    def take(self, n=1):
+        first = self.count
+        self.count += n
+        return first
+
+
+def remote(lane, index, src, dst, device):
+    return pltpu.make_async_remote_copy(
+        src_ref=src, dst_ref=dst, send_sem=lane.send.at[index], recv_sem=lane.recv.at[index],
+        device_id=device, device_id_type=MESH)
+
+
+class Gather:
+    def __init__(self, geo, lane):
+        self.geo, self.lane = geo, lane
+        self.zs = lane.take(geo.Z - 1)
+        self.second = lane.take(max(geo.X, geo.Y) - 1)
+        self.third = lane.take(max(geo.X, geo.Y) - 1)
+        self.core = lane.take()
+
+    def bind(self, own, full):
+        self.own, self.full = own, full
+
+    def z_copies(self, incoming):
+        g = self.geo
+        z, x, y, c = g.me()
+        for k in range(1, g.Z):
+            if incoming:
+                slot = self.full.at[(z + g.Z - k) % g.Z, x, y, c]
+                yield remote(self.lane, self.zs + k - 1, slot, slot, g.device((z + k) % g.Z, x, y, c))
+            else:
+                yield remote(self.lane, self.zs + k - 1, self.own, self.full.at[z, x, y, c],
+                             g.device((z + k) % g.Z, x, y, c))
+
+    def axis_copies(self, phase, order, incoming):
+        g = self.geo
+        z, x, y, c = g.me()
+        base = self.second if phase == 2 else self.third
+        along_x = (phase == 2) == (order == 0)
+        size = g.X if along_x else g.Y
+        for k in range(1, size):
+            if along_x:
+                source = (x + g.X - k) % g.X if incoming else x
+                device = g.device(z, (x + k) % g.X, y, c)
+                slot = self.full.at[:, source, y, c] if phase == 2 else self.full.at[:, source, :, c]
+            else:
+                source = (y + g.Y - k) % g.Y if incoming else y
+                device = g.device(z, x, (y + k) % g.Y, c)
+                slot = self.full.at[:, x, source, c] if phase == 2 else self.full.at[:, :, source, c]
+            yield remote(self.lane, base + k - 1, slot, slot, device)
+
+    def both(self, action):
+        c = self.geo.me()[3]
+        for order in range(2):
+            @pl.when(c == order)
+            def _():
+                action(order)
+
+    def step(self, n):
+        g = self.geo
+        z, x, y, c = g.me()
+        if n == 0:
+            for copy in self.z_copies(False):
+                copy.start()
+            self.full[z, x, y, c] = self.own[...]
+        elif n == 1:
+            for copy in self.z_copies(True):
+                copy.wait_recv()
+            self.both(lambda order: [copy.start() for copy in self.axis_copies(2, order, False)])
+        elif n == 2:
+            def go(order):
+                for copy in self.axis_copies(2, order, True):
+                    copy.wait_recv()
+                for copy in self.axis_copies(3, order, False):
+                    copy.start()
+            self.both(go)
+        elif n == 3:
+            def go(order):
+                for copy in self.axis_copies(3, order, True):
+                    copy.wait_recv()
+            self.both(go)
+            slot = self.full.at[:, :, :, c]
+            remote(self.lane, self.core, slot, slot, g.device(z, x, y, 1 - c)).start()
+        else:
+            slot = self.full.at[:, :, :, 1 - c]
+            remote(self.lane, self.core, slot, slot, g.device(z, x, y, 1 - c)).wait_recv()
+
+    def drain(self):
+        g = self.geo
+        z, x, y, c = g.me()
+        for copy in self.z_copies(False):
+            copy.wait_send()
+
+        def go(order):
+            for phase in (2, 3):
+                for copy in self.axis_copies(phase, order, False):
+                    copy.wait_send()
+        self.both(go)
+        slot = self.full.at[:, :, :, c]
+        remote(self.lane, self.core, slot, slot, g.device(z, x, y, 1 - c)).wait_send()
+
+
+class Scatter:
+    def __init__(self, geo, lane):
+        self.geo, self.lane = geo, lane
+        self.core = lane.take()
+        self.first = lane.take(max(geo.X, geo.Y) - 1)
+        self.second = lane.take(max(geo.X, geo.Y) - 1)
+        self.zs = lane.take(geo.Z - 1)
+
+    @staticmethod
+    def scratch(geo, rows, width):
+        wide = max(geo.X, geo.Y)
+        kind = jnp.bfloat16
+        return [
+            pltpu.VMEM((geo.Z, geo.X, geo.Y, rows, width), kind),
+            pltpu.VMEM((wide - 1, geo.Z, wide, rows, width), kind),
+            pltpu.VMEM((wide - 1, geo.Z, rows, width), kind),
+            pltpu.VMEM((geo.Z - 1, rows, width), kind),
+        ]
+
+    def bind(self, part, out, buffers):
+        self.part, self.out = part, out
+        self.rc, self.ra, self.rb, self.rz = buffers
+
+    def both(self, action):
+        c = self.geo.me()[3]
+        for order in range(2):
+            @pl.when(c == order)
+            def _():
+                action(order)
+
+    def core_copy(self):
+        z, x, y, c = self.geo.me()
+        return remote(self.lane, self.core, self.part.at[:, :, :, 1 - c], self.rc,
+                      self.geo.device(z, x, y, 1 - c))
+
+    def axis_copies(self, phase, order):
+        g = self.geo
+        z, x, y, c = g.me()
+        base = self.first if phase == 1 else self.second
+        along_x = (phase == 1) == (order == 1)
+        for k in range(1, g.X if along_x else g.Y):
+            if along_x:
+                far = (x + k) % g.X
+                device = g.device(z, far, y, c)
+                src = self.part.at[:, far, :, c] if phase == 1 else self.part.at[:, far, y, c]
+                dst = self.ra.at[k - 1, :, pl.ds(0, g.Y)] if phase == 1 else self.rb.at[k - 1]
+            else:
+                far = (y + k) % g.Y
+                device = g.device(z, x, far, c)
+                src = self.part.at[:, :, far, c] if phase == 1 else self.part.at[:, x, far, c]
+                dst = self.ra.at[k - 1, :, pl.ds(0, g.X)] if phase == 1 else self.rb.at[k - 1]
+            yield remote(self.lane, base + k - 1, src, dst, device)
+
+    def z_copies(self):
+        g = self.geo
+        z, x, y, c = g.me()
+        for k in range(1, g.Z):
+            far = (z + k) % g.Z
+            yield remote(self.lane, self.zs + k - 1, self.part.at[far, x, y, c], self.rz.at[k - 1],
+                         g.device(far, x, y, c))
+
+    def step(self, n):
+        g = self.geo
+        z, x, y, c = g.me()
+        wide = lambda ref: ref.astype(jnp.float32)
+        if n == 0:
+            self.core_copy().start()
+        elif n == 1:
+            self.core_copy().wait_recv()
+
+            def add(i, _):
+                total = wide(self.part[i, :, :, c]) + wide(self.rc[i])
+                self.part[i, :, :, c] = total.astype(jnp.bfloat16)
+                return 0
+            lax.fori_loop(0, g.Z, add, 0)
+            self.both(lambda order: [copy.start() for copy in self.axis_copies(1, order)])
+        elif n == 2:
+            def go(order):
+                copies = list(self.axis_copies(1, order))
+                for copy in copies:
+                    copy.wait_recv()
+                count = len(copies)
+                if order == 0:
+                    def add(i, _):
+                        total = wide(self.part[i, :, y, c])
+                        for k in range(count):
+                            total += wide(self.ra[k, i, : g.X])
+                        self.part[i, :, y, c] = total.astype(jnp.bfloat16)
+                        return 0
+                else:
+                    def add(i, _):
+                        total = wide(self.part[i, x, :, c])
+                        for k in range(count):
+                            total += wide(self.ra[k, i, : g.Y])
+                        self.part[i, x, :, c] = total.astype(jnp.bfloat16)
+                        return 0
+                lax.fori_loop(0, g.Z, add, 0)
+                for copy in self.axis_copies(2, order):
+                    copy.start()
+            self.both(go)
+        elif n == 3:
+            def go(order):
+                copies = list(self.axis_copies(2, order))
+                for copy in copies:
+                    copy.wait_recv()
+
+                def add(i, _):
+                    total = wide(self.part[i, x, y, c])
+                    for k in range(len(copies)):
+                        total += wide(self.rb[k, i])
+                    self.part[i, x, y, c] = total.astype(jnp.bfloat16)
+                    return 0
+                lax.fori_loop(0, g.Z, add, 0)
+            self.both(go)
+            for copy in self.z_copies():
+                copy.start()
+        else:
+            total = wide(self.part[z, x, y, c])
+            for k, copy in enumerate(self.z_copies()):
+                copy.wait_recv()
+                total += wide(self.rz[k])
+            self.out[...] = total
+
+    def drain(self):
+        self.core_copy().wait_send()
+
+        def go(order):
+            for phase in (1, 2):
+                for copy in self.axis_copies(phase, order):
+                    copy.wait_send()
+        self.both(go)
+        for copy in self.z_copies():
+            copy.wait_send()
+
+
+def run_steps(tasks):
+    for n in range(5 + len(tasks) - 1):
+        for i, task in enumerate(tasks):
+            if 0 <= n - i < 5:
+                task.step(n - i)
+    for task in tasks:
+        task.drain()
+
+
+def gather_all(geo, shards):
+    lane = Lane()
+    tasks = [Gather(geo, lane) for _ in shards]
+    n = len(shards)
+
+    def body(*refs):
+        own, full = refs[:n], refs[n:2 * n]
+        lane.send, lane.recv = refs[2 * n], refs[2 * n + 1]
+        for task, a, b in zip(tasks, own, full):
+            task.bind(a, b)
+        geo.barrier()
+        run_steps(tasks)
+
+    vmem = pl.BlockSpec(memory_space=pltpu.VMEM)
+    return pl.pallas_call(
+        body,
+        out_shape=[jax.ShapeDtypeStruct((geo.Z, geo.X, geo.Y, 2) + s.shape, s.dtype) for s in shards],
+        in_specs=[vmem] * n, out_specs=[vmem] * n,
+        scratch_shapes=[pltpu.SemaphoreType.DMA((lane.count,)), pltpu.SemaphoreType.DMA((lane.count,))],
+        compiler_params=pltpu.CompilerParams(collective_id=0, has_side_effects=True, vmem_limit_bytes=56 << 20),
+    )(*shards)
+
+
+def scatter_all(geo, parts):
+    lane = Lane()
+    tasks = [Scatter(geo, lane) for _ in parts]
+    n = len(parts)
+
+    def body(*refs):
+        part, out = refs[:n], refs[n:2 * n]
+        held = refs[2 * n:3 * n]
+        buffers = refs[3 * n:7 * n]
+        lane.send, lane.recv = refs[7 * n], refs[7 * n + 1]
+        for i, task in enumerate(tasks):
+            held[i][...] = part[i][...]
+            task.bind(held[i], out[i], buffers[4 * i:4 * i + 4])
+        geo.barrier()
+        run_steps(tasks)
+
+    vmem = pl.BlockSpec(memory_space=pltpu.VMEM)
+    scratch = [pltpu.VMEM(p.shape, p.dtype) for p in parts]
+    for p in parts:
+        scratch += Scatter.scratch(geo, p.shape[-2], p.shape[-1])
+    scratch += [pltpu.SemaphoreType.DMA((lane.count,)), pltpu.SemaphoreType.DMA((lane.count,))]
+    return pl.pallas_call(
+        body,
+        out_shape=[jax.ShapeDtypeStruct(p.shape[-2:], jnp.float32) for p in parts],
+        in_specs=[vmem] * n, out_specs=[vmem] * n,
+        scratch_shapes=scratch,
+        compiler_params=pltpu.CompilerParams(collective_id=1, has_side_effects=True, vmem_limit_bytes=56 << 20),
+    )(*parts)
 
 
 epsilon = 1e-05
@@ -211,7 +547,7 @@
     )
     active_float, gelu_pull = jax.vjp(gelu_tanh, hidden)
     active = active_float.astype(jnp.bfloat16)
-    stored = {"front": pieces, "carry": block_carry}
+    stored = {"front": pieces, "carry": block_carry, "middle": middle}
     down_term = upstream.astype(jnp.bfloat16)
     stored["down"] = jnp.einsum("rf,rd->fd", active, down_term, preferred_element_type=jnp.float32)
     stored["down_bias"] = jnp.sum(upstream, axis=0)
@@ -318,6 +654,41 @@
     )
     inputs_part, gain_one_grad, shift_one_grad = first_pull(normed_grad)
     return (stored["middle_grad"] + inputs_part, input_part, gain_one_grad, shift_one_grad)
+
+
+def fused(geo, args):
+    (tokens, feature_matrix, input_weight, output_weight, output_bias, up_weight, up_bias, down_weight,
+     down_bias, first_gain, first_shift, second_gain, second_shift, cotangent) = args
+    small = jnp.stack([output_bias, down_bias, first_gain, first_shift, second_gain, second_shift], axis=1)
+    small = jnp.concatenate([small, up_bias.reshape(-1, 4), jnp.zeros((small.shape[0], 118), small.dtype)], axis=1)
+    full = gather_all(geo, [small, input_weight, output_weight, up_weight, down_weight])
+    small, wi, wo, wu, wd = [f.reshape(-1, f.shape[-1]) for f in full]
+    params = (wi, wo, small[:, 0], wu, small[:, 6:10].reshape(-1), wd, small[:, 1], small[:, 2], small[:, 3],
+              small[:, 4], small[:, 5])
+    micros = tokens.shape[0]
+    carries, results, stored_list, later_list = [], [], [], []
+    for m in range(micros):
+        pieces = front(tokens[m], feature_matrix, params)
+        carry = prefix((pieces[8], pieces[9]), "seq", add_pair, (jnp.zeros_like(pieces[8]), jnp.zeros_like(pieces[9])))
+        stored = upper_back(tokens[m], cotangent[m].astype(jnp.float32), feature_matrix, params, carry)
+        results.append(feed(stored["middle"], params))
+        stored_list.append(stored)
+        later_list.append(prefix_2((stored["state_grad"], stored["sum_grad"]), "seq", add_pair,
+                                   (jnp.zeros_like(stored["state_grad"]), jnp.zeros_like(stored["sum_grad"]))))
+    names = ["out", "out_bias", "up", "up_bias", "down", "down_bias", "gain_two", "shift_two"]
+    upper = [sum(s[name] for s in stored_list) for name in names]
+    token_grads, lower = [], None
+    for m in range(micros):
+        tg, *parts = lower_back(stored_list[m], later_list[m], feature_matrix, params)
+        token_grads.append(tg)
+        lower = parts if lower is None else [a + b for a, b in zip(lower, parts)]
+    shape = (geo.Z, geo.X, geo.Y, 2)
+    cut = lambda a: a.astype(jnp.bfloat16).reshape(shape + (-1, a.shape[-1]))
+    vec = jnp.stack([upper[1], upper[5], lower[1], lower[2], upper[6], upper[7]], axis=1)
+    vec = jnp.concatenate([vec, upper[3].reshape(-1, 4), jnp.zeros((vec.shape[0], 118), jnp.float32)], axis=1)
+    down, up, out, inp, vec = scatter_all(geo, [cut(upper[4]), cut(upper[2]), cut(upper[0]), cut(lower[0]), cut(vec)])
+    return (jnp.stack(results), jnp.stack(token_grads), inp, out, vec[:, 0], up, vec[:, 6:10].reshape(-1), down,
+            vec[:, 1], vec[:, 2], vec[:, 3], vec[:, 4], vec[:, 5])
 
 
 def local(
@@ -484,4 +855,11 @@
         P(("dp", "seq")),
         P(("dp", "seq")),
     )
-    return jax.shard_map(local, mesh=mesh, in_specs=in_specs, out_specs=out_specs, check_vma=False)
+    geo = Geometry(mesh)
+    rows = 512 // (mesh.shape["dp"] * mesh.shape["seq"])
+    if rows % 16 == 0:
+        def body(*args):
+            return fused(geo, args)
+    else:
+        body = local
+    return jax.shard_map(body, mesh=mesh, in_specs=in_specs, out_specs=out_specs, check_vma=False)

time: 867 us -> 464 us (0.54)
  waiting for transfers between devices: 421 us -> 0.09 us
  blocking collectives: 146 us -> 21.1 us
  Pallas kernels: 0 us -> 111 us
  local copies, waits for them, and re-layouts: 66.6 us -> 84.2 us
  other arithmetic: 34.8 us -> 44.1 us
    reduce_scatter x4 -> x0, waiting for transfers between devices: 405 us -> none  [the longest x1 143 us: local(): lax.psum_scatter(upper_totals[2], ('dp', 'seq'), scatter_dimension=0, til...]
    pallas_call x0 -> x2, Pallas kernels: none -> 111 us  [the longest x1 56.4 us: gather_all(): pl.pallas_call(body, out_shape=[jax.ShapeDtypeStruct((geo.Z, geo.X, geo.Y...]
    unnamed x2 -> x0, blocking collectives: 81.1 us -> none
    all_gather x1 -> x0, blocking collectives: 43.9 us -> none  [local(): lax.all_gather(output_weight, ('dp', 'seq'), axis=0, tiled=True)]
    all_gather x3 -> x0, waiting for transfers between devices: 14.3 us -> none  [the longest x1 10.2 us: local(): lax.all_gather(input_weight, ('dp', 'seq'), axis=0, tiled=True)]
    unnamed x263 -> x269, local copies, waits for them, and re-layouts: 32.4 us -> 29.8 us
  transfers between devices with their start and end apart: 11 -> 4, of which waited for: 6 -> 0; matrix products, arithmetic and copies ran while one was open for 25% -> 29% of each run, Pallas kernels for 0% -> 0%
where the time goes in v1:
time: 464 us; the launch traced here: 455 us
  matrix products  178 us (38%)
  Pallas kernels  111 us (24%)
  local copies, waits for them, and re-layouts  84.2 us (18%)
  other arithmetic  44.1 us (10%)
  blocking collectives  21.1 us (5%)
  between operations  15.6 us (3%)
    pallas_call x1, Pallas kernels, gather_all(): pl.pallas_call(body, out_shape=[jax.ShapeDtypeStruct((geo.Z, geo.X, geo.Y...  56.4 us
    pallas_call x1, Pallas kernels, scatter_all(): pl.pallas_call(body, out_shape=[jax.ShapeDtypeStruct(p.shape[-2:], jnp.fl...  54.8 us
    unnamed x269, local copies, waits for them, and re-layouts  29.8 us
    select_n x16, other arithmetic, hop(): return jax.tree.map(lambda a, b: jnp.where(reached, a, b), new, before)  21.9 us
    dot_general x2, matrix products, attend(): jnp.einsum('ihm,jhm->hij', query_reduced, key_reduced, preferred_element_...  16.5 us
    dot_general x4, matrix products, favor_map(): jnp.einsum('rhd,dm->rhm', proj_low, matrix, preferred_element_type=jnp.fl...  16.4 us
    dynamic_slice x16, local copies, waits for them, and re-layouts, hop(): part[k].astype(own.dtype)  15.8 us
    dot_general x2, matrix products, lower_back(): jnp.einsum('gvw,vcw->gvc', numerator_grad, running_prefix_state.astype(jn...  12.8 us
  transfers between devices with their start and end apart: 4, of which 0 were waited for; matrix products, arithmetic and copies ran while one was open for 29% of the time, Pallas kernels for 0%

profile of v1, /device:TPU:0, one launch (start us, length us, event | category | flops | bytes accessed | tf_op | source)
XLA Modules:
  0.0 454.9 jit_solution(9387790050470347951)
XLA Ops:
  13.2 56.4 %shard_map.237 = (bf16[4,2,2,2,16,128]{5,4,3,2,1,0:T(8,128)(2,1)}, bf16[4,2,2,2,16,1536]{5,4,3,2,1,0:T(8,128)(2,1)}, bf16[4,2,2,2,16,512]{5,4,3,2,1,0:T(8,128)(2...) custom-call(bf16[16,128]{1,0:T(8,128)(2,1)} %concatenate.8.refs_0_, ...), custom_call_target="tpu_custom_call" | custom-call | tf_op jit(solution)/shard_map/pallas_call | solution.py:309
  73.1 2.3 convolution_convert_fusion
  77.5 4.0 fusion.170
  84.8 3.7 convolution_convert_fusion.1
  90.6 3.4 fusion.168
  98.2 4.2 fusion.22
  102.4 6.1 %fusion.186 = f32[8,512,512]{1,2,0:T(8,128)} fusion(bf16[512,8,256]{0,2,1:T(8,128)(2,1)S(1)} %get-tuple-element.678, bf16[512,8,256]{0,2,1:T(8,128)(2,1)} %copy-done.4), kind=kOutput, calls=%fused_computation.339 | convolution fusion | flops 1073741824 | bytes 12582912 | tf_op jit(solution)/shard_map/ihm,jhm->hij/dot_general | solution.py:478
  108.5 4.8 %fusion.20 = (bf16[512,8,256]{0,2,1:T(8,128)(2,1)}, f32[512,8,256]{0,2,1:T(8,128)}) fusion(f32[512,8]{0,1:T(8,128)S(1)} %get-tuple-element.716, bf16[64,256]{1,0:T(8,128)(2,1)S(1)} %copy-done, bf16[512,3,8,64]{0,3,2,1:T(8,128)(2,1)} %bitcast.430), kind=kOutput, calls=%fused_computation.63 | convolution fusion | flops 138412032 | bytes 6864896 | tf_op jit(solution)/shard_map/rhd,dm->rhm/dot_general | solution.py:421
  113.4 5.2 %all-gather.3 = bf16[32,256]{1,0:T(8,128)(2,1)S(1)} all-gather(bf16[8,256]{1,0:T(8,128)(2,1)S(1)} %copy-done.118), channel_id=5, replica_groups=mesh['dp'=8,'seq'=4] {'seq'}, dimensions={0}, use_global_device_ids=true | all-gather | bytes 20480 | tf_op jit(solution)/shard_map/all_gather | solution.py:355
  120.9 5.6 %all-gather.1 = bf16[32,256]{1,0:T(8,128)(2,1)} all-gather(bf16[8,256]{1,0:T(8,128)(2,1)S(1)} %get-tuple-element.658), channel_id=3, replica_groups=mesh['dp'=8,'seq'=4] {'seq'}, dimensions={0}, use_global_device_ids=true | all-gather | bytes 20480 | tf_op jit(solution)/shard_map/all_gather | solution.py:355
  126.5 2.2 fusion.172
  132.8 10.4 %multiply_reduce_fusion.1 = (f32[8,512]{1,0:T(8,128)}, f32[8,512]{1,0:T(8,128)S(1)}, f32[8,512,512]{1,2,0:T(8,128)}) fusion(f32[512,512]{0,1:T(8,128)S(1)} %fusion.95, f32[8,512,512]{1,2,0:T(8,128)} %fusion.186, bf16[512,8,256]{0,2,1:T(8,128)(2,1)} %get-tuple-element.681, bf16[512,8,256]{0,2,1:T(8,128)(2,1)} %copy-done.6), kind=kOutput, calls=%fused_computation.16 | convolution fusion | flops 1082122240 | bytes 22052864 | tf_op jit(solution)/shard_map/ihm,jhm->hij/dot_general | solution.py:478
  143.2 17.7 %while.63 = (s32[]{:T(128)}, f32[8,256,64]{2,1,0:T(8,128)}, f32[8,256]{1,0:T(8,128)S(1)}, s32[]{:T(128)}, bf16[4,8,256,64]{2,3,1,0:T(8,128)(2,1)}, /*index=5*/bf16[4,8,256]{2,1,0:T(8,128)(2,1)S(1)}, s32[]{:T(128)}, s32[]{:T(128)}) while((s32[]{:T(128)}, f32[8,256,64]{2,1,0:T(8,128)}, f32[8,256]{1,0:T(8,128)S(1)}, s32[]{:T(128)}, ...), condition=%wide.region_16.17_spmd.clone, body=%wide.region_15.16_spmd.clone.sunk | while | flops 532484 | bytes 2379899 | solution.py:372
  145.4 2.1 add_select_fusion.10
  149.6 2.5 add_select_fusion.10
  154.0 2.5 add_select_fusion.10
  158.5 2.5 add_select_fusion.10
  163.6 5.8 %divide_convert_fusion.2 = (bf16[512,8,64]{0,2,1:T(8,128)(2,1)S(1)}, f32[512,8,64]{0,2,1:T(8,128)}) fusion(f32[512,8]{0,1:T(8,128)S(1)} %fusion.146, f32[8,64,512]{2,1,0:T(8,128)S(1)} %fusion.122, f32[8,512,512]{1,2,0:T(8,128)} %fusion.186, f32[512,512]{0,1:T(8,128)S(1)} %fusion.95, bf16[512,3,8,64]{0,3,2,1:T(8,128)(2,1)} %bitcast.422), kind=kOutput, calls=%fused_computation.191 | convolution fusion | flops 273416192 | bytes 12599296 | tf_op jit(solution)/shard_map/hij,jhd->ihd/dot_general | solution.py:484
  171.7 20.2 %while.62 = (s32[]{:T(128)}, f32[8,256,64]{2,1,0:T(8,128)}, f32[8,256]{1,0:T(8,128)S(1)}, s32[]{:T(128)}, bf16[4,8,256,64]{2,3,1,0:T(8,128)(2,1)}, /*index=5*/bf16[4,8,256]{2,1,0:T(8,128)(2,1)}, s32[]{:T(128)}, s32[]{:T(128)}) while((s32[]{:T(128)}, f32[8,256,64]{2,1,0:T(8,128)}, f32[8,256]{1,0:T(8,128)S(1)}, s32[]{:T(128)}, ...), condition=%wide.region_6.7_spmd.clone, body=%wide.region_5.6_spmd.clone.sunk | while | flops 532484 | bytes 2379899 | solution.py:372
  173.7 2.2 add_select_fusion.8
  178.5 2.5 add_select_fusion.8
  183.6 2.5 add_select_fusion.8
  188.7 2.5 add_select_fusion.8
  191.9 2.5 fusion.143
  194.4 2.4 fusion.125
  196.9 5.9 %divide_convert_fusion.3 = (bf16[512,8,64]{0,2,1:T(8,128)(2,1)S(1)}, f32[512,8,64]{0,2,1:T(8,128)}) fusion(f32[512,8]{0,1:T(8,128)S(1)} %fusion.145, f32[8,64,512]{2,1,0:T(8,128)S(1)} %fusion.125, f32[8,512,512]{1,2,0:T(8,128)} %get-tuple-element.684, f32[512,512]{0,1:T(8,128)S(1)} %fusion.95, bf16[512,3,8,64]{0,3,2,1:T(8,128)(2,1)} %bitcast.431), kind=kOutput, calls=%fused_computation.194 | convolution fusion | flops 273416192 | bytes 12599296 | tf_op jit(solution)/shard_map/hij,jhd->ihd/dot_general | solution.py:484
  207.0 2.2 copy-done.124
  209.2 4.2 fusion.184
  213.5 3.1 fusion.54
  216.6 3.0 fusion.52
  219.6 4.9 %fusion.185 = (f32[2048]{0:T(1024)S(1)}, bf16[512,2048]{1,0:T(8,128)(2,1)}) fusion(f32[512,2048]{1,0:T(8,128)S(1)} %fusion.165, f32[2048]{0:T(1024)S(1)} %copy-done.119, bf16[2048,512]{1,0:T(8,128)(2,1)S(1)} %bitcast.484, bf16[2,512,512]{2,1,0:T(8,128)(2,1)S(1)} %copy-done.77), kind=kOutput, calls=%fused_computation.338 | convolution fusion | flops 1096808448 | bytes 8929280 | tf_op jit(solution)/shard_map/rd,fd->rf/dot_general | solution.py:554
  224.5 2.3 fusion.182
  226.8 2.5 copy.200
  229.4 4.5 fusion.183
  233.8 2.6 copy.216
  236.4 2.9 multiply_reduce_fusion.3
  245.6 2.6 multiply_convert_fusion.1
  248.3 3.2 fusion.188
  251.5 3.2 fusion.187
  258.0 2.5 multiply_convert_fusion
  260.5 3.4 fusion.190
  263.9 3.5 fusion.189
  267.5 3.3 fusion.91
  273.8 2.9 copy.241
  276.7 3.3 fusion.139
  280.1 5.2 %all-gather.5 = bf16[32,256]{1,0:T(8,128)(2,1)S(1)} all-gather(bf16[8,256]{1,0:T(8,128)(2,1)S(1)} %bitcast.471), channel_id=7, replica_groups=mesh['dp'=8,'seq'=4] {'seq'}, dimensions={0}, use_global_device_ids=true | all-gather | bytes 20480 | tf_op jit(solution)/shard_map/all_gather | solution.py:380
  285.3 7.6 %fusion.177 = (f32[512,8]{0,1:T(8,128)S(1)}, f32[512,8,256]{0,2,1:T(8,128)}) fusion(f32[512,8]{0,1:T(8,128)S(1)} %copy-done.87, f32[512,8,256]{0,2,1:T(8,128)} %get-tuple-element.682, f32[8,256]{1,0:T(8,128)S(1)} %get-tuple-element.408, f32[512,8]{0,1:T(8,128)S(1)} %multiply_divide_fusion.1, f32[8,256,512]{2,1,0:T(8,128)} %fusion.187, ...), kind=kOutput, calls=%fused_computation.330 | convolution fusion | flops 142733312 | bytes 13688832 | tf_op jit(solution)/shard_map/gvw,vcw->gvc/dot_general | solution.py:619
  295.2 5.2 %all-gather.7 = bf16[32,256]{1,0:T(8,128)(2,1)S(1)} all-gather(bf16[8,256]{1,0:T(8,128)(2,1)S(1)} %bitcast.472), channel_id=9, replica_groups=mesh['dp'=8,'seq'=4] {'seq'}, dimensions={0}, use_global_device_ids=true | all-gather | bytes 20480 | tf_op jit(solution)/shard_map/all_gather | solution.py:380
  300.4 2.7 add_convert_fusion
  307.2 3.0 fusion.67
  310.8 5.2 %fusion.179 = (f32[512,8]{0,1:T(8,128)S(1)}, f32[512,8,256]{0,2,1:T(8,128)}) fusion(f32[512,8]{0,1:T(8,128)S(1)} %get-tuple-element.714, f32[512,8,256]{0,2,1:T(8,128)} %get-tuple-element.679, f32[8,256]{1,0:T(8,128)S(1)} %get-tuple-element.413, f32[512,8]{0,1:T(8,128)S(1)} %multiply_divide_fusion, f32[8,256,512]{2,1,0:T(8,128)S(1)} %copy-done.15, ...), kind=kOutput, calls=%fused_computation.332 | convolution fusion | flops 142733312 | bytes 13688832 | tf_op jit(solution)/shard_map/gvw,vcw->gvc/dot_general | solution.py:619
  318.2 3.6 add_convert_fusion.1
  321.9 3.6 fusion.65
  325.6 4.6 %while.60 = (s32[]{:T(128)}, f32[8,256,64]{2,1,0:T(8,128)S(1)}, f32[8,256]{1,0:T(8,128)S(1)}, s32[]{:T(128)}, bf16[4,8,256,64]{2,3,1,0:T(8,128)(2,1)}, /*index=5...) while((s32[]{:T(128)}, f32[8,256,64]{2,1,0:T(8,128)S(1)}, ...), condition=%wide.region_25.26_spmd, body=%wide.region_24.25_spmd.sunk | while | flops 266246 | bytes 2379939 | solution.py:397
  330.2 2.2 fusion.118
  332.4 5.0 %fusion.63 = bf16[512,1,8,64]{0,3,2,1:T(8,128)(2,1)S(1)} fusion(f32[8,64,512]{2,1,0:T(8,128)S(1)} %fusion.118, bf16[512,8,64]{0,2,1:T(8,128)(2,1)S(1)} %copy-done.44, f32[8,512,512]{1,2,0:T(8,128)} %get-tuple-element.684, f32[512,512]{0,1:T(8,128)S(1)} %fusion.95), kind=kOutput, calls=%fused_computation.143 | convolution fusion | flops 273154048 | bytes 11534336 | tf_op jit(solution)/shard_map/hij,ihd->jhd/dot_general | solution.py:633
  345.9 4.3 fusion.159
  350.3 4.8 %while.61 = (s32[]{:T(128)}, f32[8,256,64]{2,1,0:T(8,128)S(1)}, f32[8,256]{1,0:T(8,128)S(1)}, s32[]{:T(128)}, bf16[4,8,256,64]{2,3,1,0:T(8,128)(2,1)}, /*index=5...) while((s32[]{:T(128)}, f32[8,256,64]{2,1,0:T(8,128)S(1)}, ...), condition=%wide.region_34.35_spmd, body=%wide.region_33.34_spmd.sunk | while | flops 266246 | bytes 2379939 | solution.py:397
  355.1 2.2 fusion.115
  357.3 5.0 %fusion.62 = bf16[512,1,8,64]{0,3,2,1:T(8,128)(2,1)S(1)} fusion(f32[8,64,512]{2,1,0:T(8,128)S(1)} %fusion.115, bf16[512,8,64]{0,2,1:T(8,128)(2,1)S(1)} %copy-done.42, f32[8,512,512]{1,2,0:T(8,128)} %fusion.186, f32[512,512]{0,1:T(8,128)S(1)} %fusion.95), kind=kOutput, calls=%fused_computation.142 | convolution fusion | flops 273154048 | bytes 11534336 | tf_op jit(solution)/shard_map/hij,ihd->jhd/dot_general | solution.py:633
  369.8 2.5 copy.230
  374.5 3.7 convert_reduce_fusion.3
  379.9 2.2 fusion.24
  384.4 54.8 %shard_map.238 = (f32[64,512]{1,0:T(8,128)}, f32[16,2048]{1,0:T(8,128)}, f32[16,512]{1,0:T(8,128)}, f32[16,1536]{1,0:T(8,128)}, f32[16,128]{1,0:T(8,128)}) custom-call(bf16[4,2,2,2,64,512]{5,4,3,2,1,0:T(8,128)(2,1)} %bitcast.448, bf16[4,2,2,2,16,2048]{5,4,3,2,1,0:T(8,128)(2,1)} %bitcast.436, bf16[4,2,2,2,16,512]{5,4,3,2,1,0:T(8,128)(2,1)} %bitcast.453, ...), custom_call_target="tpu_custom_call" | custom-call | tf_op jit(solution)/shard_map/pallas_call | solution.py:339
  (442 shorter events, 116.5 us)
Async XLA Ops:
  7.2 70.3 %copy-start = (bf16[64,256]{1,0:T(8,128)(2,1)S(1)}, bf16[64,256]{1,0:T(8,128)(2,1)}, u32[]{:S(2)}) copy-start(bf16[64,256]{1,0:T(8,128)(2,1)} %param.23) | copy-start | bytes 98308
  7.2 136.0 %all-gather.15.cloned.1.call-start = ((), (), s32[]{:S(2)}) async-start(), calls=%async_computation.1 | async-start | bytes 1310720 | tf_op jit(solution)/shard_map/all_gather | solution.py:355
  71.2 13.6 %copy-start.95 = (f32[512]{0:T(512)}, f32[512]{0:T(512)S(1)}, u32[]{:S(2)}) copy-start(f32[512]{0:T(512)S(1)} %get-tuple-element.598) | copy-start | bytes 6148
  71.3 13.6 %copy-start.121 = (f32[512]{0:T(512)}, f32[512]{0:T(512)S(1)}, u32[]{:S(2)}) copy-start(f32[512]{0:T(512)S(1)} %get-tuple-element.597) | copy-start | bytes 6148
  71.3 98.1 %copy-start.102 = (f32[512]{0:T(512)}, f32[512]{0:T(512)S(1)}, u32[]{:S(2)}) copy-start(f32[512]{0:T(512)S(1)} %get-tuple-element.596) | copy-start | bytes 6148
  77.1 7.0 %copy-start.22 = (bf16[512,1536]{0,1:T(8,128)(2,1)}, bf16[512,1536]{0,1:T(8,128)(2,1)S(1)}, u32[]{:S(2)}) copy-start(bf16[512,1536]{0,1:T(8,128)(2,1)S(1)} %copy.189) | copy-start | bytes 4718596
  77.4 6.8 %copy-start.84 = (f32[512,8]{0,1:T(8,128)}, f32[512,8]{0,1:T(8,128)S(1)}, u32[]{:S(2)}) copy-start(f32[512,8]{0,1:T(8,128)S(1)} %get-tuple-element.713) | copy-start | bytes 49156
  84.2 86.9 %all-gather.13.cloned.1.call-start = ((), (), s32[]{:S(2)}) async-start(), calls=%async_computation | async-start | bytes 1310720 | tf_op jit(solution)/shard_map/all_gather | solution.py:355
  84.8 5.5 %copy-start.114 = (f32[512]{0:T(512)}, f32[512]{0:T(512)S(1)}, u32[]{:S(2)}) copy-start(f32[512]{0:T(512)S(1)} %fusion.76) | copy-start | bytes 6148
  84.8 5.5 %copy-start.106 = (f32[512]{0:T(512)}, f32[512]{0:T(512)S(1)}, u32[]{:S(2)}) copy-start(f32[512]{0:T(512)S(1)} %fusion.147) | copy-start | bytes 6148
  90.3 6.5 %copy-start.24 = (bf16[512,1536]{0,1:T(8,128)(2,1)}, bf16[512,1536]{0,1:T(8,128)(2,1)S(1)}, u32[]{:S(2)}) copy-start(bf16[512,1536]{0,1:T(8,128)(2,1)S(1)} %copy.177) | copy-start | bytes 4718596
  90.6 17.9 %copy-start.86 = (f32[512,8]{0,1:T(8,128)}, f32[512,8]{0,1:T(8,128)S(1)}, u32[]{:S(2)}) copy-start(f32[512,8]{0,1:T(8,128)S(1)} %get-tuple-element.716) | copy-start | bytes 49156
  90.6 6.7 %copy-start.45 = (bf16[4,2,2,2,16,128]{5,4,3,2,1,0:T(8,128)(2,1)S(1)}, bf16[4,2,2,2,16,128]{5,4,3,2,1,0:T(8,128)(2,1)}, u32[]{:S(2)}) copy-start(bf16[4,2,2,2,16,128]{5,4,3,2,1,0:T(8,128)(2,1)} %get-tuple-element.405) | copy-start | bytes 393220
  96.9 228.7 %all-gather.17.cloned.1.call-start = ((), (), s32[]{:S(2)}) async-start(), calls=%async_computation.2 | async-start | bytes 1310720 | tf_op jit(solution)/shard_map/all_gather | solution.py:380
  108.5 4.8 %copy-start.118 = (bf16[8,256]{1,0:T(8,128)(2,1)S(1)}, bf16[8,256]{1,0:T(8,128)(2,1)}, u32[]{:S(2)}) copy-start(bf16[8,256]{1,0:T(8,128)(2,1)} %get-tuple-element.660) | copy-start | bytes 12292
  143.2 20.4 %copy-start.88 = (f32[8,512]{1,0:T(8,128)}, f32[8,512]{1,0:T(8,128)S(1)}, u32[]{:S(2)}) copy-start(f32[8,512]{1,0:T(8,128)S(1)} %get-tuple-element.589) | copy-start | bytes 49156
  163.6 5.8 %copy-start.20 = (bf16[1,512,512]{1,2,0:T(8,128)(2,1)S(1)}, bf16[1,512,512]{1,2,0:T(8,128)(2,1)}, u32[]{:S(2)}) copy-start(bf16[1,512,512]{1,2,0:T(8,128)(2,1)} %copy-done.19) | copy-start | bytes 1572868
  163.6 5.8 %copy-start.60 = (bf16[4,2,2,2,16,512]{5,4,3,2,1,0:T(8,128)(2,1)S(1)}, bf16[4,2,2,2,16,512]{5,4,3,2,1,0:T(8,128)(2,1)}, u32[]{:S(2)}) copy-start(bf16[4,2,2,2,16,512]{5,4,3,2,1,0:T(8,128)(2,1)} %get-tuple-element.409) | copy-start | bytes 1572868
  191.9 5.0 %copy-start.90 = (f32[8,512]{1,0:T(8,128)S(1)}, f32[8,512]{1,0:T(8,128)}, u32[]{:S(2)}) copy-start(f32[8,512]{1,0:T(8,128)} %get-tuple-element.588) | copy-start | bytes 49156
  196.9 5.9 %copy-start.17 = (bf16[1,512,512]{1,2,0:T(8,128)(2,1)S(1)}, bf16[1,512,512]{1,2,0:T(8,128)(2,1)}, u32[]{:S(2)}) copy-start(bf16[1,512,512]{1,2,0:T(8,128)(2,1)} %copy-done.16) | copy-start | bytes 1572868
  196.9 5.9 %copy-start.61 = (bf16[4,2,2,2,16,512]{5,4,3,2,1,0:T(8,128)(2,1)S(1)}, bf16[4,2,2,2,16,512]{5,4,3,2,1,0:T(8,128)(2,1)}, u32[]{:S(2)}) copy-start(bf16[4,2,2,2,16,512]{5,4,3,2,1,0:T(8,128)(2,1)} %get-tuple-element.409) | copy-start | bytes 1572868
  196.9 5.9 %copy-start.103 = (f32[512]{0:T(512)S(1)}, f32[512]{0:T(512)}, u32[]{:S(2)}) copy-start(f32[512]{0:T(512)} %copy-done.102) | copy-start | bytes 6148
  196.9 6.6 %copy-start.12 = (f32[512,512]{0,1:T(8,128)S(1)}, f32[512,512]{0,1:T(8,128)}, u32[]{:S(2)}) copy-start(f32[512,512]{0,1:T(8,128)} %copy-done.11) | copy-start | bytes 3145732
  196.9 6.6 %copy-start.39 = (bf16[4,2,2,2,16,2048]{5,4,3,2,1,0:T(8,128)(2,1)S(1)}, bf16[4,2,2,2,16,2048]{5,4,3,2,1,0:T(8,128)(2,1)}, u32[]{:S(2)}) copy-start(bf16[4,2,2,2,16,2048]{5,4,3,2,1,0:T(8,128)(2,1)} %get-tuple-element.410) | copy-start | bytes 6291460
  203.3 10.1 %copy-start.8 = (f32[512,512]{0,1:T(8,128)}, f32[512,512]{0,1:T(8,128)S(1)}, u32[]{:S(2)}) copy-start(f32[512,512]{0,1:T(8,128)S(1)} %get-tuple-element.692) | copy-start | bytes 3145732
  205.0 14.6 %copy-start.54 = (f32[512,2048]{1,0:T(8,128)}, f32[512,2048]{1,0:T(8,128)S(1)}, u32[]{:S(2)}) copy-start(f32[512,2048]{1,0:T(8,128)S(1)} %fusion.165) | copy-start | bytes 12582916
  206.4 7.0 %copy-start.56 = (f32[512,2048]{1,0:T(8,128)}, f32[512,2048]{1,0:T(8,128)S(1)}, u32[]{:S(2)}) copy-start(f32[512,2048]{1,0:T(8,128)S(1)} %fusion.164) | copy-start | bytes 12582916
  213.4 11.1 %copy-start.70 = (bf16[512,2048]{1,0:T(8,128)(2,1)}, bf16[512,2048]{1,0:T(8,128)(2,1)S(1)}, u32[]{:S(2)}) copy-start(bf16[512,2048]{1,0:T(8,128)(2,1)S(1)} %get-tuple-element.710) | copy-start | bytes 6291460
  233.8 5.6 %copy-start.117 = (f32[512]{0:T(512)S(1)}, f32[512]{0:T(512)}, u32[]{:S(2)}) copy-start(f32[512]{0:T(512)} %copy-done.116) | copy-start | bytes 6148
  267.5 4.8 %copy-start.79 = (f32[1,512,512]{1,2,0:T(8,128)S(1)}, f32[1,512,512]{1,2,0:T(8,128)}, u32[]{:S(2)}) copy-start(f32[1,512,512]{1,2,0:T(8,128)} %fusion.54) | copy-start | bytes 3145732
  273.8 11.5 %copy-start.87 = (f32[512,8]{0,1:T(8,128)S(1)}, f32[512,8]{0,1:T(8,128)}, u32[]{:S(2)}) copy-start(f32[512,8]{0,1:T(8,128)} %copy-done.86) | copy-start | bytes 49156
  276.7 73.5 %all-gather.19.cloned.1.call-start = ((), (), s32[]{:S(2)}) async-start(), calls=%async_computation.3 | async-start | bytes 1310720 | tf_op jit(solution)/shard_map/all_gather | solution.py:380
  285.2 15.1 %copy-start.14 = (f32[512,512]{0,1:T(8,128)S(1)}, f32[512,512]{0,1:T(8,128)}, u32[]{:S(2)}) copy-start(f32[512,512]{0,1:T(8,128)} %copy-done.11) | copy-start | bytes 3145732
  285.2 15.1 %copy-start.32 = (f32[512,2048]{1,0:T(8,128)S(1)}, f32[512,2048]{1,0:T(8,128)}, u32[]{:S(2)}) copy-start(f32[512,2048]{1,0:T(8,128)} %fusion.91) | copy-start | bytes 12582916
  285.2 15.1 %copy-start.69 = (bf16[512,2048]{1,0:T(8,128)(2,1)S(1)}, bf16[512,2048]{1,0:T(8,128)(2,1)}, u32[]{:S(2)}) copy-start(bf16[512,2048]{1,0:T(8,128)(2,1)} %get-tuple-element.712) | copy-start | bytes 6291460
  300.4 6.8 %copy-start.94 = (f32[512,8]{0,1:T(8,128)S(1)}, f32[512,8]{0,1:T(8,128)}, u32[]{:S(2)}) copy-start(f32[512,8]{0,1:T(8,128)} %broadcast_multiply_fusion.3) | copy-start | bytes 49156
  303.1 7.1 %copy-start.3 = (f32[8,256,64]{2,1,0:T(8,128)S(1)}, f32[8,256,64]{2,1,0:T(8,128)}, u32[]{:S(2)}) copy-start(f32[8,256,64]{2,1,0:T(8,128)} %get-tuple-element.412) | copy-start | bytes 1572868
  303.1 7.1 %copy-start.41 = (bf16[512,8,64]{0,2,1:T(8,128)(2,1)S(1)}, bf16[512,8,64]{0,2,1:T(8,128)(2,1)}, u32[]{:S(2)}) copy-start(bf16[512,8,64]{0,2,1:T(8,128)(2,1)} %copy-done.40) | copy-start | bytes 1572868
  310.8 5.2 %copy-start.57 = (f32[512,2048]{1,0:T(8,128)S(1)}, f32[512,2048]{1,0:T(8,128)}, u32[]{:S(2)}) copy-start(f32[512,2048]{1,0:T(8,128)} %copy-done.56) | copy-start | bytes 12582916
  310.8 5.2 %copy-start.78 = (bf16[2,512,512]{2,1,0:T(8,128)(2,1)S(1)}, bf16[2,512,512]{2,1,0:T(8,128)(2,1)}, u32[]{:S(2)}) copy-start(bf16[2,512,512]{2,1,0:T(8,128)(2,1)} %param.35) | copy-start | bytes 3145732
  310.8 5.2 %copy-start.120 = (f32[2048]{0:T(1024)S(1)}, f32[2048]{0:T(1024)}, u32[]{:S(2)}) copy-start(f32[2048]{0:T(1024)} %reshape.610) | copy-start | bytes 24580
  332.4 5.1 %copy-start.25 = (bf16[512,1536]{0,1:T(8,128)(2,1)S(1)}, bf16[512,1536]{0,1:T(8,128)(2,1)}, u32[]{:S(2)}) copy-start(bf16[512,1536]{0,1:T(8,128)(2,1)} %copy-done.24) | copy-start | bytes 4718596
  332.4 5.1 %copy-start.27 = (f32[512,8,256]{0,2,1:T(8,128)S(1)}, f32[512,8,256]{0,2,1:T(8,128)}, u32[]{:S(2)}) copy-start(f32[512,8,256]{0,2,1:T(8,128)} %get-tuple-element.683) | copy-start | bytes 12582916
  332.4 6.4 %copy-start.29 = (f32[8,256,512]{2,1,0:T(8,128)S(1)}, f32[8,256,512]{2,1,0:T(8,128)}, u32[]{:S(2)}) copy-start(f32[8,256,512]{2,1,0:T(8,128)} %fusion.188) | copy-start | bytes 12582916
  357.3 5.0 %copy-start.23 = (bf16[512,1536]{0,1:T(8,128)(2,1)S(1)}, bf16[512,1536]{0,1:T(8,128)(2,1)}, u32[]{:S(2)}) copy-start(bf16[512,1536]{0,1:T(8,128)(2,1)} %copy-done.22) | copy-start | bytes 4718596
  357.3 5.0 %copy-start.26 = (f32[512,8,256]{0,2,1:T(8,128)S(1)}, f32[512,8,256]{0,2,1:T(8,128)}, u32[]{:S(2)}) copy-start(f32[512,8,256]{0,2,1:T(8,128)} %get-tuple-element.680) | copy-start | bytes 12582916
  357.3 6.3 %copy-start.28 = (f32[8,256,512]{2,1,0:T(8,128)S(1)}, f32[8,256,512]{2,1,0:T(8,128)}, u32[]{:S(2)}) copy-start(f32[8,256,512]{2,1,0:T(8,128)} %fusion.190) | copy-start | bytes 12582916
  357.3 6.3 %copy-start.85 = (f32[512,8]{0,1:T(8,128)S(1)}, f32[512,8]{0,1:T(8,128)}, u32[]{:S(2)}) copy-start(f32[512,8]{0,1:T(8,128)} %copy-done.84) | copy-start | bytes 49156
  366.6 5.7 %copy-start.21 = (bf16[1,512,512]{1,2,0:T(8,128)(2,1)S(1)}, bf16[1,512,512]{1,2,0:T(8,128)(2,1)}, u32[]{:S(2)}) copy-start(bf16[1,512,512]{1,2,0:T(8,128)(2,1)} %copy-done.19) | copy-start | bytes 1572868
  366.6 5.7 %copy-start.31 = (f32[512,512]{0,1:T(8,128)S(1)}, f32[512,512]{0,1:T(8,128)}, u32[]{:S(2)}) copy-start(f32[512,512]{0,1:T(8,128)} %copy-done.30) | copy-start | bytes 3145732
  366.6 5.7 %copy-start.98 = (f32[512]{0:T(512)S(1)}, f32[512]{0:T(512)}, u32[]{:S(2)}) copy-start(f32[512]{0:T(512)} %copy-done.97) | copy-start | bytes 6148
  367.8 6.7 %copy-start.113 = (f32[512]{0:T(512)S(1)}, f32[512]{0:T(512)}, u32[]{:S(2)}) copy-start(f32[512]{0:T(512)} %copy-done.112) | copy-start | bytes 6148
  367.8 6.7 %copy-start.53 = (bf16[1,512,512]{1,2,0:T(8,128)(2,1)S(1)}, bf16[1,512,512]{1,2,0:T(8,128)(2,1)}, u32[]{:S(2)}) copy-start(bf16[1,512,512]{1,2,0:T(8,128)(2,1)} %copy.299) | copy-start | bytes 1572868
  367.8 6.7 %copy-start.105 = (f32[512]{0:T(512)S(1)}, f32[512]{0:T(512)}, u32[]{:S(2)}) copy-start(f32[512]{0:T(512)} %copy-done.104) | copy-start | bytes 6148
  367.8 6.7 %copy-start.109 = (f32[512]{0:T(512)S(1)}, f32[512]{0:T(512)}, u32[]{:S(2)}) copy-start(f32[512]{0:T(512)} %copy-done.108) | copy-start | bytes 6148
  372.3 5.8 %copy-start.33 = (f32[512,512]{0,1:T(8,128)S(1)}, f32[512,512]{0,1:T(8,128)}, u32[]{:S(2)}) copy-start(f32[512,512]{0,1:T(8,128)} %copy.230) | copy-start | bytes 3145732
  372.3 5.8 %copy-start.35 = (f32[512,512]{0,1:T(8,128)S(1)}, f32[512,512]{0,1:T(8,128)}, u32[]{:S(2)}) copy-start(f32[512,512]{0,1:T(8,128)} %get-tuple-element.675) | copy-start | bytes 3145732
  372.4 5.8 %copy-start.51 = (bf16[1,512,512]{1,2,0:T(8,128)(2,1)S(1)}, bf16[1,512,512]{1,2,0:T(8,128)(2,1)}, u32[]{:S(2)}) copy-start(bf16[1,512,512]{1,2,0:T(8,128)(2,1)} %copy.300) | copy-start | bytes 1572868
  372.4 5.8 %copy-start.111 = (f32[512]{0:T(512)S(1)}, f32[512]{0:T(512)}, u32[]{:S(2)}) copy-start(f32[512]{0:T(512)} %copy-done.110) | copy-start | bytes 6148
  374.5 5.4 %copy-start.73 = (bf16[512,3,8,64]{0,3,2,1:T(8,128)(2,1)S(1)}, bf16[512,3,8,64]{0,3,2,1:T(8,128)(2,1)}, u32[]{:S(2)}) copy-start(bf16[512,3,8,64]{0,3,2,1:T(8,128)(2,1)} %copy-done.72) | copy-start | bytes 4718596
  374.5 5.4 %copy-start.128 = (f32[512,1536]{1,0:T(8,128)S(1)}, f32[512,1536]{1,0:T(8,128)}, u32[]{:S(2)}) copy-start(f32[512,1536]{1,0:T(8,128)} %fusion.159) | copy-start | bytes 9437188
  382.1 59.6 %copy-start.59 = (f32[1,512,512]{1,2,0:T(8,128)S(1)}, f32[1,512,512]{1,2,0:T(8,128)}, u32[]{:S(2)}) copy-start(f32[1,512,512]{1,2,0:T(8,128)} %get-tuple-element.663) | copy-start | bytes 3145732
  441.7 5.1 %copy-start.92 = (f32[16,2048]{1,0:T(8,128)S(1)}, f32[16,2048]{1,0:T(8,128)}, u32[]{:S(2)}) copy-start(f32[16,2048]{1,0:T(8,128)} %get-tuple-element.997) | copy-start | bytes 393220
  441.7 5.8 %copy-start.91 = (f32[64,512]{1,0:T(8,128)S(1)}, f32[64,512]{1,0:T(8,128)}, u32[]{:S(2)}) copy-start(f32[64,512]{1,0:T(8,128)} %get-tuple-element.999) | copy-start | bytes 393220
  (69 other events, 191.6 us)
Sparse Core Ops, SparseCore 0:
  84.3 15.9 all-gather.14
  101.9 16.7 all-gather.12
  276.8 15.9 all-gather.16
  322.0 15.9 all-gather.18

commit v2 on v1

--- a/solution.py
+++ b/solution.py
@@ -1,3 +1,4 @@
+import functools
 import math
 
 import jax
@@ -61,10 +62,20 @@
 class Gather:
     def __init__(self, geo, lane):
         self.geo, self.lane = geo, lane
+        self.begin = lane.count
         self.zs = lane.take(geo.Z - 1)
         self.second = lane.take(max(geo.X, geo.Y) - 1)
         self.third = lane.take(max(geo.X, geo.Y) - 1)
         self.core = lane.take()
+
+    indices = ("zs", "second", "third", "core")
+
+    def shifted(self, by):
+        other = object.__new__(type(self))
+        other.geo, other.lane = self.geo, self.lane
+        for name in self.indices:
+            setattr(other, name, getattr(self, name) + by)
+        return other
 
     def bind(self, own, full):
         self.own, self.full = own, full
@@ -151,6 +162,7 @@
 class Scatter:
     def __init__(self, geo, lane):
         self.geo, self.lane = geo, lane
+        self.begin = lane.count
         self.core = lane.take()
         self.first = lane.take(max(geo.X, geo.Y) - 1)
         self.second = lane.take(max(geo.X, geo.Y) - 1)
@@ -166,6 +178,15 @@
             pltpu.VMEM((wide - 1, geo.Z, rows, width), kind),
             pltpu.VMEM((geo.Z - 1, rows, width), kind),
         ]
+
+    indices = ("core", "first", "second", "zs")
+
+    def shifted(self, by):
+        other = object.__new__(type(self))
+        other.geo, other.lane = self.geo, self.lane
+        for name in self.indices:
+            setattr(other, name, getattr(self, name) + by)
+        return other
 
     def bind(self, part, out, buffers):
         self.part, self.out = part, out
@@ -283,68 +304,6 @@
             copy.wait_send()
 
 
-def run_steps(tasks):
-    for n in range(5 + len(tasks) - 1):
-        for i, task in enumerate(tasks):
-            if 0 <= n - i < 5:
-                task.step(n - i)
-    for task in tasks:
-        task.drain()
-
-
-def gather_all(geo, shards):
-    lane = Lane()
-    tasks = [Gather(geo, lane) for _ in shards]
-    n = len(shards)
-
-    def body(*refs):
-        own, full = refs[:n], refs[n:2 * n]
-        lane.send, lane.recv = refs[2 * n], refs[2 * n + 1]
-        for task, a, b in zip(tasks, own, full):
-            task.bind(a, b)
-        geo.barrier()
-        run_steps(tasks)
-
-    vmem = pl.BlockSpec(memory_space=pltpu.VMEM)
-    return pl.pallas_call(
-        body,
-        out_shape=[jax.ShapeDtypeStruct((geo.Z, geo.X, geo.Y, 2) + s.shape, s.dtype) for s in shards],
-        in_specs=[vmem] * n, out_specs=[vmem] * n,
-        scratch_shapes=[pltpu.SemaphoreType.DMA((lane.count,)), pltpu.SemaphoreType.DMA((lane.count,))],
-        compiler_params=pltpu.CompilerParams(collective_id=0, has_side_effects=True, vmem_limit_bytes=56 << 20),
-    )(*shards)
-
-
-def scatter_all(geo, parts):
-    lane = Lane()
-    tasks = [Scatter(geo, lane) for _ in parts]
-    n = len(parts)
-
-    def body(*refs):
-        part, out = refs[:n], refs[n:2 * n]
-        held = refs[2 * n:3 * n]
-        buffers = refs[3 * n:7 * n]
-        lane.send, lane.recv = refs[7 * n], refs[7 * n + 1]
-        for i, task in enumerate(tasks):
-            held[i][...] = part[i][...]
-            task.bind(held[i], out[i], buffers[4 * i:4 * i + 4])
-        geo.barrier()
-        run_steps(tasks)
-
-    vmem = pl.BlockSpec(memory_space=pltpu.VMEM)
-    scratch = [pltpu.VMEM(p.shape, p.dtype) for p in parts]
-    for p in parts:
-        scratch += Scatter.scratch(geo, p.shape[-2], p.shape[-1])
-    scratch += [pltpu.SemaphoreType.DMA((lane.count,)), pltpu.SemaphoreType.DMA((lane.count,))]
-    return pl.pallas_call(
-        body,
-        out_shape=[jax.ShapeDtypeStruct(p.shape[-2:], jnp.float32) for p in parts],
-        in_specs=[vmem] * n, out_specs=[vmem] * n,
-        scratch_shapes=scratch,
-        compiler_params=pltpu.CompilerParams(collective_id=1, has_side_effects=True, vmem_limit_bytes=56 << 20),
-    )(*parts)
-
-
 epsilon = 1e-05
 finest_precision = lax.Precision.HIGHEST
 
@@ -547,7 +506,7 @@
     )
     active_float, gelu_pull = jax.vjp(gelu_tanh, hidden)
     active = active_float.astype(jnp.bfloat16)
-    stored = {"front": pieces, "carry": block_carry, "middle": middle}
+    stored = {"front": pieces, "carry": block_carry}
     down_term = upstream.astype(jnp.bfloat16)
     stored["down"] = jnp.einsum("rf,rd->fd", active, down_term, preferred_element_type=jnp.float32)
     stored["down_bias"] = jnp.sum(upstream, axis=0)
@@ -656,38 +615,578 @@
     return (stored["middle_grad"] + inputs_part, input_part, gain_one_grad, shift_one_grad)
 
 
+BF = jnp.bfloat16
+F32 = jnp.float32
+M = 256
+SCALE = DH ** (-0.25)
+LOG2E = math.log2(math.e)
+PAIRS = H // 2
+STATE_ROWS = 160
+
+
+def dot(a, b):
+    return jnp.dot(a, b, preferred_element_type=F32)
+
+
+def dot_nt(a, b):
+    return lax.dot_general(a, b, (((1,), (1,)), ((), ())), preferred_element_type=F32)
+
+
+class States:
+    def __init__(self, geo, lane, earlier):
+        self.geo, self.lane, self.earlier = geo, lane, earlier
+        self.per = geo.Y + 1
+        self.first = lane.take(self.per * PAIRS)
+
+    @staticmethod
+    def scratch(geo):
+        one = (PAIRS, STATE_ROWS, M)
+        two = (PAIRS, 2, STATE_ROWS, M)
+        return [pltpu.VMEM(two, BF), pltpu.VMEM(two, BF), pltpu.VMEM(one, BF),
+                pltpu.VMEM((PAIRS, max(geo.Y - 1, 1), STATE_ROWS, M), BF), pltpu.VMEM(one, BF),
+                pltpu.VMEM(one, BF), pltpu.VMEM(two, BF)]
+
+    def bind(self, buffers):
+        self.own, self.sibling, self.chip, self.chips, self.base, self.base_sibling, self.total = buffers
+
+    def copies(self, p, phase):
+        g = self.geo
+        z, x, y, c = g.me()
+        index = self.first + p * self.per
+        other = g.device(z, x, y, 1 - c)
+        if phase == 0:
+            return [remote(self.lane, index, self.own.at[p], self.sibling.at[p], other)]
+        if phase == 1:
+            return [remote(self.lane, index + k, self.chip.at[p], self.chips.at[p, k - 1],
+                           g.device(z, x, (y + k) % g.Y, c)) for k in range(1, g.Y)]
+        return [remote(self.lane, index + g.Y, self.base.at[p], self.base_sibling.at[p], other)]
+
+    def step(self, n, p):
+        g = self.geo
+        z, x, y, c = g.me()
+        if n > 0:
+            for copy in self.copies(p, n - 1):
+                copy.wait_recv()
+        if n == 1:
+            self.chip[p] = (self.own[p, c].astype(F32) + self.sibling[p, c].astype(F32)).astype(BF)
+        elif n == 2:
+            total = jnp.zeros((STATE_ROWS, M), F32)
+            for k in range(1, g.Y):
+                source = (y + g.Y - k) % g.Y
+                counts = source < y if self.earlier else source > y
+                total += jnp.where(counts, 1.0, 0.0) * self.chips[p, k - 1].astype(F32)
+            self.base[p] = total.astype(BF)
+        elif n == 3:
+            near = jnp.where(c == (1 if self.earlier else 0), 1.0, 0.0)
+            self.total[p, c] = (self.base[p].astype(F32) + near * self.sibling[p, c].astype(F32)).astype(BF)
+            self.total[p, 1 - c] = (self.base_sibling[p].astype(F32)
+                                    + near * self.sibling[p, 1 - c].astype(F32)).astype(BF)
+        if n < 3:
+            for copy in self.copies(p, n):
+                copy.start()
+
+    def drain(self):
+        for p in range(PAIRS):
+            for phase in range(3):
+                for copy in self.copies(p, phase):
+                    copy.wait_send()
+
+
+class Many:
+    def __init__(self, kind, geo, lane, count):
+        self.tasks = [kind(geo, lane) for _ in range(count)]
+        self.per = (lane.count - self.tasks[0].begin) // count
+
+    def bind(self, chunk):
+        self.chunk = chunk
+
+    def step(self, n, p):
+        task = self.tasks[0].shifted(p * self.per)
+        task.bind(*self.chunk(p))
+        task.step(n)
+
+    def drain(self):
+        for p in range(len(self.tasks)):
+            task = self.tasks[0].shifted(p * self.per)
+            task.bind(*self.chunk(p))
+            task.drain()
+
+
+def layer_kernel(geo, lane, plan, *refs):
+    (tokens, cot, feat, small_own, wi_in, wo_in, wu_in, wd_own,
+     result, tokens_grad, inp_out, ou_out, down_out, vec_out,
+     small, wi_own, wi, wou_own, wou, wd, normed, normed_t, mixed, pq, pk, den, attended, middle, n2_t,
+     act, hg, vecs, ub, ubg, grads, fa, ft,
+     part_i, part_u, part_d, part_v) = refs[:41]
+    rest = list(refs[41:])
+    fwd, bwd, gs, gi, gu, gd, ri, ru, rd, rv = plan
+    take = lambda n: [rest.pop(0) for _ in range(n)]
+    fwd.bind(take(7))
+    bwd.bind(take(7))
+    bi, bu, bd, bv = take(4), take(4), take(4), take(4)
+    lane.send, lane.recv = take(2)
+    gs.bind(small_own, small)
+    gi.bind(lambda p: (wi_own.at[p], wi.at[p]))
+    gu.bind(wou_own, wou)
+    gd.bind(wd_own, wd)
+    inp_parts = inp_out
+    ri.bind(lambda p: (part_i.at[p], inp_parts.at[p], [b.at[p] for b in bi]))
+    ru.bind(part_u, ou_out, bu)
+    rd.bind(part_d, down_out, bd)
+    rv.bind(part_v, vec_out, bv)
+    n2 = normed
+    D = tokens.shape[-1]
+    L = tokens.shape[1]
+    FF = wd.shape[0] * wd.shape[1] * wd.shape[2] * 2 * wd.shape[4]
+    HALF = L // 2
+    lead = (geo.Z, geo.X, geo.Y, 2)
+
+    def loop(n, body):
+        def step(i, _):
+            body(i)
+            return 0
+        lax.fori_loop(0, n, step, 0)
+
+    for p in range(PAIRS):
+        wi_own[p] = jnp.concatenate([wi_in[:, k * D + p * 128: k * D + (p + 1) * 128] for k in range(3)], axis=1)
+    wou_own[:, :D] = wo_in[...]
+    wou_own[:, D:] = wu_in[...]
+    geo.barrier()
+    gs.step(0)
+    for p in range(PAIRS):
+        gi.step(0, p)
+    gu.step(0)
+    gd.step(0)
+
+    f = feat[...]
+    zero = jnp.zeros((DH, M), BF)
+    one = jnp.ones((DH, M), BF)
+    fa[0] = jnp.concatenate([f, zero, -one, zero], axis=0)
+    fa[1] = jnp.concatenate([zero, f, zero, -one], axis=0)
+    ft[...] = jnp.concatenate([jnp.concatenate([f, zero], axis=1), jnp.concatenate([zero, f], axis=1),
+                               jnp.concatenate([one, zero], axis=1), jnp.concatenate([zero, one], axis=1)], axis=0)
+    low_lane = lax.broadcasted_iota(jnp.int32, (1, 128), 1) < DH
+    m0f = jnp.where(low_lane, 1.0, 0.0)
+    m0 = m0f.astype(BF)
+    m1 = (1.0 - m0f).astype(BF)
+    tri_r = lax.broadcasted_iota(jnp.int32, (HALF, HALF), 0)
+    tri_c = lax.broadcasted_iota(jnp.int32, (HALF, HALF), 1)
+
+    gs.step(1)
+    gi.step(1, 0)
+    gs.step(2)
+    gi.step(1, 1)
+    gi.step(2, 0)
+    gs.step(3)
+    gi.step(1, 2)
+    gi.step(2, 1)
+    gs.step(4)
+
+    flat = lambda v: v.reshape(-1, v.shape[-1])
+    sm = small[...]
+    vecs[...] = flat(sm[..., :128]).astype(F32).T[:8]
+    ub[...] = jnp.sum(sm[..., 128:].astype(F32).reshape(-1, 2 * sm.shape[-2], 128), axis=1)
+    out_bias, down_bias = lambda: vecs[0:1], lambda: vecs[1:2]
+
+    def norm_parts(rows):
+        center = jnp.mean(rows, axis=-1, keepdims=True)
+        centred = rows - center
+        spread = jnp.mean(centred * centred, axis=-1, keepdims=True)
+        inv = lax.rsqrt(spread + epsilon)
+        return centred * inv, inv
+
+    def first_norm(s):
+        hat, _ = norm_parts(tokens[s].astype(F32))
+        value = (hat * vecs[2:3] + vecs[3:4]).astype(BF)
+        normed[s] = value
+        normed_t[s] = value.T
+    gi.step(3, 0)
+    loop(2, first_norm)
+    gi.step(1, 3)
+    gi.step(2, 2)
+    gi.step(3, 1)
+
+    def vx(s, p):
+        v = mixed[s, p, :, 2 * 128:]
+        ones = jnp.ones(v.shape, BF)
+        return (jnp.concatenate([v * m0, ones * m0], axis=1), jnp.concatenate([v * m1, ones * m1], axis=1))
+
+    def project(p):
+        gi.step(4, p)
+        w = flat(wi[p])
+
+        def seq(s):
+            mixed[s, p] = dot(normed[s], w).astype(BF)
+            for part, target in ((0, pq), (1, pk)):
+                rows = mixed[s, p, :, part * 128:(part + 1) * 128]
+                wide = rows.astype(F32)
+                lhs = jnp.concatenate([rows, (wide * wide * (0.5 * SCALE)).astype(BF)], axis=1)
+                for h in range(2):
+                    power = dot(lhs, fa[h]) * (SCALE * LOG2E) - 0.5 * math.log2(M)
+                    target[s, 2 * p + h] = jnp.exp2(power).astype(BF)
+            v = mixed[s, p, :, 2 * 128:]
+            lhs = jnp.concatenate([v.T, jnp.ones((16, L), BF)], axis=0)
+            r0 = dot(lhs, pk[s, 2 * p])
+            r1 = dot(lhs, pk[s, 2 * p + 1])
+            fwd.own[p, s] = jnp.concatenate([r0[:64], r1[64:128], r0[128:], r1[128:]], axis=0).astype(BF)
+        loop(2, seq)
+        fwd.step(0, p)
+
+        @pl.when(p == 0)
+        def _():
+            gi.step(2, 3)
+            gi.step(3, 2)
+            gu.step(1)
+
+        @pl.when(p == 1)
+        def _():
+            gi.step(3, 3)
+            gd.step(1)
+
+        @pl.when(p == 2)
+        def _():
+            gu.step(2)
+
+        for n in range(1, 4):
+            @pl.when(p >= n)
+            def _():
+                fwd.step(n, p - n)
+    loop(PAIRS, project)
+    gd.step(2)
+    fwd.step(1, 3)
+    fwd.step(2, 2)
+    fwd.step(3, 1)
+
+    def state_cols(total, p, s, h, copies):
+        state = total[p, s, h * 64:(h + 1) * 64]
+        extra = total[p, s, 128 + 16 * h:144 + 16 * h]
+        zeros = jnp.zeros((DH, M), BF)
+        if copies:
+            extra = jnp.concatenate([extra] * 4, axis=0)
+        else:
+            extra = jnp.concatenate([extra, jnp.zeros((48, M), BF)], axis=0)
+        parts = [state, zeros, extra, zeros] if h == 0 else [zeros, state, zeros, extra]
+        return jnp.concatenate(parts, axis=0)
+
+    lower = tri_r >= tri_c
+    upper = tri_r <= tri_c
+
+    def attend_pair(p):
+        def seq(s):
+            v0, v1 = vx(s, p)
+            states = jnp.concatenate([state_cols(fwd.total, p, s, h, True) for h in range(2)], axis=1)
+            lanes = pl.ds(pl.multiple_of(p * 128, 128), 128)
+            for b in range(2):
+                rows = slice(b * HALF, (b + 1) * HALF)
+                scores = []
+                for h in range(2):
+                    q = pq[s, 2 * p + h, rows]
+                    if b == 1:
+                        scores.append(dot_nt(q, pk[s, 2 * p + h, :HALF]).astype(BF))
+                    scores.append(jnp.where(lower, dot_nt(q, pk[s, 2 * p + h, rows]), 0.0).astype(BF))
+                rhs = jnp.concatenate([v0[:(b + 1) * HALF], v1[:(b + 1) * HALF]], axis=0)
+                ext = dot(jnp.concatenate(scores, axis=1), rhs)
+                ext += dot_nt(jnp.concatenate([pq[s, 2 * p, rows], pq[s, 2 * p + 1, rows]], axis=1), states)
+                n_, d_ = ext[:, :128], ext[:, 128:]
+                inv = 1.0 / d_
+                den[s, rows, lanes] = inv
+                attended[s, rows, lanes] = (n_ * inv).astype(BF)
+        loop(2, seq)
+
+        @pl.when(p == 0)
+        def _():
+            fwd.step(2, 3)
+            fwd.step(3, 2)
+            gu.step(3)
+
+        @pl.when(p == 1)
+        def _():
+            fwd.step(3, 3)
+            gd.step(3)
+    loop(PAIRS, attend_pair)
+    gu.step(4)
+    gd.step(4)
+
+    def wo():
+        return flat(wou[..., :D])
+
+    def to_middle(s):
+        value = tokens[s].astype(F32) + dot(attended[s], wo()) + out_bias()
+        middle[s] = value
+        hat, _ = norm_parts(value)
+        low = (hat * vecs[4:5] + vecs[5:6]).astype(BF)
+        n2[s] = low
+        n2_t[s] = low.T
+        result[s] = value + down_bias()
+        tokens_grad[s] = jnp.zeros((L, D), F32)
+    loop(2, to_middle)
+    ubg[...] = jnp.zeros(ubg.shape, F32)
+    grads[...] = jnp.zeros(grads.shape, F32)
+
+    k0 = math.sqrt(2.0 / math.pi)
+
+    def feed_tile(t):
+        lanes = pl.ds(pl.multiple_of(D + t * 512, 512), 512)
+        bias = jnp.concatenate([ub[pl.ds(4 * t + i, 1)] for i in range(4)], axis=1)
+        wut = lambda: flat(wou[:, :, :, :, :, lanes])
+        wdt = lambda: flat(wd[t])
+
+        def seq(s):
+            for b in range(2):
+                rows = slice(b * HALF, (b + 1) * HALF)
+                u = dot(n2[s, rows], wut()) + bias
+                uu = u * u
+                th = jnp.tanh(u * (k0 + (k0 * 0.044715) * uu))
+                half = 0.5 + 0.5 * th
+                a = (u * half).astype(BF)
+                act[s, rows] = a
+                slope = half + (0.5 * u) * (1.0 - th * th) * (k0 + (3.0 * 0.044715 * k0) * uu)
+                back = dot_nt(cot[s, rows], wdt()) * slope
+                total = jnp.sum(back, axis=0, keepdims=True)
+                for i in range(4):
+                    ubg[pl.ds(4 * t + i, 1)] += total[:, i * 128:(i + 1) * 128]
+                low = back.astype(BF)
+                hg[s, rows] = low
+                result[s, rows] += dot(a, wdt())
+                tokens_grad[s, rows] += dot_nt(low, wut())
+        loop(2, seq)
+        dwd = dot(act[0].T, cot[0]) + dot(act[1].T, cot[1])
+        part_d[t] = dwd.astype(BF).reshape(part_d.shape[1:])
+        dwu = dot(n2_t[0], hg[0]) + dot(n2_t[1], hg[1])
+        part_u[:, :, :, :, :, lanes] = dwu.astype(BF).reshape(lead + (-1, 512))
+    loop(FF // 512, feed_tile)
+    rd.step(0)
+
+    ones_block = jnp.concatenate([jnp.concatenate([jnp.ones((64, 64), F32), jnp.zeros((64, 64), F32)], axis=1),
+                                  jnp.concatenate([jnp.zeros((64, 64), F32), jnp.ones((64, 64), F32)], axis=1)],
+                                 axis=0).astype(BF)
+    ones_two = jnp.concatenate([ones_block, ones_block], axis=0)
+    lane_id = lax.broadcasted_iota(jnp.int32, (1, 128), 1)
+    hi_lane = jnp.where((lane_id % DH) == 0, 1.0, 0.0)
+    lo_lane = jnp.where((lane_id % DH) == 1, 1.0, 0.0)
+
+    def norm_back(rows, dy, gain):
+        hat, inv = norm_parts(rows)
+        dg = dy * gain
+        m_a = jnp.mean(dg, axis=-1, keepdims=True)
+        m_b = jnp.mean(dg * hat, axis=-1, keepdims=True)
+        return (inv * (dg - m_a - hat * m_b), jnp.sum(dy * hat, axis=0, keepdims=True),
+                jnp.sum(dy, axis=0, keepdims=True))
+
+    def out_back(s):
+        dx, dgain, dshift = norm_back(middle[s], tokens_grad[s], vecs[4:5])
+        up = cot[s].astype(F32)
+        mg = up + dx
+        middle[s] = mg
+        low = mg.astype(BF)
+        act[s] = low
+        grads[0:1] += jnp.sum(mg, axis=0, keepdims=True)
+        grads[1:2] += jnp.sum(up, axis=0, keepdims=True)
+        grads[4:5] += dgain
+        grads[5:6] += dshift
+        ag = dot_nt(low, wo())
+        inv = den[s]
+        ng = ag * inv
+        prod = ng * attended[s].astype(F32)
+        n2[s] = ng.astype(BF)
+        for p in range(PAIRS):
+            cols = slice(p * 128, (p + 1) * 128)
+            pr = prod[:, cols]
+            hi = pr.astype(BF)
+            lo = (pr - hi.astype(F32)).astype(BF)
+            dgr = -dot(jnp.concatenate([hi, lo], axis=1), ones_two)
+            dhi = dgr.astype(BF).astype(F32)
+            dlo = dgr - dhi
+            hg[s, :, cols] = (dhi * hi_lane + dlo * lo_lane).astype(BF)
+    loop(2, out_back)
+    dwo = dot(attended[0].T, act[0]) + dot(attended[1].T, act[1])
+    part_u[:, :, :, :, :, :D] = dwo.astype(BF).reshape(lead + (-1, D))
+    ru.step(0)
+
+    def ngx(s, p):
+        lanes = pl.ds(pl.multiple_of(p * 128, 128), 128)
+        return jnp.concatenate([n2[s, :, lanes], hg[s, :, lanes]], axis=1)
+
+    def state_back(p):
+        def seq(s):
+            lhs = ngx(s, p).T
+            r0 = dot(lhs, pq[s, 2 * p])
+            r1 = dot(lhs, pq[s, 2 * p + 1])
+            bwd.own[p, s] = jnp.concatenate([r0[:64], r1[64:128], r0[128:144], r1[192:208]], axis=0).astype(BF)
+        loop(2, seq)
+        bwd.step(0, p)
+
+        @pl.when(p == 1)
+        def _():
+            rd.step(1)
+
+        @pl.when(p == 3)
+        def _():
+            ru.step(1)
+        for n in range(1, 4):
+            @pl.when(p >= n)
+            def _():
+                bwd.step(n, p - n)
+    loop(PAIRS, state_back)
+    bwd.step(1, 3)
+    bwd.step(2, 2)
+    bwd.step(3, 1)
+
+    def pair_back(i):
+        p, s = i // 2, i % 2
+        v0, v1 = vx(s, p)
+        x = ngx(s, p)
+        ng = x[:, :128]
+        logs_q, logs_k, at = [], [], []
+        for h, v in ((0, v0), (1, v1)):
+            q, k = pq[s, 2 * p + h], pk[s, 2 * p + h]
+            sx = state_cols(fwd.total, p, s, h, True)
+            sg = state_cols(bwd.total, p, s, h, False)
+            lo, hi = slice(0, HALF), slice(HALF, L)
+
+            def masked(keep, value):
+                return jnp.where(keep, value, 0.0).astype(BF)
+            g00 = masked(lower, dot_nt(x[lo], v[lo]))
+            g10 = dot_nt(x[hi], v[lo]).astype(BF)
+            g11 = masked(lower, dot_nt(x[hi], v[hi]))
+            qg0 = dot(jnp.concatenate([g00, x[lo]], axis=1), jnp.concatenate([k[lo], sx], axis=0))
+            qg1 = dot(jnp.concatenate([g10, g11, x[hi]], axis=1), jnp.concatenate([k, sx], axis=0))
+            logs_q.append((jnp.concatenate([qg0, qg1], axis=0) * q.astype(F32)).astype(BF))
+            t00 = masked(upper, dot_nt(v[lo], x[lo]))
+            t01 = dot_nt(v[lo], x[hi]).astype(BF)
+            t11 = masked(upper, dot_nt(v[hi], x[hi]))
+            kg0 = dot(jnp.concatenate([t00, t01, v[lo]], axis=1), jnp.concatenate([q, sg], axis=0))
+            kg1 = dot(jnp.concatenate([t11, v[hi]], axis=1), jnp.concatenate([q[hi], sg], axis=0))
+            logs_k.append((jnp.concatenate([kg0, kg1], axis=0) * k.astype(F32)).astype(BF))
+            a00 = masked(upper, dot_nt(k[lo], q[lo]))
+            a01 = dot_nt(k[lo], q[hi]).astype(BF)
+            a11 = masked(upper, dot_nt(k[hi], q[hi]))
+            at.append((a00, a01, a11))
+        n0, n1 = ng * m0, ng * m1
+        vg0 = dot(jnp.concatenate([at[0][0], at[0][1], at[1][0], at[1][1]], axis=1),
+                  jnp.concatenate([n0, n1], axis=0))
+        vg1 = dot(jnp.concatenate([at[0][2], at[1][2]], axis=1), jnp.concatenate([n0[HALF:], n1[HALF:]], axis=0))
+        zeros = jnp.zeros((DH, M), BF)
+        sgt = jnp.concatenate([jnp.concatenate([bwd.total[p, s, :64], zeros], axis=0),
+                               jnp.concatenate([zeros, bwd.total[p, s, 64:128]], axis=0)], axis=1)
+        vg = jnp.concatenate([vg0, vg1], axis=0)
+        vg += dot_nt(jnp.concatenate([pk[s, 2 * p], pk[s, 2 * p + 1]], axis=1), sgt)
+        out = []
+        for part, logs in ((0, logs_q), (1, logs_k)):
+            through = dot_nt(jnp.concatenate(logs, axis=1), ft[...])
+            rows = mixed[s, p, :, part * 128:(part + 1) * 128].astype(F32)
+            out.append((SCALE * through[:, :128] - SCALE * SCALE * through[:, 128:] * rows).astype(BF))
+        mg = jnp.concatenate(out + [vg.astype(BF)], axis=1)
+        act[s, :, :384] = mg
+        back = dot_nt(mg, flat(wi[p]))
+
+        @pl.when(p == 0)
+        def _():
+            tokens_grad[s] = back
+
+        @pl.when(p > 0)
+        def _():
+            tokens_grad[s] += back
+
+        @pl.when(s == 1)
+        def _():
+            dwi = dot(normed_t[0], act[0, :, :384]) + dot(normed_t[1], act[1, :, :384])
+            part_i[p] = dwi.astype(BF).reshape(lead + (-1, 384))
+            ri.step(0, p)
+        schedule = {0: [lambda: bwd.step(2, 3), lambda: bwd.step(3, 2)], 1: [lambda: bwd.step(3, 3)],
+                    2: [lambda: rd.step(2), lambda: ri.step(1, 0)],
+                    3: [lambda: ru.step(2)],
+                    4: [lambda: rd.step(3), lambda: ri.step(2, 0), lambda: ri.step(1, 1)],
+                    5: [lambda: ru.step(3)],
+                    6: [lambda: rd.step(4), lambda: ri.step(3, 0), lambda: ri.step(2, 1), lambda: ri.step(1, 2)],
+                    7: [lambda: ru.step(4), lambda: ri.step(4, 0), lambda: ri.step(3, 1), lambda: ri.step(2, 2)]}
+        for at_step, actions in schedule.items():
+            @pl.when(i == at_step)
+            def _():
+                for action in actions:
+                    action()
+    loop(2 * PAIRS, pair_back)
+    ri.step(1, 3)
+
+    def first_back(s):
+        dx, dgain, dshift = norm_back(tokens[s].astype(F32), tokens_grad[s], vecs[2:3])
+        tokens_grad[s] = middle[s] + dx
+        grads[2:3] += dgain
+        grads[3:4] += dshift
+    loop(2, first_back)
+    part_v[..., :128] = jnp.concatenate([grads[...], jnp.zeros((120, D), F32)], axis=0).T.astype(BF).reshape(lead + (-1, 128))
+    first_row = lax.broadcasted_iota(jnp.int32, (16, 128), 0) == 0
+    for z in range(geo.Z):
+        for x in range(geo.X):
+            for y in range(geo.Y):
+                chip = (z * geo.X + x) * geo.Y + y
+                tile = jnp.where(first_row, ubg[chip:chip + 1], 0.0).astype(BF)
+                for c in range(2):
+                    part_v[z, x, y, c, :, 128:] = tile
+    rv.step(0)
+    ri.step(4, 1)
+    ri.step(3, 2)
+    ri.step(2, 3)
+    rv.step(1)
+    ri.step(4, 2)
+    ri.step(3, 3)
+    rv.step(2)
+    ri.step(4, 3)
+    rv.step(3)
+    rv.step(4)
+    for task in (gs, gi, gu, gd, fwd, bwd, ri, ru, rd, rv):
+        task.drain()
+
+
 def fused(geo, args):
     (tokens, feature_matrix, input_weight, output_weight, output_bias, up_weight, up_bias, down_weight,
      down_bias, first_gain, first_shift, second_gain, second_shift, cotangent) = args
-    small = jnp.stack([output_bias, down_bias, first_gain, first_shift, second_gain, second_shift], axis=1)
-    small = jnp.concatenate([small, up_bias.reshape(-1, 4), jnp.zeros((small.shape[0], 118), small.dtype)], axis=1)
-    full = gather_all(geo, [small, input_weight, output_weight, up_weight, down_weight])
-    small, wi, wo, wu, wd = [f.reshape(-1, f.shape[-1]) for f in full]
-    params = (wi, wo, small[:, 0], wu, small[:, 6:10].reshape(-1), wd, small[:, 1], small[:, 2], small[:, 3],
-              small[:, 4], small[:, 5])
-    micros = tokens.shape[0]
-    carries, results, stored_list, later_list = [], [], [], []
-    for m in range(micros):
-        pieces = front(tokens[m], feature_matrix, params)
-        carry = prefix((pieces[8], pieces[9]), "seq", add_pair, (jnp.zeros_like(pieces[8]), jnp.zeros_like(pieces[9])))
-        stored = upper_back(tokens[m], cotangent[m].astype(jnp.float32), feature_matrix, params, carry)
-        results.append(feed(stored["middle"], params))
-        stored_list.append(stored)
-        later_list.append(prefix_2((stored["state_grad"], stored["sum_grad"]), "seq", add_pair,
-                                   (jnp.zeros_like(stored["state_grad"]), jnp.zeros_like(stored["sum_grad"]))))
-    names = ["out", "out_bias", "up", "up_bias", "down", "down_bias", "gain_two", "shift_two"]
-    upper = [sum(s[name] for s in stored_list) for name in names]
-    token_grads, lower = [], None
-    for m in range(micros):
-        tg, *parts = lower_back(stored_list[m], later_list[m], feature_matrix, params)
-        token_grads.append(tg)
-        lower = parts if lower is None else [a + b for a, b in zip(lower, parts)]
-    shape = (geo.Z, geo.X, geo.Y, 2)
-    cut = lambda a: a.astype(jnp.bfloat16).reshape(shape + (-1, a.shape[-1]))
-    vec = jnp.stack([upper[1], upper[5], lower[1], lower[2], upper[6], upper[7]], axis=1)
-    vec = jnp.concatenate([vec, upper[3].reshape(-1, 4), jnp.zeros((vec.shape[0], 118), jnp.float32)], axis=1)
-    down, up, out, inp, vec = scatter_all(geo, [cut(upper[4]), cut(upper[2]), cut(upper[0]), cut(lower[0]), cut(vec)])
-    return (jnp.stack(results), jnp.stack(token_grads), inp, out, vec[:, 0], up, vec[:, 6:10].reshape(-1), down,
+    rows, D = input_weight.shape[0], tokens.shape[-1]
+    L = tokens.shape[1]
+    FF = up_weight.shape[1]
+    core = geo.me()[3]
+    cols = jnp.stack([output_bias, down_bias, first_gain, first_shift, second_gain, second_shift], axis=1)
+    width = up_bias.shape[0]
+    placed = jnp.where(jnp.arange(128) // width == core, jnp.tile(up_bias, 128 // width), 0)
+    small = jnp.concatenate([jnp.pad(cols, ((0, 0), (0, 122))),
+                             jnp.pad(placed[None], ((0, rows - 1), (0, 0)))], axis=1)
+    lane = Lane()
+    fwd, bwd = States(geo, lane, True), States(geo, lane, False)
+    gs, gi, gu, gd = Gather(geo, lane), Many(Gather, geo, lane, PAIRS), Gather(geo, lane), Gather(geo, lane)
+    ri = Many(Scatter, geo, lane, PAIRS)
+    ru, rd, rv = Scatter(geo, lane), Scatter(geo, lane), Scatter(geo, lane)
+    plan = (fwd, bwd, gs, gi, gu, gd, ri, ru, rd, rv)
+    lead = (geo.Z, geo.X, geo.Y, 2)
+    down_rows = down_weight.shape[0]
+    wide = D + FF
+    V = pltpu.VMEM
+    scratch = [
+        V(lead + (rows, 256), BF), V((PAIRS, rows, 384), BF), V((PAIRS,) + lead + (rows, 384), BF),
+        V((rows, wide), BF), V(lead + (rows, wide), BF), V(lead + (down_rows, D), BF),
+        V((2, L, D), BF), V((2, D, L), BF), V((2, PAIRS, L, 384), BF), V((2, H, L, M), BF), V((2, H, L, M), BF),
+        V((2, L, D), F32), V((2, L, D), BF), V((2, L, D), F32), V((2, D, L), BF),
+        V((2, L, 512), BF), V((2, L, 512), BF),
+        V((8, D), F32), V((FF // 128, 128), F32), V((FF // 128, 128), F32), V((8, D), F32),
+        V((2, M, M), BF), V((M, 2 * M), BF),
+        V((PAIRS,) + lead + (rows, 384), BF), V(lead + (rows, wide), BF), V(lead + (down_rows, D), BF),
+        V(lead + (rows, 256), BF),
+    ]
+    scratch += States.scratch(geo) + States.scratch(geo)
+    scratch += [V((PAIRS,) + s.shape, s.dtype) for s in Scatter.scratch(geo, rows, 384)]
+    scratch += Scatter.scratch(geo, rows, wide) + Scatter.scratch(geo, down_rows, D) + Scatter.scratch(geo, rows, 256)
+    scratch += [pltpu.SemaphoreType.DMA((lane.count,)), pltpu.SemaphoreType.DMA((lane.count,))]
+    vmem = pl.BlockSpec(memory_space=pltpu.VMEM)
+    shape = jax.ShapeDtypeStruct
+    outs = [shape(tokens.shape, F32), shape(tokens.shape, F32), shape((PAIRS, rows, 384), F32),
+            shape((rows, wide), F32), shape((down_rows, D), F32), shape((rows, 256), F32)]
+    result, tokens_grad, inp, ou, down, vec = pl.pallas_call(
+        functools.partial(layer_kernel, geo, lane, plan),
+        out_shape=outs, in_specs=[vmem] * 8, out_specs=[vmem] * 6, scratch_shapes=scratch,
+        compiler_params=pltpu.CompilerParams(collective_id=0, has_side_effects=True, vmem_limit_bytes=60 << 20),
+    )(tokens, cotangent, feature_matrix, small, input_weight, output_weight, up_weight, down_weight)
+    inp = inp.reshape(PAIRS, rows, 3, 128).transpose(1, 2, 0, 3).reshape(rows, 3 * D)
+    up_bias_grad = lax.dynamic_slice(vec[0], (128 + core * width,), (width,))
+    return (result, tokens_grad, inp, ou[:, :D], vec[:, 0], ou[:, D:], up_bias_grad, down,
             vec[:, 1], vec[:, 2], vec[:, 3], vec[:, 4], vec[:, 5])
 
 

time: 464 us -> 178 us (0.38); the launches traced: 455 us -> 178 us
  matrix products: 178 us -> 0 us
  local copies, waits for them, and re-layouts: 84.2 us -> 18.1 us
  Pallas kernels: 111 us -> 158 us
  other arithmetic: 44.1 us -> 0.62 us
  blocking collectives: 21.1 us -> 0 us
  between operations: 15.6 us -> 0.69 us
    dot_general x60 -> x0, matrix products: 178 us -> none  [the longest x2 16.5 us: attend(): jnp.einsum('ihm,jhm->hij', query_reduced, key_reduced, preferred_element_...]
    pallas_call x2 -> x1, Pallas kernels: 111 us -> 158 us  [fused(): pl.pallas_call(functools.partial(layer_kernel, geo, lane, plan), out_shap...]
    unnamed x269 -> x7, local copies, waits for them, and re-layouts: 29.8 us -> 5.21 us
    dynamic_slice x28 -> x1, local copies, waits for them, and re-layouts: 23.3 us -> 0.58 us  [fused(): up_bias_grad = lax.dynamic_slice(vec[0], (128 + core * width,), (width,))]
    select_n x16 -> x1, other arithmetic: 21.9 us -> 0.01 us  [fused(): jnp.where(jnp.arange(128) // width == core, jnp.tile(up_bias, 128 // widt...]
    all_gather x4 -> x0, blocking collectives: 21.1 us -> none  [the longest x2 10.8 us: prefix(): lax.all_gather(part.astype(kind), axis)]
    reduce_sum x14 -> x0, other arithmetic: 13.5 us -> none  [the longest x2 5.31 us: upper_back(): stored['down_bias'] = jnp.sum(upstream, axis=0)]
    dot_general x6 -> x0, local copies, waits for them, and re-layouts: 9.23 us -> none  [the longest x2 5.11 us: upper_back(): jnp.einsum('rf,df->rd', up_term, params[3], preferred_element_type=jnp.fl...]
  transfers between devices with their start and end apart: 4 -> 0, of which waited for: 0 -> 0; matrix products, arithmetic and copies ran while one was open for 29% -> 0% of each run, Pallas kernels for 0% -> 0%
where the time goes in v2:
time: 178 us
  Pallas kernels  158 us (89%)
  local copies, waits for them, and re-layouts  18.1 us (10%)
    pallas_call x1, Pallas kernels, fused(): pl.pallas_call(functools.partial(layer_kernel, geo, lane, plan), out_shap...  158 us
    unnamed x7, local copies, waits for them, and re-layouts  5.21 us
    another operation x7, local copies, waits for them, and re-layouts, fused(): jnp.stack([output_bias, down_bias, first_gain, first_shift, second_gain,...  4.56 us

profile of v2, /device:TPU:0, one launch (start us, length us, event | category | flops | bytes accessed | tf_op | source)
XLA Modules:
  0.0 177.7 jit_solution(1814265188923192339)
XLA Ops:
  0.7 0.7 tile.4
  1.3 0.1 tile.10
  1.4 0.7 copy.40
  2.2 0.7 copy.41
  2.9 0.7 copy.42
  3.6 0.7 copy.43
  4.4 0.7 copy.44
  5.1 0.7 copy.45
  5.9 0.1 stack.27
  6.0 0.6 fusion.2.refs_3_
  6.6 158.2 %shard_map.237 = (f32[2,512,512]{2,1,0:T(8,128)}, f32[2,512,512]{2,1,0:T(8,128)}, f32[4,16,384]{2,1,0:T(8,128)}, f32[16,2560]{1,0:T(8,128)}, f32[64,512]{1,0:T(8,128)}, /*index=5*/f32[16,256]{1,0:T(8,128)}) custom-call(bf16[2,512,512]{2,1,0:T(8,128)(2,1)} %refs_0_.1, bf16[2,512,512]{2,1,0:T(8,128)(2,1)} %refs_1_.1, bf16[64,256]{1,0:T(8,128)(2,1)} %refs_2_.1, ...), custom_call_target="tpu_custom_call" | custom-call | tf_op jit(solution)/shard_map/pallas_call | solution.py:1182
  164.8 0.7 slice.30
  165.5 1.7 slice_reduce_fusion
  167.2 0.6 dynamic-slice_bitcast_fusion
  167.8 1.4 slice.27
  169.2 1.6 slice.29
  170.7 0.9 reshape.81
  171.7 0.1 copy.46
  171.8 0.7 reshape.82
  172.4 0.0 copy-start
  172.4 3.2 %copy.50 = f32[2,512,512]{2,1,0:T(8,128)} copy(f32[2,512,512]{2,1,0:T(8,128)} %get-tuple-element.44) | data formatting | bytes 4194304
  175.7 0.0 copy-done
  175.7 0.0 copy-start.1
  175.7 1.3 copy.51
  177.0 0.0 copy-done.1
  177.0 0.7 copy.52
  (1 shorter events, 0.0 us)
Async XLA Ops:
  172.4 3.2 %copy-start = (f32[2,512,512]{2,1,0:T(8,128)S(1)}, f32[2,512,512]{2,1,0:T(8,128)}, u32[]{:S(2)}) copy-start(f32[2,512,512]{2,1,0:T(8,128)} %get-tuple-element.45) | copy-start | bytes 6291460
  175.7 1.3 copy-start.1

commit v3 on v2

--- a/solution.py
+++ b/solution.py
@@ -33,9 +33,8 @@
     def barrier(self):
         z, x, y, c = self.me()
         peers = [self.device(z, x, y, 1 - c)]
-        peers += [self.device((z + k) % self.Z, x, y, c) for k in range(1, self.Z)]
-        peers += [self.device(z, (x + k) % self.X, y, c) for k in range(1, self.X)]
-        peers += [self.device(z, x, (y + k) % self.Y, c) for k in range(1, self.Y)]
+        peers += [self.device((z + i) % self.Z, (x + j) % self.X, (y + k) % self.Y, c)
+                  for i in range(self.Z) for j in range(self.X) for k in range(self.Y)][1:]
         semaphore = pltpu.get_barrier_semaphore()
         for peer in peers:
             pl.semaphore_signal(semaphore, inc=1, device_id=peer, device_id_type=MESH)
@@ -62,20 +61,10 @@
 class Gather:
     def __init__(self, geo, lane):
         self.geo, self.lane = geo, lane
-        self.begin = lane.count
         self.zs = lane.take(geo.Z - 1)
         self.second = lane.take(max(geo.X, geo.Y) - 1)
         self.third = lane.take(max(geo.X, geo.Y) - 1)
         self.core = lane.take()
-
-    indices = ("zs", "second", "third", "core")
-
-    def shifted(self, by):
-        other = object.__new__(type(self))
-        other.geo, other.lane = self.geo, self.lane
-        for name in self.indices:
-            setattr(other, name, getattr(self, name) + by)
-        return other
 
     def bind(self, own, full):
         self.own, self.full = own, full
@@ -162,7 +151,6 @@
 class Scatter:
     def __init__(self, geo, lane):
         self.geo, self.lane = geo, lane
-        self.begin = lane.count
         self.core = lane.take()
         self.first = lane.take(max(geo.X, geo.Y) - 1)
         self.second = lane.take(max(geo.X, geo.Y) - 1)
@@ -178,15 +166,6 @@
             pltpu.VMEM((wide - 1, geo.Z, rows, width), kind),
             pltpu.VMEM((geo.Z - 1, rows, width), kind),
         ]
-
-    indices = ("core", "first", "second", "zs")
-
-    def shifted(self, by):
-        other = object.__new__(type(self))
-        other.geo, other.lane = self.geo, self.lane
-        for name in self.indices:
-            setattr(other, name, getattr(self, name) + by)
-        return other
 
     def bind(self, part, out, buffers):
         self.part, self.out = part, out
@@ -692,54 +671,162 @@
                     copy.wait_send()
 
 
-class Many:
-    def __init__(self, kind, geo, lane, count):
-        self.tasks = [kind(geo, lane) for _ in range(count)]
-        self.per = (lane.count - self.tasks[0].begin) // count
-
-    def bind(self, chunk):
-        self.chunk = chunk
-
-    def step(self, n, p):
-        task = self.tasks[0].shifted(p * self.per)
-        task.bind(*self.chunk(p))
-        task.step(n)
+class PairStates:
+    def __init__(self, states, p):
+        self.states, self.p = states, p
+
+    def step(self, n):
+        self.states.step(n, self.p)
+
+
+class ScatterDirect:
+    def __init__(self, geo, lane):
+        self.geo, self.lane = geo, lane
+        self.far = [(i, j, k) for i in range(geo.Z) for j in range(geo.X) for k in range(geo.Y)][1:]
+        self.core = lane.take()
+        self.first = lane.take(len(self.far))
+
+    @staticmethod
+    def scratch(geo, rows, width):
+        return [pltpu.VMEM((geo.Z, geo.X, geo.Y, rows, width), jnp.bfloat16),
+                pltpu.VMEM((geo.Z * geo.X * geo.Y - 1, rows, width), jnp.bfloat16)]
+
+    def bind(self, part, out, buffers):
+        self.part, self.out = part, out
+        self.rc, self.rz = buffers
+
+    def core_copy(self):
+        z, x, y, c = self.geo.me()
+        return remote(self.lane, self.core, self.part.at[:, :, :, 1 - c], self.rc, self.geo.device(z, x, y, 1 - c))
+
+    def copies(self):
+        g = self.geo
+        z, x, y, c = g.me()
+        for n, (i, j, k) in enumerate(self.far):
+            to = ((z + i) % g.Z, (x + j) % g.X, (y + k) % g.Y, c)
+            yield remote(self.lane, self.first + n, self.part.at[to], self.rz.at[n], g.device(*to))
+
+    def step(self, n):
+        g = self.geo
+        z, x, y, c = g.me()
+        if n == 0:
+            self.core_copy().start()
+        elif n == 1:
+            self.core_copy().wait_recv()
+
+            def add(i, _):
+                total = self.part[i, :, :, c].astype(F32) + self.rc[i].astype(F32)
+                self.part[i, :, :, c] = total.astype(BF)
+                return 0
+            lax.fori_loop(0, g.Z, add, 0)
+            for copy in self.copies():
+                copy.start()
+        else:
+            total = self.part[z, x, y, c].astype(F32)
+            for n, copy in enumerate(self.copies()):
+                copy.wait_recv()
+                total += self.rz[n].astype(F32)
+            self.out[...] = total
 
     def drain(self):
-        for p in range(len(self.tasks)):
-            task = self.tasks[0].shifted(p * self.per)
-            task.bind(*self.chunk(p))
-            task.drain()
+        self.core_copy().wait_send()
+        for copy in self.copies():
+            copy.wait_send()
+
+
+DIRECT = ("rI3", "rV",)
+PLAN = {
+    "start": (("S", 0), ("I0", 0), ("I1", 0), ("I2", 0), ("I3", 0),),
+    "first": (("O", 0), ("F0", 0), ("F1", 0), ("S", 1), ("I0", 1), ("I1", 1), ("S", 2), ("I2", 1), ("I0", 2),
+        ("I3", 1), ("I1", 2), ("S", 3), ("O", 1), ("I2", 2), ("S", 4),),
+    "norm1": (("I0", 3), ("I3", 2),),
+    "proj0.pre": (("F0", 1), ("I1", 3), ("O", 2), ("I0", 4),),
+    "proj0.1": (("f0", 0), ("I2", 3), ("F1", 1), ("I3", 3),),
+    "proj1.pre": (("I1", 4),),
+    "proj1.1": (("f1", 0), ("f0", 1),),
+    "proj2.pre": (("I2", 4),),
+    "proj2.0": (("I3", 4), ("O", 3),),
+    "proj2.1": (("f2", 0), ("f1", 1),),
+    "proj3.1": (("f3", 0), ("f2", 1), ("O", 4), ("F2", 0),),
+    "att0.pre": (("f0", 2), ("f3", 1), ("f0", 3),),
+    "att0.0": (("f1", 2), ("F0", 2),),
+    "att0.1": (("F3", 0),),
+    "att1.pre": (("f2", 2), ("f1", 3),),
+    "att1.1": (("f2", 3), ("F2", 1), ("f3", 2),),
+    "att2.0": (("F1", 2),),
+    "att2.1": (("f3", 3),),
+    "att3.0": (("F0", 3),),
+    "att3.1": (("F3", 1),),
+    "mid.0": (("F2", 2),),
+    "feed0.pre": (("F0", 4),),
+    "feed0.0": (("F1", 3),),
+    "feed0.1": (("F3", 2),),
+    "feed0.end": (("rF0", 0), ("F1", 4),),
+    "feed1.0": (("F2", 3),),
+    "feed1.1": (("rF0", 1), ("F3", 3),),
+    "feed2.pre": (("F2", 4),),
+    "feed2.0": (("F3", 4),),
+    "feed2.end": (("rF2", 0), ("rF0", 2),),
+    "feed3.1": (("rF2", 1),),
+    "feed3.end": (("rF0", 3),),
+    "out.end": (("rO", 0),),
+    "st0": (("b0", 0), ("rF2", 2),),
+    "st1": (("b1", 0), ("rF1", 0),),
+    "st2": (("b2", 0), ("rF0", 4), ("b0", 1), ("rO", 1),),
+    "st3": (("b3", 0), ("b1", 1),),
+    "pb0.pre": (("rF3", 0), ("rF2", 3), ("rF1", 1), ("b2", 1), ("b3", 1), ("b0", 2), ("rF3", 1), ("b0", 3),),
+    "pb0.m": (("rF2", 4), ("b1", 2), ("rO", 2),),
+    "pb1.m": (("b1", 3),),
+    "pb1": (("rI0", 0), ("rF1", 2),),
+    "pb2.m": (("b2", 2), ("rI0", 1),),
+    "pb3.m": (("b2", 3),),
+    "pb3": (("rI1", 0),),
+    "pb4.m": (("b3", 2), ("rI0", 2), ("rI1", 1), ("rF1", 3),),
+    "pb5.m": (("b3", 3), ("rF3", 2),),
+    "pb5": (("rI2", 0), ("rI1", 2),),
+    "pb6": (("rF3", 3),),
+    "pb7.m": (("rI2", 1), ("rI1", 3), ("rO", 3),),
+    "pb7": (("rI3", 0), ("rI0", 3),),
+    "nb1": (("rI3", 1), ("rI2", 2), ("rI1", 4), ("rF3", 4),),
+    "fb1": (("rV", 0), ("rF1", 4), ("rO", 4),),
+    "end": (("rI0", 4), ("rV", 1), ("rI2", 3), ("rI3", 2), ("rV", 2), ("rI2", 4),),
+}
 
 
 def layer_kernel(geo, lane, plan, *refs):
-    (tokens, cot, feat, small_own, wi_in, wo_in, wu_in, wd_own,
-     result, tokens_grad, inp_out, ou_out, down_out, vec_out,
-     small, wi_own, wi, wou_own, wou, wd, normed, normed_t, mixed, pq, pk, den, attended, middle, n2_t,
-     act, hg, vecs, ub, ubg, grads, fa, ft,
-     part_i, part_u, part_d, part_v) = refs[:41]
-    rest = list(refs[41:])
-    fwd, bwd, gs, gi, gu, gd, ri, ru, rd, rv = plan
+    (tokens_hbm, cot_hbm, feat, out_bias_in, down_bias_in, first_gain_in, first_shift_in, second_gain_in,
+     second_shift_in, up_bias_in, wi_in, wo_own, wu_in, wd_in,
+     result_hbm, tokens_grad_hbm, inp_out, out_out, up_out, down_out, vec_out,
+     tokens, cot, result, tokens_grad, small_own, small, wi_own, wi, wo_all, wf_own, wf,
+     normed, normed_t, mixed, pq, pk, den, attended, middle, n2_t,
+     act, hg, vecs, grads, fa, ft, perm, part_i, part_o, part_f, part_v, up_parts, vec_sum) = refs[:54]
+    rest = list(refs[54:])
+    fwd, bwd, tasks = plan
     take = lambda n: [rest.pop(0) for _ in range(n)]
     fwd.bind(take(7))
     bwd.bind(take(7))
-    bi, bu, bd, bv = take(4), take(4), take(4), take(4)
+    scatter_buffers = {name: take(2 if type(task) is ScatterDirect else 4)
+                       for name, task in tasks.items() if name[0] == "r"}
     lane.send, lane.recv = take(2)
-    gs.bind(small_own, small)
-    gi.bind(lambda p: (wi_own.at[p], wi.at[p]))
-    gu.bind(wou_own, wou)
-    gd.bind(wd_own, wd)
-    inp_parts = inp_out
-    ri.bind(lambda p: (part_i.at[p], inp_parts.at[p], [b.at[p] for b in bi]))
-    ru.bind(part_u, ou_out, bu)
-    rd.bind(part_d, down_out, bd)
-    rv.bind(part_v, vec_out, bv)
+    local_sem = rest.pop(0)
+    tasks["S"].bind(small_own, small)
+    tasks["O"].bind(wo_own, wo_all)
+    tasks["rO"].bind(part_o, out_out, scatter_buffers["rO"])
+    tasks["rV"].bind(part_v, vec_sum, scatter_buffers["rV"])
+    for p in range(PAIRS):
+        tasks[f"I{p}"].bind(wi_own.at[p], wi.at[p])
+        tasks[f"rI{p}"].bind(part_i.at[p], inp_out.at[p], scatter_buffers[f"rI{p}"])
+    for t in range(wf.shape[0]):
+        tasks[f"F{t}"].bind(wf_own.at[t], wf.at[t])
+        tasks[f"rF{t}"].bind(part_f.at[t], up_parts.at[t], scatter_buffers[f"rF{t}"])
     n2 = normed
     D = tokens.shape[-1]
     L = tokens.shape[1]
-    FF = wd.shape[0] * wd.shape[1] * wd.shape[2] * 2 * wd.shape[4]
+    TILES = wf.shape[0]
     HALF = L // 2
     lead = (geo.Z, geo.X, geo.Y, 2)
+    z, x, y, c = geo.me()
+    place = (((z * geo.X + x) * geo.Y + y) * 2 + c) % 8
 
     def loop(n, body):
         def step(i, _):
@@ -747,16 +834,43 @@
             return 0
         lax.fori_loop(0, n, step, 0)
 
+    def pump(point):
+        for name, n in PLAN.get(point, ()):
+            tasks[name].step(n)
+
+    def pump_at(now, points):
+        for when, point in enumerate(points):
+            if point in PLAN:
+                @pl.when(now == when)
+                def _():
+                    pump(point)
+
+    def local(i, src, dst):
+        return pltpu.make_async_copy(src, dst, local_sem.at[i])
+
+    local(0, tokens_hbm, tokens).start()
+    local(1, cot_hbm, cot).start()
+    vec_sum[...] = jnp.zeros((16, 128), F32)
+    for v, ref in enumerate((out_bias_in, down_bias_in, first_gain_in, first_shift_in, second_gain_in,
+                             second_shift_in)):
+        vec_sum[v, :16] = ref[...].astype(F32)
+    up_bias_row = up_bias_in[...].astype(F32)
+    for t in range(TILES):
+        vec_sum[6 + t, :16] = up_bias_row[t * 16:(t + 1) * 16]
+    small_own[...] = pltpu.roll(vec_sum[...], place * 16, 1).astype(BF)
     for p in range(PAIRS):
         wi_own[p] = jnp.concatenate([wi_in[:, k * D + p * 128: k * D + (p + 1) * 128] for k in range(3)], axis=1)
-    wou_own[:, :D] = wo_in[...]
-    wou_own[:, D:] = wu_in[...]
     geo.barrier()
-    gs.step(0)
-    for p in range(PAIRS):
-        gi.step(0, p)
-    gu.step(0)
-    gd.step(0)
+    pump("start")
+    source = lax.broadcasted_iota(jnp.int32, (512, 1), 0)
+    target = (source % 64) // 16 * 128 + source // 64 * 16 + source % 16
+    perm[...] = jnp.where(lax.broadcasted_iota(jnp.int32, (512, 512), 1) == target, 1.0, 0.0).astype(BF)
+    stacked = jnp.concatenate([wu_in[:, g * 512:(g + 1) * 512] for g in range(TILES)], axis=0)
+    stacked = dot(stacked, perm[...]).astype(BF)
+    for t in range(TILES):
+        for g in range(TILES):
+            wf_own[t, :, g * 128:(g + 1) * 128] = stacked[g * 16:(g + 1) * 16, t * 128:(t + 1) * 128]
+        wf_own[t, :, D:] = wd_in[t * 16:(t + 1) * 16]
 
     f = feat[...]
     zero = jnp.zeros((DH, M), BF)
@@ -772,20 +886,11 @@
     tri_r = lax.broadcasted_iota(jnp.int32, (HALF, HALF), 0)
     tri_c = lax.broadcasted_iota(jnp.int32, (HALF, HALF), 1)
 
-    gs.step(1)
-    gi.step(1, 0)
-    gs.step(2)
-    gi.step(1, 1)
-    gi.step(2, 0)
-    gs.step(3)
-    gi.step(1, 2)
-    gi.step(2, 1)
-    gs.step(4)
+    pump("first")
 
     flat = lambda v: v.reshape(-1, v.shape[-1])
-    sm = small[...]
-    vecs[...] = flat(sm[..., :128]).astype(F32).T[:8]
-    ub[...] = jnp.sum(sm[..., 128:].astype(F32).reshape(-1, 2 * sm.shape[-2], 128), axis=1)
+    sums = jnp.sum(small[...].astype(F32).reshape(-1, 8, 16, 128), axis=1)
+    vecs[...] = jnp.concatenate([sums[g] for g in range(D // 128)], axis=1)
     out_bias, down_bias = lambda: vecs[0:1], lambda: vecs[1:2]
 
     def norm_parts(rows):
@@ -800,62 +905,36 @@
         value = (hat * vecs[2:3] + vecs[3:4]).astype(BF)
         normed[s] = value
         normed_t[s] = value.T
-    gi.step(3, 0)
-    loop(2, first_norm)
-    gi.step(1, 3)
-    gi.step(2, 2)
-    gi.step(3, 1)
+    pump("vec")
+    local(0, tokens_hbm, tokens).wait()
+    first_norm(0)
+    pump("norm0")
+    first_norm(1)
+    pump("norm1")
 
     def vx(s, p):
         v = mixed[s, p, :, 2 * 128:]
         ones = jnp.ones(v.shape, BF)
         return (jnp.concatenate([v * m0, ones * m0], axis=1), jnp.concatenate([v * m1, ones * m1], axis=1))
 
-    def project(p):
-        gi.step(4, p)
-        w = flat(wi[p])
-
-        def seq(s):
-            mixed[s, p] = dot(normed[s], w).astype(BF)
-            for part, target in ((0, pq), (1, pk)):
-                rows = mixed[s, p, :, part * 128:(part + 1) * 128]
-                wide = rows.astype(F32)
-                lhs = jnp.concatenate([rows, (wide * wide * (0.5 * SCALE)).astype(BF)], axis=1)
-                for h in range(2):
-                    power = dot(lhs, fa[h]) * (SCALE * LOG2E) - 0.5 * math.log2(M)
-                    target[s, 2 * p + h] = jnp.exp2(power).astype(BF)
-            v = mixed[s, p, :, 2 * 128:]
-            lhs = jnp.concatenate([v.T, jnp.ones((16, L), BF)], axis=0)
-            r0 = dot(lhs, pk[s, 2 * p])
-            r1 = dot(lhs, pk[s, 2 * p + 1])
-            fwd.own[p, s] = jnp.concatenate([r0[:64], r1[64:128], r0[128:], r1[128:]], axis=0).astype(BF)
-        loop(2, seq)
-        fwd.step(0, p)
-
-        @pl.when(p == 0)
-        def _():
-            gi.step(2, 3)
-            gi.step(3, 2)
-            gu.step(1)
-
-        @pl.when(p == 1)
-        def _():
-            gi.step(3, 3)
-            gd.step(1)
-
-        @pl.when(p == 2)
-        def _():
-            gu.step(2)
-
-        for n in range(1, 4):
-            @pl.when(p >= n)
-            def _():
-                fwd.step(n, p - n)
-    loop(PAIRS, project)
-    gd.step(2)
-    fwd.step(1, 3)
-    fwd.step(2, 2)
-    fwd.step(3, 1)
+    def project(i):
+        p, s = i // 2, i % 2
+        pump_at(i, [f"proj{n // 2}.pre" if n % 2 == 0 else "" for n in range(2 * PAIRS)])
+        mixed[s, p] = dot(normed[s], flat(wi[p])).astype(BF)
+        for part, target in ((0, pq), (1, pk)):
+            rows = mixed[s, p, :, part * 128:(part + 1) * 128]
+            wide = rows.astype(F32)
+            lhs = jnp.concatenate([rows, (wide * wide * (0.5 * SCALE)).astype(BF)], axis=1)
+            for h in range(2):
+                power = dot(lhs, fa[h]) * (SCALE * LOG2E) - 0.5 * math.log2(M)
+                target[s, 2 * p + h] = jnp.exp2(power).astype(BF)
+        v = mixed[s, p, :, 2 * 128:]
+        lhs = jnp.concatenate([v.T, jnp.ones((16, L), BF)], axis=0)
+        r0 = dot(lhs, pk[s, 2 * p])
+        r1 = dot(lhs, pk[s, 2 * p + 1])
+        fwd.own[p, s] = jnp.concatenate([r0[:64], r1[64:128], r0[128:], r1[128:]], axis=0).astype(BF)
+        pump_at(i, [f"proj{n // 2}.{n % 2}" for n in range(2 * PAIRS)])
+    loop(2 * PAIRS, project)
 
     def state_cols(total, p, s, h, copies):
         state = total[p, s, h * 64:(h + 1) * 64]
@@ -871,44 +950,34 @@
     lower = tri_r >= tri_c
     upper = tri_r <= tri_c
 
-    def attend_pair(p):
-        def seq(s):
-            v0, v1 = vx(s, p)
-            states = jnp.concatenate([state_cols(fwd.total, p, s, h, True) for h in range(2)], axis=1)
-            lanes = pl.ds(pl.multiple_of(p * 128, 128), 128)
-            for b in range(2):
-                rows = slice(b * HALF, (b + 1) * HALF)
-                scores = []
-                for h in range(2):
-                    q = pq[s, 2 * p + h, rows]
-                    if b == 1:
-                        scores.append(dot_nt(q, pk[s, 2 * p + h, :HALF]).astype(BF))
-                    scores.append(jnp.where(lower, dot_nt(q, pk[s, 2 * p + h, rows]), 0.0).astype(BF))
-                rhs = jnp.concatenate([v0[:(b + 1) * HALF], v1[:(b + 1) * HALF]], axis=0)
-                ext = dot(jnp.concatenate(scores, axis=1), rhs)
-                ext += dot_nt(jnp.concatenate([pq[s, 2 * p, rows], pq[s, 2 * p + 1, rows]], axis=1), states)
-                n_, d_ = ext[:, :128], ext[:, 128:]
-                inv = 1.0 / d_
-                den[s, rows, lanes] = inv
-                attended[s, rows, lanes] = (n_ * inv).astype(BF)
-        loop(2, seq)
-
-        @pl.when(p == 0)
-        def _():
-            fwd.step(2, 3)
-            fwd.step(3, 2)
-            gu.step(3)
-
-        @pl.when(p == 1)
-        def _():
-            fwd.step(3, 3)
-            gd.step(3)
-    loop(PAIRS, attend_pair)
-    gu.step(4)
-    gd.step(4)
+    def attend_pair(i):
+        p, s = i // 2, i % 2
+        pump_at(i, [f"att{n // 2}.pre" if n % 2 == 0 else "" for n in range(2 * PAIRS)])
+        v0, v1 = vx(s, p)
+        states = jnp.concatenate([state_cols(fwd.total, p, s, h, True) for h in range(2)], axis=1)
+        lanes = pl.ds(pl.multiple_of(p * 128, 128), 128)
+        for b in range(2):
+            rows = slice(b * HALF, (b + 1) * HALF)
+            scores = []
+            for h in range(2):
+                q = pq[s, 2 * p + h, rows]
+                if b == 1:
+                    scores.append(dot_nt(q, pk[s, 2 * p + h, :HALF]).astype(BF))
+                scores.append(jnp.where(lower, dot_nt(q, pk[s, 2 * p + h, rows]), 0.0).astype(BF))
+            rhs = jnp.concatenate([v0[:(b + 1) * HALF], v1[:(b + 1) * HALF]], axis=0)
+            ext = dot(jnp.concatenate(scores, axis=1), rhs)
+            ext += dot_nt(jnp.concatenate([pq[s, 2 * p, rows], pq[s, 2 * p + 1, rows]], axis=1), states)
+            n_, d_ = ext[:, :128], ext[:, 128:]
+            inv = 1.0 / d_
+            den[s, rows, lanes] = inv
+            attended[s, rows, lanes] = (n_ * inv).astype(BF)
+        pump_at(i, [f"att{n // 2}.{n % 2}" for n in range(2 * PAIRS)])
+    loop(2 * PAIRS, attend_pair)
+    pump("mid.pre")
+    local(1, cot_hbm, cot).wait()
 
     def wo():
-        return flat(wou[..., :D])
+        return flat(wo_all[...])
 
     def to_middle(s):
         value = tokens[s].astype(F32) + dot(attended[s], wo()) + out_bias()
@@ -919,17 +988,17 @@
         n2_t[s] = low.T
         result[s] = value + down_bias()
         tokens_grad[s] = jnp.zeros((L, D), F32)
+        pump_at(s, ["mid.0", "mid.1"])
     loop(2, to_middle)
-    ubg[...] = jnp.zeros(ubg.shape, F32)
     grads[...] = jnp.zeros(grads.shape, F32)
 
     k0 = math.sqrt(2.0 / math.pi)
 
     def feed_tile(t):
-        lanes = pl.ds(pl.multiple_of(D + t * 512, 512), 512)
-        bias = jnp.concatenate([ub[pl.ds(4 * t + i, 1)] for i in range(4)], axis=1)
-        wut = lambda: flat(wou[:, :, :, :, :, lanes])
-        wdt = lambda: flat(wd[t])
+        pump_at(t, [f"feed{n}.pre" for n in range(TILES)])
+        bias = vecs[pl.ds(6 + t, 1)]
+        wut = lambda: flat(wf[t, :, :, :, :, :, :D])
+        wdt = lambda: flat(wf[t, :, :, :, :, :, D:])
 
         def seq(s):
             for b in range(2):
@@ -942,20 +1011,20 @@
                 act[s, rows] = a
                 slope = half + (0.5 * u) * (1.0 - th * th) * (k0 + (3.0 * 0.044715 * k0) * uu)
                 back = dot_nt(cot[s, rows], wdt()) * slope
-                total = jnp.sum(back, axis=0, keepdims=True)
-                for i in range(4):
-                    ubg[pl.ds(4 * t + i, 1)] += total[:, i * 128:(i + 1) * 128]
+                grads[pl.ds(6 + t, 1)] += jnp.sum(back, axis=0, keepdims=True)
                 low = back.astype(BF)
                 hg[s, rows] = low
                 result[s, rows] += dot(a, wdt())
                 tokens_grad[s, rows] += dot_nt(low, wut())
+            pump_at(2 * t + s, [f"feed{n // 2}.{n % 2}" for n in range(2 * TILES)])
         loop(2, seq)
         dwd = dot(act[0].T, cot[0]) + dot(act[1].T, cot[1])
-        part_d[t] = dwd.astype(BF).reshape(part_d.shape[1:])
+        part_f[t, :, :, :, :, :, D:] = dwd.astype(BF).reshape(lead + (-1, D))
         dwu = dot(n2_t[0], hg[0]) + dot(n2_t[1], hg[1])
-        part_u[:, :, :, :, :, lanes] = dwu.astype(BF).reshape(lead + (-1, 512))
-    loop(FF // 512, feed_tile)
-    rd.step(0)
+        part_f[t, :, :, :, :, :, :D] = dwu.astype(BF).reshape(lead + (-1, 512))
+        pump_at(t, [f"feed{n}.end" for n in range(TILES)])
+    loop(TILES, feed_tile)
+    local(2, result, result_hbm).start()
 
     ones_block = jnp.concatenate([jnp.concatenate([jnp.ones((64, 64), F32), jnp.zeros((64, 64), F32)], axis=1),
                                   jnp.concatenate([jnp.zeros((64, 64), F32), jnp.ones((64, 64), F32)], axis=1)],
@@ -998,10 +1067,11 @@
             dhi = dgr.astype(BF).astype(F32)
             dlo = dgr - dhi
             hg[s, :, cols] = (dhi * hi_lane + dlo * lo_lane).astype(BF)
+        pump_at(s, ["out.0", "out.1"])
     loop(2, out_back)
     dwo = dot(attended[0].T, act[0]) + dot(attended[1].T, act[1])
-    part_u[:, :, :, :, :, :D] = dwo.astype(BF).reshape(lead + (-1, D))
-    ru.step(0)
+    part_o[...] = dwo.astype(BF).reshape(lead + (-1, D))
+    pump("out.end")
 
     def ngx(s, p):
         lanes = pl.ds(pl.multiple_of(p * 128, 128), 128)
@@ -1014,30 +1084,16 @@
             r1 = dot(lhs, pq[s, 2 * p + 1])
             bwd.own[p, s] = jnp.concatenate([r0[:64], r1[64:128], r0[128:144], r1[192:208]], axis=0).astype(BF)
         loop(2, seq)
-        bwd.step(0, p)
-
-        @pl.when(p == 1)
-        def _():
-            rd.step(1)
-
-        @pl.when(p == 3)
-        def _():
-            ru.step(1)
-        for n in range(1, 4):
-            @pl.when(p >= n)
-            def _():
-                bwd.step(n, p - n)
+        pump_at(p, [f"st{n}" for n in range(PAIRS)])
     loop(PAIRS, state_back)
-    bwd.step(1, 3)
-    bwd.step(2, 2)
-    bwd.step(3, 1)
 
     def pair_back(i):
         p, s = i // 2, i % 2
+        pump_at(i, [f"pb{n}.pre" for n in range(2 * PAIRS)])
         v0, v1 = vx(s, p)
         x = ngx(s, p)
         ng = x[:, :128]
-        logs_q, logs_k, at = [], [], []
+        logs_q, logs_k, att = [], [], []
         for h, v in ((0, v0), (1, v1)):
             q, k = pq[s, 2 * p + h], pk[s, 2 * p + h]
             sx = state_cols(fwd.total, p, s, h, True)
@@ -1061,11 +1117,12 @@
             a00 = masked(upper, dot_nt(k[lo], q[lo]))
             a01 = dot_nt(k[lo], q[hi]).astype(BF)
             a11 = masked(upper, dot_nt(k[hi], q[hi]))
-            at.append((a00, a01, a11))
+            att.append((a00, a01, a11))
+        pump_at(i, [f"pb{n}.m" for n in range(2 * PAIRS)])
         n0, n1 = ng * m0, ng * m1
-        vg0 = dot(jnp.concatenate([at[0][0], at[0][1], at[1][0], at[1][1]], axis=1),
+        vg0 = dot(jnp.concatenate([att[0][0], att[0][1], att[1][0], att[1][1]], axis=1),
                   jnp.concatenate([n0, n1], axis=0))
-        vg1 = dot(jnp.concatenate([at[0][2], at[1][2]], axis=1), jnp.concatenate([n0[HALF:], n1[HALF:]], axis=0))
+        vg1 = dot(jnp.concatenate([att[0][2], att[1][2]], axis=1), jnp.concatenate([n0[HALF:], n1[HALF:]], axis=0))
         zeros = jnp.zeros((DH, M), BF)
         sgt = jnp.concatenate([jnp.concatenate([bwd.total[p, s, :64], zeros], axis=0),
                                jnp.concatenate([zeros, bwd.total[p, s, 64:128]], axis=0)], axis=1)
@@ -1078,64 +1135,95 @@
             out.append((SCALE * through[:, :128] - SCALE * SCALE * through[:, 128:] * rows).astype(BF))
         mg = jnp.concatenate(out + [vg.astype(BF)], axis=1)
         act[s, :, :384] = mg
-        back = dot_nt(mg, flat(wi[p]))
-
-        @pl.when(p == 0)
-        def _():
-            tokens_grad[s] = back
-
-        @pl.when(p > 0)
-        def _():
-            tokens_grad[s] += back
+        mixed[s, p] = mg
 
         @pl.when(s == 1)
         def _():
             dwi = dot(normed_t[0], act[0, :, :384]) + dot(normed_t[1], act[1, :, :384])
             part_i[p] = dwi.astype(BF).reshape(lead + (-1, 384))
-            ri.step(0, p)
-        schedule = {0: [lambda: bwd.step(2, 3), lambda: bwd.step(3, 2)], 1: [lambda: bwd.step(3, 3)],
-                    2: [lambda: rd.step(2), lambda: ri.step(1, 0)],
-                    3: [lambda: ru.step(2)],
-                    4: [lambda: rd.step(3), lambda: ri.step(2, 0), lambda: ri.step(1, 1)],
-                    5: [lambda: ru.step(3)],
-                    6: [lambda: rd.step(4), lambda: ri.step(3, 0), lambda: ri.step(2, 1), lambda: ri.step(1, 2)],
-                    7: [lambda: ru.step(4), lambda: ri.step(4, 0), lambda: ri.step(3, 1), lambda: ri.step(2, 2)]}
-        for at_step, actions in schedule.items():
-            @pl.when(i == at_step)
-            def _():
-                for action in actions:
-                    action()
+        pump_at(i, [f"pb{n}" for n in range(2 * PAIRS)])
     loop(2 * PAIRS, pair_back)
-    ri.step(1, 3)
+
+    def normed_back(s):
+        for b in range(2):
+            rows = slice(b * HALF, (b + 1) * HALF)
+            back = dot_nt(mixed[s, 0, rows], flat(wi[0]))
+            for p in range(1, PAIRS):
+                back += dot_nt(mixed[s, p, rows], flat(wi[p]))
+            tokens_grad[s, rows] = back
+    normed_back(0)
+    pump("nb0")
+    normed_back(1)
+    pump("nb1")
 
     def first_back(s):
         dx, dgain, dshift = norm_back(tokens[s].astype(F32), tokens_grad[s], vecs[2:3])
         tokens_grad[s] = middle[s] + dx
         grads[2:3] += dgain
         grads[3:4] += dshift
-    loop(2, first_back)
-    part_v[..., :128] = jnp.concatenate([grads[...], jnp.zeros((120, D), F32)], axis=0).T.astype(BF).reshape(lead + (-1, 128))
-    first_row = lax.broadcasted_iota(jnp.int32, (16, 128), 0) == 0
-    for z in range(geo.Z):
-        for x in range(geo.X):
-            for y in range(geo.Y):
-                chip = (z * geo.X + x) * geo.Y + y
-                tile = jnp.where(first_row, ubg[chip:chip + 1], 0.0).astype(BF)
-                for c in range(2):
-                    part_v[z, x, y, c, :, 128:] = tile
-    rv.step(0)
-    ri.step(4, 1)
-    ri.step(3, 2)
-    ri.step(2, 3)
-    rv.step(1)
-    ri.step(4, 2)
-    ri.step(3, 3)
-    rv.step(2)
-    ri.step(4, 3)
-    rv.step(3)
-    rv.step(4)
-    for task in (gs, gi, gu, gd, fwd, bwd, ri, ru, rd, rv):
+    first_back(0)
+    pump("fb0")
+    first_back(1)
+    for g in range(D // 128):
+        tile = grads[:, g * 128:(g + 1) * 128].astype(BF)
+        for k in range(8):
+            chip, core = (8 * g + k) // 2, k % 2
+            part_v[chip // (geo.X * geo.Y), chip // geo.Y % geo.X, chip % geo.Y, core] = tile
+    local(3, tokens_grad, tokens_grad_hbm).start()
+    pump("fb1")
+    stacked = jnp.concatenate([jnp.concatenate([up_parts[t, :, g * 128:(g + 1) * 128] for t in range(TILES)], axis=1)
+                               for g in range(TILES)], axis=0)
+    high = stacked.astype(BF)
+    low = (stacked - high.astype(F32)).astype(BF)
+    stacked = dot_nt(high, perm[...]) + dot_nt(low, perm[...])
+    for g in range(TILES):
+        up_out[:, g * 512:(g + 1) * 512] = stacked[g * 16:(g + 1) * 16]
+    for t in range(TILES):
+        down_out[t * 16:(t + 1) * 16] = up_parts[t, :, D:]
+    late = {name for name, n in PLAN["end"]}
+    drains = [fwd, bwd] + [task for name, task in tasks.items() if name not in late and hasattr(task, "drain")]
+    for task in drains:
         task.drain()
+    pump("end")
+    vec_out[...] = pltpu.roll(vec_sum[...], lax.rem(8 - place, 8) * 16, 1)
+    local(2, result, result_hbm).wait()
+    local(3, tokens_grad, tokens_grad_hbm).wait()
+    for name in sorted(late):
+        if hasattr(tasks[name], "drain"):
+            tasks[name].drain()
+
+
+def finish_kernel(result_in, tokens_grad_in, inp, out, up, down, vec, *refs):
+    (result, tokens_grad, inp_out, out_out, out_bias, up_out, up_bias, down_out, down_bias,
+     first_gain, first_shift, second_gain, second_shift, held, in_sems, out_sems) = refs
+    cuts = []
+    for a, b, n in ((result_in, result, 0), (tokens_grad_in, tokens_grad, 1)):
+        for m in range(a.shape[0]):
+            for k in range(2):
+                rows = pl.ds(k * (a.shape[1] // 2), a.shape[1] // 2)
+                i = len(cuts)
+                slot = held.at[n, m, rows]
+                cuts.append((pltpu.make_async_copy(a.at[m, rows], slot, in_sems.at[i]),
+                             pltpu.make_async_copy(slot, b.at[m, rows], out_sems.at[i])))
+    for first, _ in cuts:
+        first.start()
+    D = out.shape[-1]
+    for p in range(PAIRS):
+        for k in range(3):
+            inp_out[:, k * D + p * 128: k * D + (p + 1) * 128] = inp[p, :, k * 128:(k + 1) * 128]
+    out_out[...] = out[...]
+    up_out[...] = up[...]
+    down_out[...] = down[...]
+    n = out_bias.shape[-1]
+    for v, ref in enumerate((out_bias, down_bias, first_gain, first_shift, second_gain, second_shift)):
+        ref[...] = vec[v, :n]
+    for t in range(4):
+        up_bias[pl.ds(t * n, n)] = vec[6 + t, :n]
+    for first, second in cuts:
+        first.wait()
+        second.start()
+    for _, second in cuts:
+        second.wait()
 
 
 def fused(geo, args):
@@ -1144,51 +1232,57 @@
     rows, D = input_weight.shape[0], tokens.shape[-1]
     L = tokens.shape[1]
     FF = up_weight.shape[1]
-    core = geo.me()[3]
-    cols = jnp.stack([output_bias, down_bias, first_gain, first_shift, second_gain, second_shift], axis=1)
-    width = up_bias.shape[0]
-    placed = jnp.where(jnp.arange(128) // width == core, jnp.tile(up_bias, 128 // width), 0)
-    small = jnp.concatenate([jnp.pad(cols, ((0, 0), (0, 122))),
-                             jnp.pad(placed[None], ((0, rows - 1), (0, 0)))], axis=1)
+    tiles = FF // 512
     lane = Lane()
     fwd, bwd = States(geo, lane, True), States(geo, lane, False)
-    gs, gi, gu, gd = Gather(geo, lane), Many(Gather, geo, lane, PAIRS), Gather(geo, lane), Gather(geo, lane)
-    ri = Many(Scatter, geo, lane, PAIRS)
-    ru, rd, rv = Scatter(geo, lane), Scatter(geo, lane), Scatter(geo, lane)
-    plan = (fwd, bwd, gs, gi, gu, gd, ri, ru, rd, rv)
+    tasks = {name: Gather(geo, lane) for name in ["S", "O"] + [f"I{p}" for p in range(PAIRS)]
+             + [f"F{t}" for t in range(tiles)]}
+    scatters = {"rO": D, "rV": 128}
+    scatters.update({f"rI{p}": 384 for p in range(PAIRS)})
+    scatters.update({f"rF{t}": 2 * D for t in range(tiles)})
+    for name in scatters:
+        tasks[name] = (ScatterDirect if name in DIRECT else Scatter)(geo, lane)
+    for p in range(PAIRS):
+        tasks[f"f{p}"], tasks[f"b{p}"] = PairStates(fwd, p), PairStates(bwd, p)
+    plan = (fwd, bwd, tasks)
     lead = (geo.Z, geo.X, geo.Y, 2)
-    down_rows = down_weight.shape[0]
-    wide = D + FF
     V = pltpu.VMEM
     scratch = [
-        V(lead + (rows, 256), BF), V((PAIRS, rows, 384), BF), V((PAIRS,) + lead + (rows, 384), BF),
-        V((rows, wide), BF), V(lead + (rows, wide), BF), V(lead + (down_rows, D), BF),
+        V((2, L, D), BF), V((2, L, D), BF), V((2, L, D), F32), V((2, L, D), F32),
+        V((rows, 128), BF), V(lead + (rows, 128), BF), V((PAIRS, rows, 384), BF), V((PAIRS,) + lead + (rows, 384), BF),
+        V(lead + (rows, D), BF), V((tiles, rows, 2 * D), BF), V((tiles,) + lead + (rows, 2 * D), BF),
         V((2, L, D), BF), V((2, D, L), BF), V((2, PAIRS, L, 384), BF), V((2, H, L, M), BF), V((2, H, L, M), BF),
         V((2, L, D), F32), V((2, L, D), BF), V((2, L, D), F32), V((2, D, L), BF),
-        V((2, L, 512), BF), V((2, L, 512), BF),
-        V((8, D), F32), V((FF // 128, 128), F32), V((FF // 128, 128), F32), V((8, D), F32),
-        V((2, M, M), BF), V((M, 2 * M), BF),
-        V((PAIRS,) + lead + (rows, 384), BF), V(lead + (rows, wide), BF), V(lead + (down_rows, D), BF),
-        V(lead + (rows, 256), BF),
+        V((2, L, 512), BF), V((2, L, 512), BF), V((16, D), F32), V((16, D), F32),
+        V((2, M, M), BF), V((M, 2 * M), BF), V((512, 512), BF),
+        V((PAIRS,) + lead + (rows, 384), BF), V(lead + (rows, D), BF), V((tiles,) + lead + (rows, 2 * D), BF),
+        V(lead + (rows, 128), BF), V((tiles, rows, 2 * D), F32), V((rows, 128), F32),
     ]
     scratch += States.scratch(geo) + States.scratch(geo)
-    scratch += [V((PAIRS,) + s.shape, s.dtype) for s in Scatter.scratch(geo, rows, 384)]
-    scratch += Scatter.scratch(geo, rows, wide) + Scatter.scratch(geo, down_rows, D) + Scatter.scratch(geo, rows, 256)
-    scratch += [pltpu.SemaphoreType.DMA((lane.count,)), pltpu.SemaphoreType.DMA((lane.count,))]
+    for name, width in scatters.items():
+        scratch += type(tasks[name]).scratch(geo, rows, width)
+    scratch += [pltpu.SemaphoreType.DMA((lane.count,)), pltpu.SemaphoreType.DMA((lane.count,)),
+                pltpu.SemaphoreType.DMA((4,))]
     vmem = pl.BlockSpec(memory_space=pltpu.VMEM)
+    hbm = pl.BlockSpec(memory_space=pl.ANY)
     shape = jax.ShapeDtypeStruct
     outs = [shape(tokens.shape, F32), shape(tokens.shape, F32), shape((PAIRS, rows, 384), F32),
-            shape((rows, wide), F32), shape((down_rows, D), F32), shape((rows, 256), F32)]
-    result, tokens_grad, inp, ou, down, vec = pl.pallas_call(
+            shape((rows, D), F32), shape((rows, FF), F32), shape(down_weight.shape, F32), shape((rows, 128), F32)]
+    parts = pl.pallas_call(
         functools.partial(layer_kernel, geo, lane, plan),
-        out_shape=outs, in_specs=[vmem] * 8, out_specs=[vmem] * 6, scratch_shapes=scratch,
+        out_shape=outs, in_specs=[hbm] * 2 + [vmem] * 12, out_specs=[hbm] * 2 + [vmem] * 5, scratch_shapes=scratch,
         compiler_params=pltpu.CompilerParams(collective_id=0, has_side_effects=True, vmem_limit_bytes=60 << 20),
-    )(tokens, cotangent, feature_matrix, small, input_weight, output_weight, up_weight, down_weight)
-    inp = inp.reshape(PAIRS, rows, 3, 128).transpose(1, 2, 0, 3).reshape(rows, 3 * D)
-    up_bias_grad = lax.dynamic_slice(vec[0], (128 + core * width,), (width,))
-    return (result, tokens_grad, inp, ou[:, :D], vec[:, 0], ou[:, D:], up_bias_grad, down,
-            vec[:, 1], vec[:, 2], vec[:, 3], vec[:, 4], vec[:, 5])
-
+    )(tokens, cotangent, feature_matrix, output_bias, down_bias, first_gain, first_shift, second_gain, second_shift,
+      up_bias, input_weight, output_weight, up_weight, down_weight)
+    vector = shape((rows,), F32)
+    return pl.pallas_call(
+        finish_kernel,
+        out_shape=[outs[0], outs[1], shape(input_weight.shape, F32), outs[3], vector, outs[4],
+                   shape(up_bias.shape, F32), outs[5]] + [vector] * 5,
+        in_specs=[hbm] * 2 + [vmem] * 5, out_specs=[hbm] * 2 + [vmem] * 11,
+        scratch_shapes=[V((2,) + tokens.shape, F32), pltpu.SemaphoreType.DMA((8,)), pltpu.SemaphoreType.DMA((8,))],
+        compiler_params=pltpu.CompilerParams(vmem_limit_bytes=60 << 20),
+    )(*parts)
 
 def local(
     tokens,
@@ -1356,7 +1450,7 @@
     )
     geo = Geometry(mesh)
     rows = 512 // (mesh.shape["dp"] * mesh.shape["seq"])
-    if rows % 16 == 0:
+    if rows == 16:
         def body(*args):
             return fused(geo, args)
     else:

time: 178 us -> 121 us (0.68)
  Pallas kernels: 158 us -> 120 us
  local copies, waits for them, and re-layouts: 18.1 us -> 0 us
    pallas_call x1, Pallas kernels: 158 us -> 114 us  [fused(): pl.pallas_call(functools.partial(layer_kernel, geo, lane, plan), out_shap...]
    pallas_call x0 -> x1, Pallas kernels: none -> 5.39 us  [fused(): pl.pallas_call(finish_kernel, out_shape=[outs[0], outs[1], shape(input_we...]
    slice x4 -> x0, local copies, waits for them, and re-layouts: 5.34 us -> none  [the longest x1 1.7 us: fused(): vec[:, 5]]
    another operation x9 -> x0, local copies, waits for them, and re-layouts: 5.31 us -> none  [the longest x7 4.56 us: fused(): jnp.stack([output_bias, down_bias, first_gain, first_shift, second_gain,...]
    unnamed x7 -> x0, local copies, waits for them, and re-layouts: 5.21 us -> none
where the time goes in v3:
time: 121 us; the launch traced here: 120 us
  Pallas kernels  120 us (99%)
    pallas_call x1, Pallas kernels, fused(): pl.pallas_call(functools.partial(layer_kernel, geo, lane, plan), out_shap...  114 us
    pallas_call x1, Pallas kernels, fused(): pl.pallas_call(finish_kernel, out_shape=[outs[0], outs[1], shape(input_we...  5.39 us

profile of v3, /device:TPU:0, one launch (start us, length us, event | category | flops | bytes accessed | tf_op | source)
XLA Modules:
  0.0 120.5 jit_solution(9659466341010658381)
XLA Ops:
  0.7 114.3 %shard_map.237 = (f32[2,512,512]{2,1,0:T(8,128)}, f32[2,512,512]{2,1,0:T(8,128)}, f32[4,16,384]{2,1,0:T(8,128)}, f32[16,512]{1,0:T(8,128)}, f32[16,2048]{1,0:T(8...) custom-call(bf16[2,512,512]{2,1,0:T(8,128)(2,1)} %refs_0_.1, bf16[2,512,512]{2,1,0:T(8,128)(2,1)} %refs_1_.1, ...), custom_call_target="tpu_custom_call" | custom-call | tf_op jit(solution)/shard_map/pallas_call | solution.py:1271
  114.9 5.4 %shard_map.238 = (f32[2,512,512]{2,1,0:T(8,128)}, f32[2,512,512]{2,1,0:T(8,128)}, f32[16,1536]{1,0:T(8,128)}, f32[16,512]{1,0:T(8,128)}, f32[16]{0:T(128)}, /*in...) custom-call(f32[2,512,512]{2,1,0:T(8,128)} %get-tuple-element.20.res, ...), custom_call_target="tpu_custom_call" | custom-call | tf_op jit(solution)/shard_map/pallas_call | solution.py:1278

commit v4 on v3

--- a/solution.py
+++ b/solution.py
@@ -30,7 +30,7 @@
     def device(self, z, x, y, c):
         return (z * self.X + x, y * 2 + c)
 
-    def barrier(self):
+    def greet(self):
         z, x, y, c = self.me()
         peers = [self.device(z, x, y, 1 - c)]
         peers += [self.device((z + i) % self.Z, (x + j) % self.X, (y + k) % self.Y, c)
@@ -38,7 +38,9 @@
         semaphore = pltpu.get_barrier_semaphore()
         for peer in peers:
             pl.semaphore_signal(semaphore, inc=1, device_id=peer, device_id_type=MESH)
-        pl.semaphore_wait(semaphore, len(peers))
+
+    def barrier(self):
+        pl.semaphore_wait(pltpu.get_barrier_semaphore(), self.Z * self.X * self.Y)
 
 
 class Lane:
@@ -59,9 +61,9 @@
 
 
 class Gather:
-    def __init__(self, geo, lane):
-        self.geo, self.lane = geo, lane
-        self.zs = lane.take(geo.Z - 1)
+    def __init__(self, geo, lane, orders):
+        self.geo, self.lane, self.orders = geo, lane, orders
+        self.zs = lane.take()
         self.second = lane.take(max(geo.X, geo.Y) - 1)
         self.third = lane.take(max(geo.X, geo.Y) - 1)
         self.core = lane.take()
@@ -69,16 +71,17 @@
     def bind(self, own, full):
         self.own, self.full = own, full
 
-    def z_copies(self, incoming):
+    def z_copies(self):
         g = self.geo
         z, x, y, c = g.me()
         for k in range(1, g.Z):
-            if incoming:
-                slot = self.full.at[(z + g.Z - k) % g.Z, x, y, c]
-                yield remote(self.lane, self.zs + k - 1, slot, slot, g.device((z + k) % g.Z, x, y, c))
-            else:
-                yield remote(self.lane, self.zs + k - 1, self.own, self.full.at[z, x, y, c],
-                             g.device((z + k) % g.Z, x, y, c))
+            yield remote(self.lane, self.zs, self.own, self.full.at[z, x, y, c], g.device((z + k) % g.Z, x, y, c))
+
+    def z_whole(self):
+        g = self.geo
+        z, x, y, c = g.me()
+        slots = self.full.at[pl.ds(0, g.Z - 1), x, y, c]
+        return remote(self.lane, self.zs, slots, slots, g.device((z + 1) % g.Z, x, y, c))
 
     def axis_copies(self, phase, order, incoming):
         g = self.geo
@@ -99,21 +102,23 @@
 
     def both(self, action):
         c = self.geo.me()[3]
-        for order in range(2):
-            @pl.when(c == order)
+        if self.orders[0] == self.orders[1]:
+            action(self.orders[0])
+            return
+        for core in range(2):
+            @pl.when(c == core)
             def _():
-                action(order)
+                action(self.orders[core])
 
     def step(self, n):
         g = self.geo
         z, x, y, c = g.me()
         if n == 0:
-            for copy in self.z_copies(False):
+            for copy in self.z_copies():
                 copy.start()
             self.full[z, x, y, c] = self.own[...]
         elif n == 1:
-            for copy in self.z_copies(True):
-                copy.wait_recv()
+            self.z_whole().wait_recv()
             self.both(lambda order: [copy.start() for copy in self.axis_copies(2, order, False)])
         elif n == 2:
             def go(order):
@@ -136,8 +141,7 @@
     def drain(self):
         g = self.geo
         z, x, y, c = g.me()
-        for copy in self.z_copies(False):
-            copy.wait_send()
+        self.z_whole().wait_send()
 
         def go(order):
             for phase in (2, 3):
@@ -149,12 +153,12 @@
 
 
 class Scatter:
-    def __init__(self, geo, lane):
-        self.geo, self.lane = geo, lane
+    def __init__(self, geo, lane, orders):
+        self.geo, self.lane, self.orders = geo, lane, orders
         self.core = lane.take()
         self.first = lane.take(max(geo.X, geo.Y) - 1)
         self.second = lane.take(max(geo.X, geo.Y) - 1)
-        self.zs = lane.take(geo.Z - 1)
+        self.zs = lane.take()
 
     @staticmethod
     def scratch(geo, rows, width):
@@ -173,10 +177,13 @@
 
     def both(self, action):
         c = self.geo.me()[3]
-        for order in range(2):
-            @pl.when(c == order)
+        if self.orders[0] == self.orders[1]:
+            action(self.orders[0])
+            return
+        for core in range(2):
+            @pl.when(c == core)
             def _():
-                action(order)
+                action(self.orders[core])
 
     def core_copy(self):
         z, x, y, c = self.geo.me()
@@ -206,8 +213,12 @@
         z, x, y, c = g.me()
         for k in range(1, g.Z):
             far = (z + k) % g.Z
-            yield remote(self.lane, self.zs + k - 1, self.part.at[far, x, y, c], self.rz.at[k - 1],
-                         g.device(far, x, y, c))
+            yield remote(self.lane, self.zs, self.part.at[far, x, y, c], self.rz.at[k - 1], g.device(far, x, y, c))
+
+    def z_whole(self):
+        g = self.geo
+        z, x, y, c = g.me()
+        return remote(self.lane, self.zs, self.rz, self.rz, g.device((z + 1) % g.Z, x, y, c))
 
     def step(self, n):
         g = self.geo
@@ -266,8 +277,8 @@
                 copy.start()
         else:
             total = wide(self.part[z, x, y, c])
-            for k, copy in enumerate(self.z_copies()):
-                copy.wait_recv()
+            self.z_whole().wait_recv()
+            for k in range(g.Z - 1):
                 total += wide(self.rz[k])
             self.out[...] = total
 
@@ -279,8 +290,7 @@
                 for copy in self.axis_copies(phase, order):
                     copy.wait_send()
         self.both(go)
-        for copy in self.z_copies():
-            copy.wait_send()
+        self.z_whole().wait_send()
 
 
 epsilon = 1e-05
@@ -671,6 +681,45 @@
                     copy.wait_send()
 
 
+class GatherPlane(Gather):
+    def __init__(self, geo, lane):
+        self.geo, self.lane = geo, lane
+        self.far = [(j, k) for j in range(geo.X) for k in range(geo.Y)][1:]
+        self.zs, self.plane, self.core = lane.take(), lane.take(len(self.far)), lane.take()
+
+    def plane_copies(self, incoming):
+        g = self.geo
+        z, x, y, c = g.me()
+        for n, (j, k) in enumerate(self.far):
+            slot = self.full.at[:, (x + g.X - j) % g.X, (y + g.Y - k) % g.Y, c] if incoming else self.full.at[:, x, y, c]
+            yield remote(self.lane, self.plane + n, slot, slot, g.device(z, (x + j) % g.X, (y + k) % g.Y, c))
+
+    def core_copy(self, own):
+        z, x, y, c = self.geo.me()
+        slot = self.full.at[:, :, :, c if own else 1 - c]
+        return remote(self.lane, self.core, slot, slot, self.geo.device(z, x, y, 1 - c))
+
+    def step(self, n):
+        if n == 0:
+            super().step(0)
+        elif n == 1:
+            self.z_whole().wait_recv()
+            for copy in self.plane_copies(False):
+                copy.start()
+        elif n == 2:
+            for copy in self.plane_copies(True):
+                copy.wait_recv()
+            self.core_copy(True).start()
+        else:
+            self.core_copy(False).wait_recv()
+
+    def drain(self):
+        self.z_whole().wait_send()
+        for copy in self.plane_copies(False):
+            copy.wait_send()
+        self.core_copy(True).wait_send()
+
+
 class PairStates:
     def __init__(self, states, p):
         self.states, self.p = states, p
@@ -684,7 +733,7 @@
         self.geo, self.lane = geo, lane
         self.far = [(i, j, k) for i in range(geo.Z) for j in range(geo.X) for k in range(geo.Y)][1:]
         self.core = lane.take()
-        self.first = lane.take(len(self.far))
+        self.first = lane.take()
 
     @staticmethod
     def scratch(geo, rows, width):
@@ -704,7 +753,11 @@
         z, x, y, c = g.me()
         for n, (i, j, k) in enumerate(self.far):
             to = ((z + i) % g.Z, (x + j) % g.X, (y + k) % g.Y, c)
-            yield remote(self.lane, self.first + n, self.part.at[to], self.rz.at[n], g.device(*to))
+            yield remote(self.lane, self.first, self.part.at[to], self.rz.at[n], g.device(*to))
+
+    def whole(self):
+        z, x, y, c = self.geo.me()
+        return remote(self.lane, self.first, self.rz, self.rz, self.geo.device((z + 1) % self.geo.Z, x, y, c))
 
     def step(self, n):
         g = self.geo
@@ -723,84 +776,80 @@
                 copy.start()
         else:
             total = self.part[z, x, y, c].astype(F32)
-            for n, copy in enumerate(self.copies()):
-                copy.wait_recv()
+            self.whole().wait_recv()
+            for n in range(len(self.far)):
                 total += self.rz[n].astype(F32)
             self.out[...] = total
 
     def drain(self):
         self.core_copy().wait_send()
-        for copy in self.copies():
-            copy.wait_send()
-
-
-DIRECT = ("rI3", "rV",)
+        self.whole().wait_send()
+
+
+DIRECT = ("rG", "rV1",)
+PLANE = ()
+ORDERS = {"F0": (1, 1), "rF3": (1, 1), "rF1": (1, 1), "rO": (1, 1), "rV0": (1, 1)}
 PLAN = {
     "start": (("S", 0), ("I0", 0), ("I1", 0), ("I2", 0), ("I3", 0),),
-    "first": (("O", 0), ("F0", 0), ("F1", 0), ("S", 1), ("I0", 1), ("I1", 1), ("S", 2), ("I2", 1), ("I0", 2),
-        ("I3", 1), ("I1", 2), ("S", 3), ("O", 1), ("I2", 2), ("S", 4),),
-    "norm1": (("I0", 3), ("I3", 2),),
-    "proj0.pre": (("F0", 1), ("I1", 3), ("O", 2), ("I0", 4),),
-    "proj0.1": (("f0", 0), ("I2", 3), ("F1", 1), ("I3", 3),),
-    "proj1.pre": (("I1", 4),),
-    "proj1.1": (("f1", 0), ("f0", 1),),
-    "proj2.pre": (("I2", 4),),
-    "proj2.0": (("I3", 4), ("O", 3),),
-    "proj2.1": (("f2", 0), ("f1", 1),),
-    "proj3.1": (("f3", 0), ("f2", 1), ("O", 4), ("F2", 0),),
-    "att0.pre": (("f0", 2), ("f3", 1), ("f0", 3),),
-    "att0.0": (("f1", 2), ("F0", 2),),
-    "att0.1": (("F3", 0),),
-    "att1.pre": (("f2", 2), ("f1", 3),),
-    "att1.1": (("f2", 3), ("F2", 1), ("f3", 2),),
-    "att2.0": (("F1", 2),),
-    "att2.1": (("f3", 3),),
-    "att3.0": (("F0", 3),),
-    "att3.1": (("F3", 1),),
-    "mid.0": (("F2", 2),),
-    "feed0.pre": (("F0", 4),),
-    "feed0.0": (("F1", 3),),
-    "feed0.1": (("F3", 2),),
-    "feed0.end": (("rF0", 0), ("F1", 4),),
-    "feed1.0": (("F2", 3),),
-    "feed1.1": (("rF0", 1), ("F3", 3),),
-    "feed2.pre": (("F2", 4),),
-    "feed2.0": (("F3", 4),),
-    "feed2.end": (("rF2", 0), ("rF0", 2),),
-    "feed3.1": (("rF2", 1),),
-    "feed3.end": (("rF0", 3),),
-    "out.end": (("rO", 0),),
-    "st0": (("b0", 0), ("rF2", 2),),
-    "st1": (("b1", 0), ("rF1", 0),),
-    "st2": (("b2", 0), ("rF0", 4), ("b0", 1), ("rO", 1),),
-    "st3": (("b3", 0), ("b1", 1),),
-    "pb0.pre": (("rF3", 0), ("rF2", 3), ("rF1", 1), ("b2", 1), ("b3", 1), ("b0", 2), ("rF3", 1), ("b0", 3),),
-    "pb0.m": (("rF2", 4), ("b1", 2), ("rO", 2),),
-    "pb1.m": (("b1", 3),),
-    "pb1": (("rI0", 0), ("rF1", 2),),
-    "pb2.m": (("b2", 2), ("rI0", 1),),
-    "pb3.m": (("b2", 3),),
-    "pb3": (("rI1", 0),),
-    "pb4.m": (("b3", 2), ("rI0", 2), ("rI1", 1), ("rF1", 3),),
-    "pb5.m": (("b3", 3), ("rF3", 2),),
-    "pb5": (("rI2", 0), ("rI1", 2),),
-    "pb6": (("rF3", 3),),
-    "pb7.m": (("rI2", 1), ("rI1", 3), ("rO", 3),),
-    "pb7": (("rI3", 0), ("rI0", 3),),
-    "nb1": (("rI3", 1), ("rI2", 2), ("rI1", 4), ("rF3", 4),),
-    "fb1": (("rV", 0), ("rF1", 4), ("rO", 4),),
-    "end": (("rI0", 4), ("rV", 1), ("rI2", 3), ("rI3", 2), ("rV", 2), ("rI2", 4),),
+    "first": (("O", 0), ("F0", 0), ("F1", 0), ("F2", 0), ("S", 1), ("I0", 1), ("I1", 1), ("S", 2), ("I2", 1),
+        ("I0", 2), ("I3", 1), ("I1", 2), ("S", 3), ("O", 1), ("I2", 2), ("S", 4),),
+    "proj.pre0": (("I0", 3), ("I3", 2), ("F0", 1), ("I1", 3), ("O", 2), ("I0", 4),),
+    "proj0": (("f0", 0), ("I2", 3), ("F1", 1), ("I3", 3),),
+    "proj.pre1": (("I1", 4),),
+    "proj1": (("f1", 0), ("f0", 1),),
+    "proj.pre2": (("I2", 4),),
+    "proj2": (("f2", 0), ("f1", 1), ("O", 3), ("F0", 2), ("F2", 1), ("F3", 0),),
+    "proj.pre3": (("I3", 4),),
+    "proj3": (("f3", 0), ("f2", 1),),
+    "block1": (("f3", 1), ("f1", 2),),
+    "block2": (("F3", 1),),
+    "att.pre0": (("F1", 2), ("f0", 2), ("f2", 2), ("F0", 3), ("f0", 3),),
+    "att.pre1": (("f1", 3), ("F2", 2), ("f3", 2),),
+    "att1": (("O", 4),),
+    "att.pre2": (("f2", 3),),
+    "att2": (("F0", 4), ("F3", 2),),
+    "att.pre3": (("f3", 3),),
+    "mid": (("F1", 3),),
+    "feed0": (("F2", 3),),
+    "feed.pre1": (("F1", 4),),
+    "feed1": (("rF1", 0), ("F2", 4), ("F3", 3),),
+    "feed2": (("rF2", 0), ("rF1", 1), ("F3", 4),),
+    "feed3": (("rF3", 0), ("rF2", 1),),
+    "out": (("rF3", 1), ("rF1", 2), ("rO", 0),),
+    "st0": (("b0", 0),),
+    "st1": (("b1", 0),),
+    "st2": (("b2", 0),),
+    "st3": (("b3", 0), ("rF2", 2), ("rO", 1), ("b0", 1),),
+    "q0": (("b1", 1), ("b2", 1), ("b3", 1), ("rF0", 0),),
+    "q1": (("rF1", 3),),
+    "q2": (("b0", 2), ("rF3", 2),),
+    "q3": (("b1", 2),),
+    "q.end": (("rQ", 0),),
+    "k.pre0": (("b0", 3),),
+    "k0": (("b2", 2), ("b1", 3), ("rF0", 1), ("b3", 2), ("rQ", 1), ("rF1", 4), ("rO", 2),),
+    "k1": (("b2", 3), ("b3", 3), ("rF3", 3),),
+    "k3": (("rF2", 3), ("rF0", 2),),
+    "k.end": (("rK", 0), ("rQ", 2),),
+    "v0": (("rV0", 0), ("rK", 1), ("rF0", 3), ("rO", 3),),
+    "v1": (("rV1", 0), ("rV0", 1), ("rQ", 3), ("rF2", 4),),
+    "nb0": (("rK", 2),),
+    "nb1": (("rV1", 1), ("rF0", 4),),
+    "fb1": (("rG", 0), ("rV0", 2), ("rO", 4),),
+    "end0": (("rF3", 4),),
+    "end": (("rK", 3), ("rQ", 4), ("rG", 1), ("rV0", 3), ("rV1", 2), ("rK", 4), ("rG", 2), ("rV0", 4),),
 }
 
 
 def layer_kernel(geo, lane, plan, *refs):
-    (tokens_hbm, cot_hbm, feat, out_bias_in, down_bias_in, first_gain_in, first_shift_in, second_gain_in,
-     second_shift_in, up_bias_in, wi_in, wo_own, wu_in, wd_in,
-     result_hbm, tokens_grad_hbm, inp_out, out_out, up_out, down_out, vec_out,
-     tokens, cot, result, tokens_grad, small_own, small, wi_own, wi, wo_all, wf_own, wf,
+    (tokens_hbm, cot_hbm, feat_hbm, out_bias_hbm, down_bias_hbm, first_gain_hbm, first_shift_hbm, second_gain_hbm,
+     second_shift_hbm, up_bias_hbm, wi_hbm, wo_hbm, wu_hbm, wd_hbm,
+     result_hbm, tokens_grad_hbm, inp_hbm, out_hbm, up_hbm, down_hbm, vec_hbm,
+     feat, out_bias_in, down_bias_in, first_gain_in, first_shift_in, second_gain_in, second_shift_in, up_bias_in,
+     wi_in, wu_in, wd_in, inp_out, out_out, up_out, down_out, vec_out,
+     tokens, cot, result, tokens_grad, small_own, small, wi_own, wi, wo_own, wo_all, wf_own, wf,
      normed, normed_t, mixed, pq, pk, den, attended, middle, n2_t,
-     act, hg, vecs, grads, fa, ft, perm, part_i, part_o, part_f, part_v, up_parts, vec_sum) = refs[:54]
-    rest = list(refs[54:])
+     act, hg, vecs, grads, fa, ft, perm, part_q, part_k, part_v, part_o, part_f, part_g, up_parts, vec_sum) = refs[:73]
+    rest = list(refs[73:])
     fwd, bwd, tasks = plan
     take = lambda n: [rest.pop(0) for _ in range(n)]
     fwd.bind(take(7))
@@ -812,10 +861,14 @@
     tasks["S"].bind(small_own, small)
     tasks["O"].bind(wo_own, wo_all)
     tasks["rO"].bind(part_o, out_out, scatter_buffers["rO"])
-    tasks["rV"].bind(part_v, vec_sum, scatter_buffers["rV"])
+    tasks["rG"].bind(part_g, vec_sum, scatter_buffers["rG"])
+    wide = tokens.shape[-1]
+    tasks["rQ"].bind(part_q, inp_out.at[:, pl.ds(0, wide)], scatter_buffers["rQ"])
+    tasks["rK"].bind(part_k, inp_out.at[:, pl.ds(wide, wide)], scatter_buffers["rK"])
+    for n in range(2):
+        tasks[f"rV{n}"].bind(part_v.at[n], inp_out.at[:, pl.ds(2 * wide + 256 * n, 256)], scatter_buffers[f"rV{n}"])
     for p in range(PAIRS):
         tasks[f"I{p}"].bind(wi_own.at[p], wi.at[p])
-        tasks[f"rI{p}"].bind(part_i.at[p], inp_out.at[p], scatter_buffers[f"rI{p}"])
     for t in range(wf.shape[0]):
         tasks[f"F{t}"].bind(wf_own.at[t], wf.at[t])
         tasks[f"rF{t}"].bind(part_f.at[t], up_parts.at[t], scatter_buffers[f"rF{t}"])
@@ -834,6 +887,15 @@
             return 0
         lax.fori_loop(0, n, step, 0)
 
+    def pairs(body, before, after):
+        def step(p):
+            if before:
+                pump_at(p, [before + f"{n}" for n in range(PAIRS)])
+            body(p, 0)
+            body(p, 1)
+            pump_at(p, [after + f"{n}" for n in range(PAIRS)])
+        loop(PAIRS, step)
+
     def pump(point):
         for name, n in PLAN.get(point, ()):
             tasks[name].step(n)
@@ -848,8 +910,18 @@
     def local(i, src, dst):
         return pltpu.make_async_copy(src, dst, local_sem.at[i])
 
+    entry = ((feat_hbm, feat), (out_bias_hbm, out_bias_in), (down_bias_hbm, down_bias_in),
+             (first_gain_hbm, first_gain_in), (first_shift_hbm, first_shift_in), (second_gain_hbm, second_gain_in),
+             (second_shift_hbm, second_shift_in), (up_bias_hbm, up_bias_in), (wi_hbm, wi_in), (wo_hbm, wo_own),
+             (wu_hbm, wu_in), (wd_hbm, wd_in))
+    entry = [local(9 + i, a, b) for i, (a, b) in enumerate(entry)]
+    for copy in entry[1:9] + entry[:1] + entry[9:]:
+        copy.start()
     local(0, tokens_hbm, tokens).start()
     local(1, cot_hbm, cot).start()
+    geo.greet()
+    for copy in entry[1:9]:
+        copy.wait()
     vec_sum[...] = jnp.zeros((16, 128), F32)
     for v, ref in enumerate((out_bias_in, down_bias_in, first_gain_in, first_shift_in, second_gain_in,
                              second_shift_in)):
@@ -862,6 +934,8 @@
         wi_own[p] = jnp.concatenate([wi_in[:, k * D + p * 128: k * D + (p + 1) * 128] for k in range(3)], axis=1)
     geo.barrier()
     pump("start")
+    for copy in entry[:1] + entry[9:]:
+        copy.wait()
     source = lax.broadcasted_iota(jnp.int32, (512, 1), 0)
     target = (source % 64) // 16 * 128 + source // 64 * 16 + source % 16
     perm[...] = jnp.where(lax.broadcasted_iota(jnp.int32, (512, 512), 1) == target, 1.0, 0.0).astype(BF)
@@ -917,9 +991,7 @@
         ones = jnp.ones(v.shape, BF)
         return (jnp.concatenate([v * m0, ones * m0], axis=1), jnp.concatenate([v * m1, ones * m1], axis=1))
 
-    def project(i):
-        p, s = i // 2, i % 2
-        pump_at(i, [f"proj{n // 2}.pre" if n % 2 == 0 else "" for n in range(2 * PAIRS)])
+    def project(p, s):
         mixed[s, p] = dot(normed[s], flat(wi[p])).astype(BF)
         for part, target in ((0, pq), (1, pk)):
             rows = mixed[s, p, :, part * 128:(part + 1) * 128]
@@ -933,8 +1005,7 @@
         r0 = dot(lhs, pk[s, 2 * p])
         r1 = dot(lhs, pk[s, 2 * p + 1])
         fwd.own[p, s] = jnp.concatenate([r0[:64], r1[64:128], r0[128:], r1[128:]], axis=0).astype(BF)
-        pump_at(i, [f"proj{n // 2}.{n % 2}" for n in range(2 * PAIRS)])
-    loop(2 * PAIRS, project)
+    pairs(project, "proj.pre", "proj")
 
     def state_cols(total, p, s, h, copies):
         state = total[p, s, h * 64:(h + 1) * 64]
@@ -950,11 +1021,8 @@
     lower = tri_r >= tri_c
     upper = tri_r <= tri_c
 
-    def attend_pair(i):
-        p, s = i // 2, i % 2
-        pump_at(i, [f"att{n // 2}.pre" if n % 2 == 0 else "" for n in range(2 * PAIRS)])
+    def attend_block(p, s):
         v0, v1 = vx(s, p)
-        states = jnp.concatenate([state_cols(fwd.total, p, s, h, True) for h in range(2)], axis=1)
         lanes = pl.ds(pl.multiple_of(p * 128, 128), 128)
         for b in range(2):
             rows = slice(b * HALF, (b + 1) * HALF)
@@ -966,13 +1034,18 @@
                 scores.append(jnp.where(lower, dot_nt(q, pk[s, 2 * p + h, rows]), 0.0).astype(BF))
             rhs = jnp.concatenate([v0[:(b + 1) * HALF], v1[:(b + 1) * HALF]], axis=0)
             ext = dot(jnp.concatenate(scores, axis=1), rhs)
-            ext += dot_nt(jnp.concatenate([pq[s, 2 * p, rows], pq[s, 2 * p + 1, rows]], axis=1), states)
-            n_, d_ = ext[:, :128], ext[:, 128:]
-            inv = 1.0 / d_
-            den[s, rows, lanes] = inv
-            attended[s, rows, lanes] = (n_ * inv).astype(BF)
-        pump_at(i, [f"att{n // 2}.{n % 2}" for n in range(2 * PAIRS)])
-    loop(2 * PAIRS, attend_pair)
+            result[s, rows, lanes] = ext[:, :128]
+            den[s, rows, lanes] = ext[:, 128:]
+    pairs(attend_block, None, "block")
+
+    def attend_earlier(p, s):
+        lanes = pl.ds(pl.multiple_of(p * 128, 128), 128)
+        states = jnp.concatenate([state_cols(fwd.total, p, s, h, True) for h in range(2)], axis=1)
+        ext = dot_nt(jnp.concatenate([pq[s, 2 * p], pq[s, 2 * p + 1]], axis=1), states)
+        inv = 1.0 / (ext[:, 128:] + den[s, :, lanes])
+        den[s, :, lanes] = inv
+        attended[s, :, lanes] = ((ext[:, :128] + result[s, :, lanes]) * inv).astype(BF)
+    pairs(attend_earlier, "att.pre", "att")
     pump("mid.pre")
     local(1, cot_hbm, cot).wait()
 
@@ -988,14 +1061,15 @@
         n2_t[s] = low.T
         result[s] = value + down_bias()
         tokens_grad[s] = jnp.zeros((L, D), F32)
-        pump_at(s, ["mid.0", "mid.1"])
-    loop(2, to_middle)
+    to_middle(0)
+    to_middle(1)
+    pump("mid")
     grads[...] = jnp.zeros(grads.shape, F32)
 
     k0 = math.sqrt(2.0 / math.pi)
 
     def feed_tile(t):
-        pump_at(t, [f"feed{n}.pre" for n in range(TILES)])
+        pump_at(t, [f"feed.pre{n}" for n in range(TILES)])
         bias = vecs[pl.ds(6 + t, 1)]
         wut = lambda: flat(wf[t, :, :, :, :, :, :D])
         wdt = lambda: flat(wf[t, :, :, :, :, :, D:])
@@ -1016,13 +1090,13 @@
                 hg[s, rows] = low
                 result[s, rows] += dot(a, wdt())
                 tokens_grad[s, rows] += dot_nt(low, wut())
-            pump_at(2 * t + s, [f"feed{n // 2}.{n % 2}" for n in range(2 * TILES)])
-        loop(2, seq)
+        seq(0)
+        seq(1)
         dwd = dot(act[0].T, cot[0]) + dot(act[1].T, cot[1])
         part_f[t, :, :, :, :, :, D:] = dwd.astype(BF).reshape(lead + (-1, D))
         dwu = dot(n2_t[0], hg[0]) + dot(n2_t[1], hg[1])
         part_f[t, :, :, :, :, :, :D] = dwu.astype(BF).reshape(lead + (-1, 512))
-        pump_at(t, [f"feed{n}.end" for n in range(TILES)])
+        pump_at(t, [f"feed{n}" for n in range(TILES)])
     loop(TILES, feed_tile)
     local(2, result, result_hbm).start()
 
@@ -1067,11 +1141,11 @@
             dhi = dgr.astype(BF).astype(F32)
             dlo = dgr - dhi
             hg[s, :, cols] = (dhi * hi_lane + dlo * lo_lane).astype(BF)
-        pump_at(s, ["out.0", "out.1"])
-    loop(2, out_back)
+    out_back(0)
+    out_back(1)
     dwo = dot(attended[0].T, act[0]) + dot(attended[1].T, act[1])
     part_o[...] = dwo.astype(BF).reshape(lead + (-1, D))
-    pump("out.end")
+    pump("out")
 
     def ngx(s, p):
         lanes = pl.ds(pl.multiple_of(p * 128, 128), 128)
@@ -1083,66 +1157,87 @@
             r0 = dot(lhs, pq[s, 2 * p])
             r1 = dot(lhs, pq[s, 2 * p + 1])
             bwd.own[p, s] = jnp.concatenate([r0[:64], r1[64:128], r0[128:144], r1[192:208]], axis=0).astype(BF)
-        loop(2, seq)
+        seq(0)
+        seq(1)
         pump_at(p, [f"st{n}" for n in range(PAIRS)])
     loop(PAIRS, state_back)
 
-    def pair_back(i):
-        p, s = i // 2, i % 2
-        pump_at(i, [f"pb{n}.pre" for n in range(2 * PAIRS)])
-        v0, v1 = vx(s, p)
+    lo, hi = slice(0, HALF), slice(HALF, L)
+
+    def masked(keep, value):
+        return jnp.where(keep, value, 0.0).astype(BF)
+
+    def through_features(s, p, part, logs):
+        through = dot_nt(jnp.concatenate(logs, axis=1), ft[...])
+        cols = slice(part * 128, (part + 1) * 128)
+        rows = mixed[s, p, :, cols].astype(F32)
+        mixed[s, p, :, cols] = (SCALE * through[:, :128] - SCALE * SCALE * through[:, 128:] * rows).astype(BF)
+
+    def input_part(part, chosen):
+        cols = slice(part * 128, (part + 1) * 128)
+        total = sum(dot(normed_t[s], jnp.concatenate([mixed[s, p, :, cols] for p in chosen], axis=1))
+                    for s in range(2))
+        return total.astype(BF).reshape(lead + (-1, 128 * len(chosen)))
+
+    def query_back(p, s):
         x = ngx(s, p)
-        ng = x[:, :128]
-        logs_q, logs_k, att = [], [], []
-        for h, v in ((0, v0), (1, v1)):
+        logs = []
+        for h, v in enumerate(vx(s, p)):
             q, k = pq[s, 2 * p + h], pk[s, 2 * p + h]
             sx = state_cols(fwd.total, p, s, h, True)
-            sg = state_cols(bwd.total, p, s, h, False)
-            lo, hi = slice(0, HALF), slice(HALF, L)
-
-            def masked(keep, value):
-                return jnp.where(keep, value, 0.0).astype(BF)
             g00 = masked(lower, dot_nt(x[lo], v[lo]))
             g10 = dot_nt(x[hi], v[lo]).astype(BF)
             g11 = masked(lower, dot_nt(x[hi], v[hi]))
             qg0 = dot(jnp.concatenate([g00, x[lo]], axis=1), jnp.concatenate([k[lo], sx], axis=0))
             qg1 = dot(jnp.concatenate([g10, g11, x[hi]], axis=1), jnp.concatenate([k, sx], axis=0))
-            logs_q.append((jnp.concatenate([qg0, qg1], axis=0) * q.astype(F32)).astype(BF))
+            logs.append((jnp.concatenate([qg0, qg1], axis=0) * q.astype(F32)).astype(BF))
+        through_features(s, p, 0, logs)
+    pairs(query_back, None, "q")
+    part_q[...] = input_part(0, range(PAIRS))
+    pump("q.end")
+
+    def key_back(p, s):
+        x = ngx(s, p)
+        logs = []
+        for h, v in enumerate(vx(s, p)):
+            q, k = pq[s, 2 * p + h], pk[s, 2 * p + h]
+            sg = state_cols(bwd.total, p, s, h, False)
             t00 = masked(upper, dot_nt(v[lo], x[lo]))
             t01 = dot_nt(v[lo], x[hi]).astype(BF)
             t11 = masked(upper, dot_nt(v[hi], x[hi]))
             kg0 = dot(jnp.concatenate([t00, t01, v[lo]], axis=1), jnp.concatenate([q, sg], axis=0))
             kg1 = dot(jnp.concatenate([t11, v[hi]], axis=1), jnp.concatenate([q[hi], sg], axis=0))
-            logs_k.append((jnp.concatenate([kg0, kg1], axis=0) * k.astype(F32)).astype(BF))
-            a00 = masked(upper, dot_nt(k[lo], q[lo]))
-            a01 = dot_nt(k[lo], q[hi]).astype(BF)
-            a11 = masked(upper, dot_nt(k[hi], q[hi]))
-            att.append((a00, a01, a11))
-        pump_at(i, [f"pb{n}.m" for n in range(2 * PAIRS)])
+            logs.append((jnp.concatenate([kg0, kg1], axis=0) * k.astype(F32)).astype(BF))
+        through_features(s, p, 1, logs)
+    pairs(key_back, "k.pre", "k")
+    part_k[...] = input_part(1, range(PAIRS))
+    pump("k.end")
+
+    def value_back(p, s):
+        lanes = pl.ds(pl.multiple_of(p * 128, 128), 128)
+        ng = n2[s, :, lanes]
+        parts = []
+        for h in range(2):
+            q, k = pq[s, 2 * p + h], pk[s, 2 * p + h]
+            parts.append((masked(upper, dot_nt(k[lo], q[lo])), dot_nt(k[lo], q[hi]).astype(BF),
+                          masked(upper, dot_nt(k[hi], q[hi]))))
         n0, n1 = ng * m0, ng * m1
-        vg0 = dot(jnp.concatenate([att[0][0], att[0][1], att[1][0], att[1][1]], axis=1),
+        vg0 = dot(jnp.concatenate([parts[0][0], parts[0][1], parts[1][0], parts[1][1]], axis=1),
                   jnp.concatenate([n0, n1], axis=0))
-        vg1 = dot(jnp.concatenate([att[0][2], att[1][2]], axis=1), jnp.concatenate([n0[HALF:], n1[HALF:]], axis=0))
+        vg1 = dot(jnp.concatenate([parts[0][2], parts[1][2]], axis=1), jnp.concatenate([n0[hi], n1[hi]], axis=0))
         zeros = jnp.zeros((DH, M), BF)
         sgt = jnp.concatenate([jnp.concatenate([bwd.total[p, s, :64], zeros], axis=0),
                                jnp.concatenate([zeros, bwd.total[p, s, 64:128]], axis=0)], axis=1)
         vg = jnp.concatenate([vg0, vg1], axis=0)
         vg += dot_nt(jnp.concatenate([pk[s, 2 * p], pk[s, 2 * p + 1]], axis=1), sgt)
-        out = []
-        for part, logs in ((0, logs_q), (1, logs_k)):
-            through = dot_nt(jnp.concatenate(logs, axis=1), ft[...])
-            rows = mixed[s, p, :, part * 128:(part + 1) * 128].astype(F32)
-            out.append((SCALE * through[:, :128] - SCALE * SCALE * through[:, 128:] * rows).astype(BF))
-        mg = jnp.concatenate(out + [vg.astype(BF)], axis=1)
-        act[s, :, :384] = mg
-        mixed[s, p] = mg
-
-        @pl.when(s == 1)
-        def _():
-            dwi = dot(normed_t[0], act[0, :, :384]) + dot(normed_t[1], act[1, :, :384])
-            part_i[p] = dwi.astype(BF).reshape(lead + (-1, 384))
-        pump_at(i, [f"pb{n}" for n in range(2 * PAIRS)])
-    loop(2 * PAIRS, pair_back)
+        mixed[s, p, :, 256:] = vg.astype(BF)
+    for n in range(2):
+        def step(i):
+            value_back(2 * n + i, 0)
+            value_back(2 * n + i, 1)
+        loop(2, step)
+        part_v[n] = input_part(2, range(2 * n, 2 * n + 2))
+        pump(f"v{n}")
 
     def normed_back(s):
         for b in range(2):
@@ -1168,9 +1263,11 @@
         tile = grads[:, g * 128:(g + 1) * 128].astype(BF)
         for k in range(8):
             chip, core = (8 * g + k) // 2, k % 2
-            part_v[chip // (geo.X * geo.Y), chip // geo.Y % geo.X, chip % geo.Y, core] = tile
+            part_g[chip // (geo.X * geo.Y), chip // geo.Y % geo.X, chip % geo.Y, core] = tile
     local(3, tokens_grad, tokens_grad_hbm).start()
     pump("fb1")
+    pump("end0")
+    local(5, out_out, out_hbm).start()
     stacked = jnp.concatenate([jnp.concatenate([up_parts[t, :, g * 128:(g + 1) * 128] for t in range(TILES)], axis=1)
                                for g in range(TILES)], axis=0)
     high = stacked.astype(BF)
@@ -1180,50 +1277,75 @@
         up_out[:, g * 512:(g + 1) * 512] = stacked[g * 16:(g + 1) * 16]
     for t in range(TILES):
         down_out[t * 16:(t + 1) * 16] = up_parts[t, :, D:]
+    local(6, up_out, up_hbm).start()
+    local(7, down_out, down_hbm).start()
     late = {name for name, n in PLAN["end"]}
     drains = [fwd, bwd] + [task for name, task in tasks.items() if name not in late and hasattr(task, "drain")]
     for task in drains:
         task.drain()
     pump("end")
     vec_out[...] = pltpu.roll(vec_sum[...], lax.rem(8 - place, 8) * 16, 1)
-    local(2, result, result_hbm).wait()
-    local(3, tokens_grad, tokens_grad_hbm).wait()
+    local(8, vec_out, vec_hbm).start()
+    local(4, inp_out, inp_hbm).start()
+    for i, (a, b) in enumerate(((result, result_hbm), (tokens_grad, tokens_grad_hbm), (inp_out, inp_hbm),
+                                (out_out, out_hbm), (up_out, up_hbm), (down_out, down_hbm), (vec_out, vec_hbm))):
+        local(2 + i, a, b).wait()
     for name in sorted(late):
         if hasattr(tasks[name], "drain"):
             tasks[name].drain()
 
 
-def finish_kernel(result_in, tokens_grad_in, inp, out, up, down, vec, *refs):
-    (result, tokens_grad, inp_out, out_out, out_bias, up_out, up_bias, down_out, down_bias,
-     first_gain, first_shift, second_gain, second_shift, held, in_sems, out_sems) = refs
+def finish_kernel(*refs):
+    ins, outs = refs[:7], refs[7:20]
+    held, (inp, out, up, down, vec), vec_rows = refs[20], refs[21:26], refs[26:33]
+    in_sems, out_sems = refs[33:]
+    waits = []
+
+    def copy(src, dst, sems, i):
+        return pltpu.make_async_copy(src, dst, sems.at[i])
+    small_in = [copy(a, b, in_sems, i) for i, (a, b) in enumerate(zip(ins[2:], (inp, out, up, down, vec)))]
+    for one in small_in[:1] + small_in[4:]:
+        one.start()
     cuts = []
-    for a, b, n in ((result_in, result, 0), (tokens_grad_in, tokens_grad, 1)):
-        for m in range(a.shape[0]):
+    for n in range(2):
+        for m in range(ins[n].shape[0]):
             for k in range(2):
-                rows = pl.ds(k * (a.shape[1] // 2), a.shape[1] // 2)
-                i = len(cuts)
+                rows = pl.ds(k * (ins[n].shape[1] // 2), ins[n].shape[1] // 2)
                 slot = held.at[n, m, rows]
-                cuts.append((pltpu.make_async_copy(a.at[m, rows], slot, in_sems.at[i]),
-                             pltpu.make_async_copy(slot, b.at[m, rows], out_sems.at[i])))
-    for first, _ in cuts:
+                cuts.append((copy(ins[n].at[m, rows], slot, in_sems, 5 + len(cuts)),
+                             copy(slot, outs[n].at[m, rows], out_sems, 11 + len(cuts))))
+    for first, _ in cuts[:4]:
         first.start()
-    D = out.shape[-1]
-    for p in range(PAIRS):
-        for k in range(3):
-            inp_out[:, k * D + p * 128: k * D + (p + 1) * 128] = inp[p, :, k * 128:(k + 1) * 128]
-    out_out[...] = out[...]
-    up_out[...] = up[...]
-    down_out[...] = down[...]
-    n = out_bias.shape[-1]
-    for v, ref in enumerate((out_bias, down_bias, first_gain, first_shift, second_gain, second_shift)):
-        ref[...] = vec[v, :n]
-    for t in range(4):
-        up_bias[pl.ds(t * n, n)] = vec[6 + t, :n]
-    for first, second in cuts:
+    for one in small_in[1:4]:
+        one.start()
+    for first, _ in cuts[4:]:
+        first.start()
+    small_in[0].wait()
+    small_in[4].wait()
+    n = vec_rows[0].shape[-1]
+    for v in range(6):
+        vec_rows[v][...] = vec[v, :n]
+    for t in range(up.shape[-1] // 512):
+        vec_rows[6][pl.ds(t * n, n)] = vec[6 + t, :n]
+    final = {2: inp, 4: vec_rows[0], 8: vec_rows[1], 9: vec_rows[2], 10: vec_rows[3], 11: vec_rows[4],
+             12: vec_rows[5], 6: vec_rows[6]}
+    for i, (place, ref) in enumerate(final.items()):
+        waits.append(copy(ref, outs[place], out_sems, i))
+        waits[-1].start()
+    for first, second in cuts[:4]:
         first.wait()
         second.start()
-    for _, second in cuts:
-        second.wait()
+        waits.append(second)
+    for i, (one, ref, place) in enumerate(zip(small_in[1:4], (out, up, down), (3, 5, 7))):
+        one.wait()
+        waits.append(copy(ref, outs[place], out_sems, 8 + i))
+        waits[-1].start()
+    for first, second in cuts[4:]:
+        first.wait()
+        second.start()
+        waits.append(second)
+    for one in waits:
+        one.wait()
 
 
 def fused(geo, args):
@@ -1235,52 +1357,56 @@
     tiles = FF // 512
     lane = Lane()
     fwd, bwd = States(geo, lane, True), States(geo, lane, False)
-    tasks = {name: Gather(geo, lane) for name in ["S", "O"] + [f"I{p}" for p in range(PAIRS)]
-             + [f"F{t}" for t in range(tiles)]}
-    scatters = {"rO": D, "rV": 128}
-    scatters.update({f"rI{p}": 384 for p in range(PAIRS)})
+    names = ["S", "O"] + [f"I{p}" for p in range(PAIRS)] + [f"F{t}" for t in range(tiles)]
+    tasks = {name: GatherPlane(geo, lane) if name in PLANE else Gather(geo, lane, ORDERS.get(name, (0, 1)))
+             for name in names}
+    scatters = {"rO": D, "rQ": D, "rK": D, "rV0": 256, "rV1": 256, "rG": 128}
     scatters.update({f"rF{t}": 2 * D for t in range(tiles)})
     for name in scatters:
-        tasks[name] = (ScatterDirect if name in DIRECT else Scatter)(geo, lane)
+        tasks[name] = ScatterDirect(geo, lane) if name in DIRECT else Scatter(geo, lane, ORDERS.get(name, (0, 1)))
     for p in range(PAIRS):
         tasks[f"f{p}"], tasks[f"b{p}"] = PairStates(fwd, p), PairStates(bwd, p)
     plan = (fwd, bwd, tasks)
     lead = (geo.Z, geo.X, geo.Y, 2)
     V = pltpu.VMEM
-    scratch = [
+    shape = jax.ShapeDtypeStruct
+    outs = [shape(tokens.shape, F32), shape(tokens.shape, F32), shape(input_weight.shape, F32),
+            shape((rows, D), F32), shape((rows, FF), F32), shape(down_weight.shape, F32), shape((rows, 128), F32)]
+    arrays = (tokens, cotangent, feature_matrix, output_bias, down_bias, first_gain, first_shift, second_gain,
+              second_shift, up_bias, input_weight, output_weight, up_weight, down_weight)
+    scratch = [V(a.shape, BF) for a in arrays[2:11] + arrays[12:]] + [V(o.shape, F32) for o in outs[2:]]
+    scratch += [
         V((2, L, D), BF), V((2, L, D), BF), V((2, L, D), F32), V((2, L, D), F32),
         V((rows, 128), BF), V(lead + (rows, 128), BF), V((PAIRS, rows, 384), BF), V((PAIRS,) + lead + (rows, 384), BF),
-        V(lead + (rows, D), BF), V((tiles, rows, 2 * D), BF), V((tiles,) + lead + (rows, 2 * D), BF),
+        V((rows, D), BF), V(lead + (rows, D), BF), V((tiles, rows, 2 * D), BF),
+        V((tiles,) + lead + (rows, 2 * D), BF),
         V((2, L, D), BF), V((2, D, L), BF), V((2, PAIRS, L, 384), BF), V((2, H, L, M), BF), V((2, H, L, M), BF),
         V((2, L, D), F32), V((2, L, D), BF), V((2, L, D), F32), V((2, D, L), BF),
         V((2, L, 512), BF), V((2, L, 512), BF), V((16, D), F32), V((16, D), F32),
         V((2, M, M), BF), V((M, 2 * M), BF), V((512, 512), BF),
-        V((PAIRS,) + lead + (rows, 384), BF), V(lead + (rows, D), BF), V((tiles,) + lead + (rows, 2 * D), BF),
-        V(lead + (rows, 128), BF), V((tiles, rows, 2 * D), F32), V((rows, 128), F32),
+        V(lead + (rows, D), BF), V(lead + (rows, D), BF), V((2,) + lead + (rows, 256), BF), V(lead + (rows, D), BF),
+        V((tiles,) + lead + (rows, 2 * D), BF), V(lead + (rows, 128), BF), V((tiles, rows, 2 * D), F32), V((rows, 128), F32),
     ]
     scratch += States.scratch(geo) + States.scratch(geo)
     for name, width in scatters.items():
         scratch += type(tasks[name]).scratch(geo, rows, width)
     scratch += [pltpu.SemaphoreType.DMA((lane.count,)), pltpu.SemaphoreType.DMA((lane.count,)),
-                pltpu.SemaphoreType.DMA((4,))]
-    vmem = pl.BlockSpec(memory_space=pltpu.VMEM)
+                pltpu.SemaphoreType.DMA((21,))]
     hbm = pl.BlockSpec(memory_space=pl.ANY)
-    shape = jax.ShapeDtypeStruct
-    outs = [shape(tokens.shape, F32), shape(tokens.shape, F32), shape((PAIRS, rows, 384), F32),
-            shape((rows, D), F32), shape((rows, FF), F32), shape(down_weight.shape, F32), shape((rows, 128), F32)]
     parts = pl.pallas_call(
         functools.partial(layer_kernel, geo, lane, plan),
-        out_shape=outs, in_specs=[hbm] * 2 + [vmem] * 12, out_specs=[hbm] * 2 + [vmem] * 5, scratch_shapes=scratch,
+        out_shape=outs, in_specs=[hbm] * 14, out_specs=[hbm] * 7, scratch_shapes=scratch,
         compiler_params=pltpu.CompilerParams(collective_id=0, has_side_effects=True, vmem_limit_bytes=60 << 20),
-    )(tokens, cotangent, feature_matrix, output_bias, down_bias, first_gain, first_shift, second_gain, second_shift,
-      up_bias, input_weight, output_weight, up_weight, down_weight)
+    )(*arrays)
     vector = shape((rows,), F32)
+    final = [outs[0], outs[1], shape(input_weight.shape, F32), outs[3], vector, outs[4],
+             shape(up_bias.shape, F32), outs[5]] + [vector] * 5
     return pl.pallas_call(
         finish_kernel,
-        out_shape=[outs[0], outs[1], shape(input_weight.shape, F32), outs[3], vector, outs[4],
-                   shape(up_bias.shape, F32), outs[5]] + [vector] * 5,
-        in_specs=[hbm] * 2 + [vmem] * 5, out_specs=[hbm] * 2 + [vmem] * 11,
-        scratch_shapes=[V((2,) + tokens.shape, F32), pltpu.SemaphoreType.DMA((8,)), pltpu.SemaphoreType.DMA((8,))],
+        out_shape=final, in_specs=[hbm] * 7, out_specs=[hbm] * 13,
+        scratch_shapes=[V((2,) + tokens.shape, F32)] + [V(o.shape, F32) for o in outs[2:]]
+        + [V((rows,), F32)] * 6 + [V(up_bias.shape, F32)]
+        + [pltpu.SemaphoreType.DMA((13,)), pltpu.SemaphoreType.DMA((19,))],
         compiler_params=pltpu.CompilerParams(vmem_limit_bytes=60 << 20),
     )(*parts)
 

time: 121 us -> 111 us (0.917)
  Pallas kernels: 120 us -> 110 us
    pallas_call x1, Pallas kernels: 114 us -> 105 us  [fused(): pl.pallas_call(functools.partial(layer_kernel, geo, lane, plan), out_shap...]
where the time goes in v4:
time: 111 us; the launch traced here: 110 us
  Pallas kernels  110 us (99%)
    pallas_call x1, Pallas kernels, fused(): pl.pallas_call(functools.partial(layer_kernel, geo, lane, plan), out_shap...  105 us
    pallas_call x1, Pallas kernels, fused(): pl.pallas_call(finish_kernel, out_shape=final, in_specs=[hbm] * 7, out_sp...  4.27 us

profile of v4, /device:TPU:0, one launch (start us, length us, event | category | flops | bytes accessed | tf_op | source)
XLA Modules:
  0.0 110.4 jit_solution(15478780485956560897)
XLA Ops:
  0.7 105.3 %shard_map.237 = (f32[2,512,512]{2,1,0:T(8,128)}, f32[2,512,512]{2,1,0:T(8,128)}, f32[16,1536]{1,0:T(8,128)}, f32[16,512]{1,0:T(8,128)}, f32[16,2048]{1,0:T(8,12...) custom-call(bf16[2,512,512]{2,1,0:T(8,128)(2,1)} %refs_0_.1, bf16[2,512,512]{2,1,0:T(8,128)(2,1)} %refs_1_.1, ...), custom_call_target="tpu_custom_call" | custom-call | tf_op jit(solution)/shard_map/pallas_call | solution.py:1396
  105.9 4.3 %shard_map.238 = (f32[2,512,512]{2,1,0:T(8,128)}, f32[2,512,512]{2,1,0:T(8,128)}, f32[16,1536]{1,0:T(8,128)}, f32[16,512]{1,0:T(8,128)}, f32[16]{0:T(128)}, /*in...) custom-call(f32[2,512,512]{2,1,0:T(8,128)} %get-tuple-element.20.ref, ...), custom_call_target="tpu_custom_call" | custom-call | tf_op jit(solution)/shard_map/pallas_call | solution.py:1404

commit v5 on v4

--- a/solution.py
+++ b/solution.py
@@ -610,7 +610,7 @@
 SCALE = DH ** (-0.25)
 LOG2E = math.log2(math.e)
 PAIRS = H // 2
-STATE_ROWS = 160
+STATE_ROWS = 144
 
 
 def dot(a, b):
@@ -786,57 +786,57 @@
         self.whole().wait_send()
 
 
-DIRECT = ("rG", "rV1",)
+DIRECT = ("rG",)
 PLANE = ()
-ORDERS = {"F0": (1, 1), "rF3": (1, 1), "rF1": (1, 1), "rO": (1, 1), "rV0": (1, 1)}
+ORDERS = {"I3": (1, 1), "F0": (1, 1), "I1": (1, 1), "rF0": (0, 0), "rF3": (1, 1)}
 PLAN = {
     "start": (("S", 0), ("I0", 0), ("I1", 0), ("I2", 0), ("I3", 0),),
     "first": (("O", 0), ("F0", 0), ("F1", 0), ("F2", 0), ("S", 1), ("I0", 1), ("I1", 1), ("S", 2), ("I2", 1),
-        ("I0", 2), ("I3", 1), ("I1", 2), ("S", 3), ("O", 1), ("I2", 2), ("S", 4),),
-    "proj.pre0": (("I0", 3), ("I3", 2), ("F0", 1), ("I1", 3), ("O", 2), ("I0", 4),),
-    "proj0": (("f0", 0), ("I2", 3), ("F1", 1), ("I3", 3),),
-    "proj.pre1": (("I1", 4),),
-    "proj1": (("f1", 0), ("f0", 1),),
-    "proj.pre2": (("I2", 4),),
-    "proj2": (("f2", 0), ("f1", 1), ("O", 3), ("F0", 2), ("F2", 1), ("F3", 0),),
-    "proj.pre3": (("I3", 4),),
-    "proj3": (("f3", 0), ("f2", 1),),
-    "block1": (("f3", 1), ("f1", 2),),
-    "block2": (("F3", 1),),
-    "att.pre0": (("F1", 2), ("f0", 2), ("f2", 2), ("F0", 3), ("f0", 3),),
-    "att.pre1": (("f1", 3), ("F2", 2), ("f3", 2),),
-    "att1": (("O", 4),),
-    "att.pre2": (("f2", 3),),
-    "att2": (("F0", 4), ("F3", 2),),
+        ("I0", 2), ("I3", 1), ("I1", 2), ("O", 1), ("S", 3), ("I2", 2), ("S", 4),),
+    "norm0": (("I0", 3),),
+    "proj.pre0": (("F0", 1), ("I3", 2), ("I0", 4),),
+    "proj0": (("f0", 0),),
+    "proj.pre1": (("F3", 0), ("I1", 3), ("O", 2), ("F1", 1), ("I2", 3), ("f0", 1), ("I1", 4),),
+    "proj1": (("f1", 0), ("I2", 4), ("I3", 3), ("F0", 2), ("F2", 1),),
+    "proj2": (("f2", 0), ("O", 3),),
+    "proj.pre3": (("f1", 1), ("I3", 4),),
+    "proj3": (("f3", 0), ("F3", 1),),
+    "block0": (("f2", 1), ("O", 4),),
+    "block1": (("f3", 1),),
+    "block2": (("F1", 2),),
+    "block3": (("f1", 2),),
+    "att.pre0": (("f0", 2), ("F0", 3), ("f0", 3),),
+    "att.pre1": (("f1", 3),),
+    "att1": (("f2", 2), ("F2", 2),),
+    "att.pre2": (("F0", 4), ("F3", 2), ("f3", 2), ("f2", 3),),
     "att.pre3": (("f3", 3),),
     "mid": (("F1", 3),),
-    "feed0": (("F2", 3),),
-    "feed.pre1": (("F1", 4),),
-    "feed1": (("rF1", 0), ("F2", 4), ("F3", 3),),
+    "feed0": (("rF0", 0), ("F1", 4), ("F2", 3),),
+    "feed1": (("rF1", 0), ("rF0", 1), ("F2", 4), ("F3", 3),),
     "feed2": (("rF2", 0), ("rF1", 1), ("F3", 4),),
     "feed3": (("rF3", 0), ("rF2", 1),),
-    "out": (("rF3", 1), ("rF1", 2), ("rO", 0),),
+    "out": (("rF0", 2),),
     "st0": (("b0", 0),),
     "st1": (("b1", 0),),
-    "st2": (("b2", 0),),
-    "st3": (("b3", 0), ("rF2", 2), ("rO", 1), ("b0", 1),),
-    "q0": (("b1", 1), ("b2", 1), ("b3", 1), ("rF0", 0),),
-    "q1": (("rF1", 3),),
-    "q2": (("b0", 2), ("rF3", 2),),
-    "q3": (("b1", 2),),
-    "q.end": (("rQ", 0),),
-    "k.pre0": (("b0", 3),),
-    "k0": (("b2", 2), ("b1", 3), ("rF0", 1), ("b3", 2), ("rQ", 1), ("rF1", 4), ("rO", 2),),
-    "k1": (("b2", 3), ("b3", 3), ("rF3", 3),),
-    "k3": (("rF2", 3), ("rF0", 2),),
+    "st2": (("b2", 0), ("rF1", 2), ("rO", 0),),
+    "st3": (("b3", 0), ("rF3", 1), ("b0", 1),),
+    "q0": (("b1", 1), ("b2", 1), ("b3", 1), ("rO", 1),),
+    "q1": (("rF2", 2), ("rF0", 3),),
+    "q2": (("rF1", 3), ("b0", 2),),
+    "q.end": (("b1", 2), ("b0", 3), ("rQ", 0),),
+    "k0": (("b2", 2), ("rF0", 4),),
+    "k.pre1": (("b1", 3),),
+    "k1": (("b3", 2), ("rQ", 1), ("rF3", 2),),
+    "k.pre2": (("b2", 3),),
+    "k2": (("b3", 3), ("rF1", 4), ("rO", 2),),
+    "k3": (("rF2", 3),),
     "k.end": (("rK", 0), ("rQ", 2),),
-    "v0": (("rV0", 0), ("rK", 1), ("rF0", 3), ("rO", 3),),
+    "v0": (("rV0", 0), ("rK", 1), ("rF3", 3),),
     "v1": (("rV1", 0), ("rV0", 1), ("rQ", 3), ("rF2", 4),),
-    "nb0": (("rK", 2),),
-    "nb1": (("rV1", 1), ("rF0", 4),),
-    "fb1": (("rG", 0), ("rV0", 2), ("rO", 4),),
-    "end0": (("rF3", 4),),
-    "end": (("rK", 3), ("rQ", 4), ("rG", 1), ("rV0", 3), ("rV1", 2), ("rK", 4), ("rG", 2), ("rV0", 4),),
+    "fb0": (("rV1", 1),),
+    "fb1": (("rG", 0), ("rK", 2), ("rO", 3),),
+    "end0": (("rF3", 4), ("rV0", 2), ("rQ", 4), ("rG", 1), ("rV1", 2), ("rK", 3), ("rV0", 3), ("rO", 4),),
+    "end": (("rV1", 3), ("rG", 2), ("rK", 4), ("rV0", 4), ("rV1", 4),),
 }
 
 
@@ -1004,17 +1004,17 @@
         lhs = jnp.concatenate([v.T, jnp.ones((16, L), BF)], axis=0)
         r0 = dot(lhs, pk[s, 2 * p])
         r1 = dot(lhs, pk[s, 2 * p + 1])
-        fwd.own[p, s] = jnp.concatenate([r0[:64], r1[64:128], r0[128:], r1[128:]], axis=0).astype(BF)
+        fwd.own[p, s] = jnp.concatenate([r0[:64], r1[64:128], r0[128:136], r1[136:]], axis=0).astype(BF)
     pairs(project, "proj.pre", "proj")
 
     def state_cols(total, p, s, h, copies):
         state = total[p, s, h * 64:(h + 1) * 64]
-        extra = total[p, s, 128 + 16 * h:144 + 16 * h]
+        extra = total[p, s, 128:144].astype(F32)[8 * h:8 * h + 8]
         zeros = jnp.zeros((DH, M), BF)
         if copies:
-            extra = jnp.concatenate([extra] * 4, axis=0)
+            extra = jnp.concatenate([extra] * 8, axis=0).astype(BF)
         else:
-            extra = jnp.concatenate([extra, jnp.zeros((48, M), BF)], axis=0)
+            extra = jnp.concatenate([extra, jnp.zeros((56, M), F32)], axis=0).astype(BF)
         parts = [state, zeros, extra, zeros] if h == 0 else [zeros, state, zeros, extra]
         return jnp.concatenate(parts, axis=0)
 
@@ -1077,14 +1077,14 @@
         def seq(s):
             for b in range(2):
                 rows = slice(b * HALF, (b + 1) * HALF)
-                u = dot(n2[s, rows], wut()) + bias
+                u = (dot(n2[s, rows], wut()) + bias).astype(BF)
                 uu = u * u
-                th = jnp.tanh(u * (k0 + (k0 * 0.044715) * uu))
-                half = 0.5 + 0.5 * th
-                a = (u * half).astype(BF)
+                th = jnp.tanh(u * (BF(k0) + BF(k0 * 0.044715) * uu))
+                half = BF(0.5) + BF(0.5) * th
+                a = u * half
                 act[s, rows] = a
-                slope = half + (0.5 * u) * (1.0 - th * th) * (k0 + (3.0 * 0.044715 * k0) * uu)
-                back = dot_nt(cot[s, rows], wdt()) * slope
+                slope = half + a * (BF(1.0) - half) * (BF(2.0 * k0) + BF(6.0 * 0.044715 * k0) * uu)
+                back = dot_nt(cot[s, rows], wdt()) * slope.astype(F32)
                 grads[pl.ds(6 + t, 1)] += jnp.sum(back, axis=0, keepdims=True)
                 low = back.astype(BF)
                 hg[s, rows] = low
@@ -1156,7 +1156,7 @@
             lhs = ngx(s, p).T
             r0 = dot(lhs, pq[s, 2 * p])
             r1 = dot(lhs, pq[s, 2 * p + 1])
-            bwd.own[p, s] = jnp.concatenate([r0[:64], r1[64:128], r0[128:144], r1[192:208]], axis=0).astype(BF)
+            bwd.own[p, s] = jnp.concatenate([r0[:64], r1[64:128], r0[128:136], r1[192:200]], axis=0).astype(BF)
         seq(0)
         seq(1)
         pump_at(p, [f"st{n}" for n in range(PAIRS)])
@@ -1190,7 +1190,7 @@
             g11 = masked(lower, dot_nt(x[hi], v[hi]))
             qg0 = dot(jnp.concatenate([g00, x[lo]], axis=1), jnp.concatenate([k[lo], sx], axis=0))
             qg1 = dot(jnp.concatenate([g10, g11, x[hi]], axis=1), jnp.concatenate([k, sx], axis=0))
-            logs.append((jnp.concatenate([qg0, qg1], axis=0) * q.astype(F32)).astype(BF))
+            logs.append(jnp.concatenate([qg0, qg1], axis=0).astype(BF) * q)
         through_features(s, p, 0, logs)
     pairs(query_back, None, "q")
     part_q[...] = input_part(0, range(PAIRS))
@@ -1207,7 +1207,7 @@
             t11 = masked(upper, dot_nt(v[hi], x[hi]))
             kg0 = dot(jnp.concatenate([t00, t01, v[lo]], axis=1), jnp.concatenate([q, sg], axis=0))
             kg1 = dot(jnp.concatenate([t11, v[hi]], axis=1), jnp.concatenate([q[hi], sg], axis=0))
-            logs.append((jnp.concatenate([kg0, kg1], axis=0) * k.astype(F32)).astype(BF))
+            logs.append(jnp.concatenate([kg0, kg1], axis=0).astype(BF) * k)
         through_features(s, p, 1, logs)
     pairs(key_back, "k.pre", "k")
     part_k[...] = input_part(1, range(PAIRS))

time: 111 us -> 108 us (0.973)
  Pallas kernels: 110 us -> 107 us
    pallas_call x1, Pallas kernels: 105 us -> 103 us  [fused(): pl.pallas_call(functools.partial(layer_kernel, geo, lane, plan), out_shap...]
where the time goes in v5:
time: 108 us
  Pallas kernels  107 us (99%)
    pallas_call x1, Pallas kernels, fused(): pl.pallas_call(functools.partial(layer_kernel, geo, lane, plan), out_shap...  103 us
    pallas_call x1, Pallas kernels, fused(): pl.pallas_call(finish_kernel, out_shape=final, in_specs=[hbm] * 7, out_sp...  4.27 us

profile of v5, /device:TPU:0, one launch (start us, length us, event | category | flops | bytes accessed | tf_op | source)
XLA Modules:
  0.0 107.9 jit_solution(15595806414216843106)
XLA Ops:
  0.7 102.8 %shard_map.237 = (f32[2,512,512]{2,1,0:T(8,128)}, f32[2,512,512]{2,1,0:T(8,128)}, f32[16,1536]{1,0:T(8,128)}, f32[16,512]{1,0:T(8,128)}, f32[16,2048]{1,0:T(8,12...) custom-call(bf16[2,512,512]{2,1,0:T(8,128)(2,1)} %refs_0_.1, bf16[2,512,512]{2,1,0:T(8,128)(2,1)} %refs_1_.1, ...), custom_call_target="tpu_custom_call" | custom-call | tf_op jit(solution)/shard_map/pallas_call | solution.py:1396
  103.4 4.3 %shard_map.238 = (f32[2,512,512]{2,1,0:T(8,128)}, f32[2,512,512]{2,1,0:T(8,128)}, f32[16,1536]{1,0:T(8,128)}, f32[16,512]{1,0:T(8,128)}, f32[16]{0:T(128)}, /*in...) custom-call(f32[2,512,512]{2,1,0:T(8,128)} %get-tuple-element.20.ref, ...), custom_call_target="tpu_custom_call" | custom-call | tf_op jit(solution)/shard_map/pallas_call | solution.py:1404

commit v6 on v5

--- a/solution.py
+++ b/solution.py
@@ -786,57 +786,56 @@
         self.whole().wait_send()
 
 
-DIRECT = ("rG",)
+DIRECT = ("rG", "rV1",)
 PLANE = ()
-ORDERS = {"I3": (1, 1), "F0": (1, 1), "I1": (1, 1), "rF0": (0, 0), "rF3": (1, 1)}
+ORDERS = {"I3": (1, 1), "F0": (1, 1), "I1": (1, 1), "rF3": (1, 1)}
 PLAN = {
     "start": (("S", 0), ("I0", 0), ("I1", 0), ("I2", 0), ("I3", 0),),
-    "first": (("O", 0), ("F0", 0), ("F1", 0), ("F2", 0), ("S", 1), ("I0", 1), ("I1", 1), ("S", 2), ("I2", 1),
-        ("I0", 2), ("I3", 1), ("I1", 2), ("O", 1), ("S", 3), ("I2", 2), ("S", 4),),
+    "first": (("O", 0), ("F0", 0), ("F1", 0), ("F2", 0), ("F3", 0), ("S", 1), ("I0", 1), ("I1", 1), ("S", 2),
+        ("I2", 1), ("I0", 2), ("I3", 1), ("I1", 2), ("O", 1), ("S", 3), ("I2", 2), ("S", 4),),
     "norm0": (("I0", 3),),
     "proj.pre0": (("F0", 1), ("I3", 2), ("I0", 4),),
     "proj0": (("f0", 0),),
-    "proj.pre1": (("F3", 0), ("I1", 3), ("O", 2), ("F1", 1), ("I2", 3), ("f0", 1), ("I1", 4),),
-    "proj1": (("f1", 0), ("I2", 4), ("I3", 3), ("F0", 2), ("F2", 1),),
-    "proj2": (("f2", 0), ("O", 3),),
+    "proj.pre1": (("I1", 3), ("O", 2), ("F1", 1), ("I2", 3), ("f0", 1), ("I1", 4),),
+    "proj1": (("f1", 0), ("I3", 3), ("F0", 2), ("F2", 1),),
+    "proj.pre2": (("I2", 4),),
+    "proj2": (("f2", 0),),
     "proj.pre3": (("f1", 1), ("I3", 4),),
     "proj3": (("f3", 0), ("F3", 1),),
-    "block0": (("f2", 1), ("O", 4),),
+    "block0": (("f2", 1),),
     "block1": (("f3", 1),),
-    "block2": (("F1", 2),),
     "block3": (("f1", 2),),
-    "att.pre0": (("f0", 2), ("F0", 3), ("f0", 3),),
-    "att.pre1": (("f1", 3),),
-    "att1": (("f2", 2), ("F2", 2),),
-    "att.pre2": (("F0", 4), ("F3", 2), ("f3", 2), ("f2", 3),),
+    "att.pre0": (("O", 3), ("F1", 2), ("f0", 2), ("F0", 3), ("f1", 3), ("O", 4), ("F2", 2), ("f0", 3),),
+    "att0": (("f2", 2),),
+    "att.pre2": (("F0", 4), ("f3", 2), ("f2", 3),),
+    "att2": (("F3", 2),),
     "att.pre3": (("f3", 3),),
     "mid": (("F1", 3),),
-    "feed0": (("rF0", 0), ("F1", 4), ("F2", 3),),
+    "feed0": (("rF0", 0), ("F2", 3),),
+    "feed.pre1": (("F1", 4),),
     "feed1": (("rF1", 0), ("rF0", 1), ("F2", 4), ("F3", 3),),
     "feed2": (("rF2", 0), ("rF1", 1), ("F3", 4),),
-    "feed3": (("rF3", 0), ("rF2", 1),),
-    "out": (("rF0", 2),),
-    "st0": (("b0", 0),),
+    "feed3": (("rF0", 2), ("rF2", 1),),
+    "out": (("rF1", 2), ("rO", 0),),
+    "st0": (("b0", 0), ("rF3", 0),),
     "st1": (("b1", 0),),
-    "st2": (("b2", 0), ("rF1", 2), ("rO", 0),),
-    "st3": (("b3", 0), ("rF3", 1), ("b0", 1),),
-    "q0": (("b1", 1), ("b2", 1), ("b3", 1), ("rO", 1),),
-    "q1": (("rF2", 2), ("rF0", 3),),
-    "q2": (("rF1", 3), ("b0", 2),),
-    "q.end": (("b1", 2), ("b0", 3), ("rQ", 0),),
-    "k0": (("b2", 2), ("rF0", 4),),
-    "k.pre1": (("b1", 3),),
-    "k1": (("b3", 2), ("rQ", 1), ("rF3", 2),),
-    "k.pre2": (("b2", 3),),
-    "k2": (("b3", 3), ("rF1", 4), ("rO", 2),),
-    "k3": (("rF2", 3),),
-    "k.end": (("rK", 0), ("rQ", 2),),
+    "st2": (("b2", 0),),
+    "st3": (("b3", 0), ("rO", 1),),
+    "q0": (("b0", 1), ("b1", 1), ("b2", 1), ("rF3", 1),),
+    "q2": (("b3", 1), ("rO", 2),),
+    "q3": (("b0", 2), ("rF1", 3),),
+    "q.end": (("rQ", 0), ("rF0", 3),),
+    "k.pre0": (("rF2", 2), ("b1", 2), ("b0", 3),),
+    "k0": (("b1", 3), ("b2", 2), ("rQ", 1),),
+    "k1": (("b3", 2), ("b2", 3), ("rF3", 2),),
+    "k2": (("b3", 3), ("rF2", 3), ("rO", 3),),
+    "k3": (("rQ", 2),),
+    "k.end": (("rK", 0),),
     "v0": (("rV0", 0), ("rK", 1), ("rF3", 3),),
-    "v1": (("rV1", 0), ("rV0", 1), ("rQ", 3), ("rF2", 4),),
-    "fb0": (("rV1", 1),),
-    "fb1": (("rG", 0), ("rK", 2), ("rO", 3),),
-    "end0": (("rF3", 4), ("rV0", 2), ("rQ", 4), ("rG", 1), ("rV1", 2), ("rK", 3), ("rV0", 3), ("rO", 4),),
-    "end": (("rV1", 3), ("rG", 2), ("rK", 4), ("rV0", 4), ("rV1", 4),),
+    "v1": (("rV1", 0), ("rV0", 1), ("rQ", 3), ("rF2", 4), ("rO", 4),),
+    "nb1": (("rK", 2), ("rF0", 4), ("rV1", 1),),
+    "fb1": (("rG", 0), ("rF1", 4), ("rF3", 4),),
+    "end": (("rV0", 2), ("rQ", 4), ("rG", 1), ("rK", 3), ("rV0", 3), ("rV1", 2), ("rG", 2), ("rK", 4), ("rV0", 4),),
 }
 
 

time: 108 us -> 107 us (level)
    pallas_call x1, Pallas kernels: 103 us -> 101 us  [fused(): pl.pallas_call(functools.partial(layer_kernel, geo, lane, plan), out_shap...]
where the time goes in v6:
time: 107 us
  Pallas kernels  106 us (99%)
    pallas_call x1, Pallas kernels, fused(): pl.pallas_call(functools.partial(layer_kernel, geo, lane, plan), out_shap...  101 us
    pallas_call x1, Pallas kernels, fused(): pl.pallas_call(finish_kernel, out_shape=final, in_specs=[hbm] * 7, out_sp...  4.27 us

profile of v6, /device:TPU:0, one launch (start us, length us, event | category | flops | bytes accessed | tf_op | source)
XLA Modules:
  0.0 106.5 jit_solution(16761627279328887823)
XLA Ops:
  0.7 101.4 %shard_map.237 = (f32[2,512,512]{2,1,0:T(8,128)}, f32[2,512,512]{2,1,0:T(8,128)}, f32[16,1536]{1,0:T(8,128)}, f32[16,512]{1,0:T(8,128)}, f32[16,2048]{1,0:T(8,12...) custom-call(bf16[2,512,512]{2,1,0:T(8,128)(2,1)} %refs_0_.1, bf16[2,512,512]{2,1,0:T(8,128)(2,1)} %refs_1_.1, ...), custom_call_target="tpu_custom_call" | custom-call | tf_op jit(solution)/shard_map/pallas_call | solution.py:1395
  102.1 4.3 %shard_map.238 = (f32[2,512,512]{2,1,0:T(8,128)}, f32[2,512,512]{2,1,0:T(8,128)}, f32[16,1536]{1,0:T(8,128)}, f32[16,512]{1,0:T(8,128)}, f32[16]{0:T(128)}, /*in...) custom-call(f32[2,512,512]{2,1,0:T(8,128)} %get-tuple-element.20.ref, ...), custom_call_target="tpu_custom_call" | custom-call | tf_op jit(solution)/shard_map/pallas_call | solution.py:1403

commit v7 on v6

--- a/solution.py
+++ b/solution.py
@@ -1308,8 +1308,8 @@
     cuts = []
     for n in range(2):
         for m in range(ins[n].shape[0]):
-            for k in range(2):
-                rows = pl.ds(k * (ins[n].shape[1] // 2), ins[n].shape[1] // 2)
+            for k in range(4):
+                rows = pl.ds(k * (ins[n].shape[1] // 4), ins[n].shape[1] // 4)
                 slot = held.at[n, m, rows]
                 cuts.append((copy(ins[n].at[m, rows], slot, in_sems, 5 + len(cuts)),
                              copy(slot, outs[n].at[m, rows], out_sems, 11 + len(cuts))))
@@ -1405,7 +1405,7 @@
         out_shape=final, in_specs=[hbm] * 7, out_specs=[hbm] * 13,
         scratch_shapes=[V((2,) + tokens.shape, F32)] + [V(o.shape, F32) for o in outs[2:]]
         + [V((rows,), F32)] * 6 + [V(up_bias.shape, F32)]
-        + [pltpu.SemaphoreType.DMA((13,)), pltpu.SemaphoreType.DMA((19,))],
+        + [pltpu.SemaphoreType.DMA((21,)), pltpu.SemaphoreType.DMA((27,))],
         compiler_params=pltpu.CompilerParams(vmem_limit_bytes=60 << 20),
     )(*parts)
 

time: 107 us -> 107 us (level)
  no operation moved by 1% of the time
where the time goes in v7:
time: 107 us
  Pallas kernels  106 us (99%)
    pallas_call x1, Pallas kernels, fused(): pl.pallas_call(functools.partial(layer_kernel, geo, lane, plan), out_shap...  101 us
    pallas_call x1, Pallas kernels, fused(): pl.pallas_call(finish_kernel, out_shape=final, in_specs=[hbm] * 7, out_sp...  4.52 us

profile of v7, /device:TPU:0, one launch (start us, length us, event | category | flops | bytes accessed | tf_op | source)
XLA Modules:
  0.0 106.8 jit_solution(6865258988521032877)
XLA Ops:
  0.7 101.4 %shard_map.237 = (f32[2,512,512]{2,1,0:T(8,128)}, f32[2,512,512]{2,1,0:T(8,128)}, f32[16,1536]{1,0:T(8,128)}, f32[16,512]{1,0:T(8,128)}, f32[16,2048]{1,0:T(8,12...) custom-call(bf16[2,512,512]{2,1,0:T(8,128)(2,1)} %refs_0_.1, bf16[2,512,512]{2,1,0:T(8,128)(2,1)} %refs_1_.1, ...), custom_call_target="tpu_custom_call" | custom-call | tf_op jit(solution)/shard_map/pallas_call | solution.py:1395
  102.1 4.5 %shard_map.238 = (f32[2,512,512]{2,1,0:T(8,128)}, f32[2,512,512]{2,1,0:T(8,128)}, f32[16,1536]{1,0:T(8,128)}, f32[16,512]{1,0:T(8,128)}, f32[16]{0:T(128)}, /*in...) custom-call(f32[2,512,512]{2,1,0:T(8,128)} %get-tuple-element.20.ref, ...), custom_call_target="tpu_custom_call" | custom-call | tf_op jit(solution)/shard_map/pallas_call | solution.py:1403
